TPU v7x, 32 devices: a whole 2x2x4 slice. The times are simulated.
32 devices in a mesh: fsdp: 16 (over z, y, x), tp: 2 (over core).
Axes of the slice: x: 2, y: 2, z: 4, core: 2. Of those that a mesh axis runs over, the one named last changes fastest.
Arguments:
- tokens: bfloat16 [8192, 2048], P(('fsdp', 'tp')), may hold values from -6 to 6
- cotangent: bfloat16 [8192, 2048], P(('fsdp', 'tp')), may hold values from -6 to 6
- segment: int32 [8192], replicated, may hold values from 0 to 8, as said below
- position: int32 [8192], replicated, may hold values from 0 to 1151, as said below
- clip_limit: float32 [8], P('tp'), may hold values from 2.5 to 8
- attn_gain: bfloat16 [2048], P('fsdp'), may hold values from 0.5 to 1.5
- query_weight: bfloat16 [2048, 2048], P('fsdp', 'tp'), may hold values from -0.125 to 0.125
- key_weight: bfloat16 [2048, 1024], P('fsdp', 'tp'), may hold values from -0.125 to 0.125
- value_weight: bfloat16 [2048, 1024], P('fsdp', 'tp'), may hold values from -0.125 to 0.125
- output_weight: bfloat16 [2048, 2048], P('fsdp', 'tp'), may hold values from -1 to 1
- mlp_gain: bfloat16 [2048], P('fsdp'), may hold values from 0.5 to 1.5
- gate_weight: bfloat16 [2048, 8192], P('fsdp', 'tp'), may hold values from -0.125 to 0.125
- up_weight: bfloat16 [2048, 8192], P('fsdp', 'tp'), may hold values from -0.125 to 0.125
- down_weight: bfloat16 [2048, 8192], P('fsdp', 'tp'), may hold values from -0.0625 to 0.0625
Outputs:
- block_out: bfloat16 [8192, 2048], P(('fsdp', 'tp'))
- tokens_grad: float32 [8192, 2048], P(('fsdp', 'tp'))
- attn_gain_grad: float32 [2048], P('fsdp')
- query_grad: float32 [2048, 2048], P('fsdp', 'tp')
- key_grad: float32 [2048, 1024], P('fsdp', 'tp')
- value_grad: float32 [2048, 1024], P('fsdp', 'tp')
- output_grad: float32 [2048, 2048], P('fsdp', 'tp')
- mlp_gain_grad: float32 [2048], P('fsdp')
- gate_grad: float32 [2048, 8192], P('fsdp', 'tp')
- up_grad: float32 [2048, 8192], P('fsdp', 'tp')
- down_grad: float32 [2048, 8192], P('fsdp', 'tp')
- head_maxima: float32 [8], P('tp')
- query_clipped: bfloat16 [2048, 2048], P('fsdp', 'tp')
- key_clipped: bfloat16 [2048, 1024], P('fsdp', 'tp')
Inputs may be any that keep to these rules, and one draw needn't show every extreme that they name: Each group of 2048 consecutive tokens is made of aligned blocks of 128 tokens of one segment: 0 is the group's prompt and 1 to 8 its continuations, each holding one block; each aligned block of 512 tokens of a group holds at least one prompt block. `position`: the prompt block number b of a group holds positions b * 128 to b * 128 + 127 in order; a continuation's tokens hold 1024 to 1151 in order.
All inputs are finite; a program needn't handle non-finite values.
Results may differ from a plain program's by a relative error of at most 0.014.
Values may be sent and summed in bfloat16 or wider, within the bound.
No kernel may reach another device: no remote copies, remote signals or barrier semaphores. Data moves between devices by JAX's collectives and lax.ppermute only.
A program may use at most 320 MiB of HBM per device.

v0:
```python
import functools

import jax
import jax.numpy as jnp
from jax import lax
from jax.experimental import pallas as pl
from jax.experimental.pallas import tpu as pltpu
from jax.sharding import Mesh, PartitionSpec as P

HS = 256
GROUP = 2048
SIXTEENTHS = (10, 6)
BLOCK = 128

epsilon = 1e-05
theta_base = 1000042.0
masked_value = -1e30

bf16 = jnp.bfloat16
f32 = jnp.float32
PLANE = ("row", "col")
FSDP = ("group", "row", "col")
VMEM_LIMIT = 48 * 1024 * 1024


def product(left, right):
    return jnp.dot(left, right, preferred_element_type=f32)


def times_transposed(left, right):
    return lax.dot_general(left, right, (((1,), (1,)), ((), ())), preferred_element_type=f32)


def outer_sum(left, right):
    return lax.dot_general(left, right, (((0,), (0,)), ((), ())), preferred_element_type=f32)


def take(array, index, axis=0):
    return lax.dynamic_index_in_dim(array, index, axis, keepdims=False)


def swap(block, axis):
    return lax.ppermute(block, axis, [(0, 1), (1, 0)])


def swap_plane(block, distance):
    return lax.ppermute(block, PLANE, [(i, i ^ distance) for i in range(4)])


def after(value, *others):
    return lax.optimization_barrier((value,) + others)[0]


def combine_all(values, groups, combine):
    distance, count = 1, 4 * groups
    rounds = []
    while distance < count:
        arrived = []
        for step in range(1, min(4, count // distance)):
            route = [(i, i ^ step * distance) for i in range(count)]
            arrived.append(lax.ppermute(values, FSDP, route))
        for other in arrived:
            values = combine(values, other)
        rounds.append(arrived)
        distance *= 4
    return values, rounds


def pack_kernel(count, *refs):
    out_ref, sems = refs[count], refs[count + 1]
    copies, start = [], 0
    for i in range(count):
        rows = refs[i].shape[0]
        copy = pltpu.make_async_copy(refs[i], out_ref.at[pl.ds(start, rows)], sems.at[i])
        copy.start()
        copies.append(copy)
        start += rows
    for copy in copies:
        copy.wait()


def pack(pieces):
    rows, width = sum(p.shape[0] for p in pieces), pieces[0].shape[1]
    count = len(pieces)
    return pl.pallas_call(
        functools.partial(pack_kernel, count),
        in_specs=[pl.BlockSpec(memory_space=pl.ANY)] * count,
        out_specs=pl.BlockSpec(memory_space=pltpu.VMEM),
        out_shape=jax.ShapeDtypeStruct((rows, width), pieces[0].dtype),
        scratch_shapes=[pltpu.SemaphoreType.DMA((count,))],
        cost_estimate=pl.CostEstimate(
            flops=0, bytes_accessed=4 * rows * width, transcendentals=0
        ),
        compiler_params=pltpu.CompilerParams(vmem_limit_bytes=VMEM_LIMIT),
        name="pack",
    )(*pieces)


def norm_kernel(count, *refs):
    gain_ref, out_ref = refs[count], refs[-2]
    pack_kernel(count, *refs[:count], *refs[-2:])
    tile = 256

    @pl.loop(0, out_ref.shape[0] // tile)
    def _(i):
        rows = pl.ds(pl.multiple_of(i * tile, tile), tile)
        values = out_ref[rows, :].astype(f32)
        out_ref[rows, :] = (values * rms_inverse(values) * gain_ref[...]).astype(bf16)


def pack_normed(pieces, gain, early):
    rows, width = sum(p.shape[0] for p in pieces), pieces[0].shape[1]
    count = len(pieces)
    return pl.pallas_call(
        functools.partial(norm_kernel, count),
        in_specs=[pl.BlockSpec(memory_space=pl.ANY)] * count
        + [pl.BlockSpec(memory_space=pltpu.VMEM)]
        + [pl.BlockSpec(memory_space=pl.ANY)] * len(early),
        out_specs=pl.BlockSpec(memory_space=pltpu.VMEM),
        out_shape=jax.ShapeDtypeStruct((rows, width), bf16),
        scratch_shapes=[pltpu.SemaphoreType.DMA((count,))],
        cost_estimate=pl.CostEstimate(
            flops=8 * rows * width, bytes_accessed=4 * rows * width, transcendentals=0
        ),
        compiler_params=pltpu.CompilerParams(vmem_limit_bytes=VMEM_LIMIT),
        name="pack_normed",
    )(*pieces, gain, *early)


def plane_neighbours(own):
    return swap(own, "col"), swap(own, "row")


def plane_far(neighbours, *waits):
    across, along = neighbours
    half = across.shape[0] // 2
    return (
        swap(after(across[:half], *waits), "row"),
        swap(after(along[half:], *waits), "col"),
    )


def with_partner(pieces, swapped=()):
    return pieces + list(swapped) + [swap(piece, "tp") for piece in pieces[len(swapped) :]]


def chip_sums(front, back):
    pairs = []
    for own, other in (front, back):
        shape = (4, own.shape[0] // 4, own.shape[1])
        pairs.append((own.reshape(shape), swap(other, "tp").reshape(shape)))
    return pairs


def quarter(pair, k):
    return pair[0][k].astype(f32) + pair[1][k].astype(f32)


def first_operands(sums):
    front, back = sums
    return (
        jnp.concatenate([quarter(front, 1), quarter(front, 3)]).astype(bf16),
        (back[0][2:].astype(f32) + back[1][2:].astype(f32)).astype(bf16),
    )


def reduce_first(operands, *waits):
    front, back = operands
    rows = front.shape[0] // 2
    return (
        swap(after(front, *waits), "col").reshape(2, rows, -1),
        swap(after(back, *waits), "row"),
    )


def reduce_operands(sums, arrived):
    front, back = sums
    got, got_back = arrived[0].astype(f32), arrived[1].astype(f32)
    return (
        (quarter(front, 0) + got[0], (quarter(front, 2) + got[1]).astype(bf16)),
        (quarter(back, 0) + got_back[0], (quarter(back, 1) + got_back[1]).astype(bf16)),
    )


def last_swaps(operands, *waits):
    return (
        swap(after(operands[0][1], *waits), "row"),
        swap(after(operands[1][1], *waits), "col"),
    )


def reduce_last(operands, swapped):
    return jnp.concatenate(
        [keep + last.astype(f32) for (keep, _), last in zip(operands, swapped)], axis=1
    )


def joined(front_ref, front_last_ref, back_ref, back_last_ref):
    return jnp.concatenate(
        [
            front_ref[...] + front_last_ref[...].astype(f32),
            back_ref[...] + back_last_ref[...].astype(f32),
        ],
        axis=1,
    )


def hidden_kernel(front, front_last, back, back_last, tokens_ref, gain_ref, hidden_ref, normed_ref):
    hidden = tokens_ref[...].astype(f32) + joined(front, front_last, back, back_last)
    hidden_ref[...] = hidden
    normed_ref[...] = (hidden * rms_inverse(hidden) * gain_ref[...]).astype(bf16)


def add_and_norm(operands, last, tokens, gain):
    halves = [part for (keep, _), got in zip(operands, last) for part in (keep, got)]
    return pl.pallas_call(
        hidden_kernel,
        in_specs=[pl.BlockSpec(memory_space=pltpu.VMEM)] * 6,
        out_specs=[pl.BlockSpec(memory_space=pltpu.VMEM)] * 2,
        out_shape=[
            jax.ShapeDtypeStruct(tokens.shape, f32),
            jax.ShapeDtypeStruct(tokens.shape, bf16),
        ],
        cost_estimate=pl.CostEstimate(
            flops=10 * tokens.size, bytes_accessed=14 * tokens.size, transcendentals=0
        ),
        compiler_params=pltpu.CompilerParams(vmem_limit_bytes=VMEM_LIMIT),
        name="add_and_norm",
    )(*halves, tokens, gain)


def back_kernel(front, front_last, back, back_last, values_ref, base_ref, gain_ref, *outs):
    values = values_ref[...].astype(f32)
    inverse = rms_inverse(values)
    unit = values * inverse
    scaled = joined(front, front_last, back, back_last) * gain_ref[...]
    grad = base_ref[...].astype(f32) + inverse * (
        scaled - unit * jnp.mean(scaled * unit, axis=-1, keepdims=True)
    )
    for out in outs:
        out[...] = grad.astype(out.dtype)


def norm_back(operands, last, values, base, gain, dtypes):
    halves = [part for (keep, _), got in zip(operands, last) for part in (keep, got)]
    return pl.pallas_call(
        back_kernel,
        in_specs=[pl.BlockSpec(memory_space=pltpu.VMEM)] * 7,
        out_specs=[pl.BlockSpec(memory_space=pltpu.VMEM)] * len(dtypes),
        out_shape=[jax.ShapeDtypeStruct(values.shape, dtype) for dtype in dtypes],
        cost_estimate=pl.CostEstimate(
            flops=16 * values.size, bytes_accessed=18 * values.size, transcendentals=0
        ),
        compiler_params=pltpu.CompilerParams(vmem_limit_bytes=VMEM_LIMIT),
        name="norm_back",
    )(*halves, values, base, gain)


def split_kernel(spans, member_ref, *refs):
    sources, outs = refs[: len(spans)], refs[len(spans) :]
    for k in range(4):
        target = member_ref[0] ^ k
        column = 0
        for source, (offset, stride, width, shift) in zip(sources, spans):
            start = pl.multiple_of((target >> shift) * stride + offset, 128)
            outs[k][:, column : column + width] = source[:, pl.ds(start, width)]
            column += width


def split(member, sources, spans):
    rows, width = sources[0].shape[0], sum(span[2] for span in spans)
    whole = pl.BlockSpec(memory_space=pltpu.VMEM)
    return pl.pallas_call(
        functools.partial(split_kernel, spans),
        in_specs=[pl.BlockSpec(memory_space=pltpu.SMEM)] + [whole] * len(sources),
        out_specs=[whole] * 4,
        out_shape=[jax.ShapeDtypeStruct((rows, width), bf16)] * 4,
        cost_estimate=pl.CostEstimate(
            flops=0, bytes_accessed=16 * rows * width, transcendentals=0
        ),
        compiler_params=pltpu.CompilerParams(vmem_limit_bytes=VMEM_LIMIT),
        name="split",
    )(member, *sources)


def place_kernel(member_ref, *refs):
    rows = refs[0].shape[0]
    for k in range(4):
        start = pl.multiple_of((member_ref[0] ^ k) * rows, rows)
        column = 0
        for out_ref in refs[4:]:
            width = out_ref.shape[1]
            out_ref[pl.ds(start, rows), :] = refs[k][:, column : column + width]
            column += width


def place_rows(member, pieces, *widths):
    rows, width = pieces[0].shape
    whole = pl.BlockSpec(memory_space=pltpu.VMEM)
    return pl.pallas_call(
        place_kernel,
        in_specs=[pl.BlockSpec(memory_space=pltpu.SMEM)] + [whole] * 4,
        out_specs=[whole] * len(widths or (width,)),
        out_shape=[
            jax.ShapeDtypeStruct((4 * rows, w), bf16) for w in widths or (width,)
        ],
        cost_estimate=pl.CostEstimate(
            flops=0, bytes_accessed=16 * rows * width, transcendentals=0
        ),
        compiler_params=pltpu.CompilerParams(vmem_limit_bytes=VMEM_LIMIT),
        name="place_rows",
    )(member, *pieces)


def pick_kernel(member_ref, *refs):
    sources, outs = refs[:-4], refs[-4:]
    rows = outs[0].shape[0]
    for k in range(4):
        start = pl.multiple_of((member_ref[0] ^ k) * rows, rows)
        column = 0
        for source in sources:
            width = source.shape[1]
            outs[k][:, column : column + width] = source[pl.ds(start, rows), :]
            column += width


def pick_rows(member, *sources):
    rows, width = sources[0].shape[0] // 4, sum(source.shape[1] for source in sources)
    whole = pl.BlockSpec(memory_space=pltpu.VMEM)
    return pl.pallas_call(
        pick_kernel,
        in_specs=[pl.BlockSpec(memory_space=pltpu.SMEM)] + [whole] * len(sources),
        out_specs=[whole] * 4,
        out_shape=[jax.ShapeDtypeStruct((rows, width), bf16)] * 4,
        cost_estimate=pl.CostEstimate(
            flops=0, bytes_accessed=16 * rows * width, transcendentals=0
        ),
        compiler_params=pltpu.CompilerParams(vmem_limit_bytes=VMEM_LIMIT),
        name="pick_rows",
    )(member, *sources)


def swap_all(pieces):
    return [pieces[0]] + [swap_plane(pieces[k], k) for k in (1, 2, 3)]


def mlp_final_kernel(parts, stride, member_ref, gate_w_ref, up_w_ref, *refs):
    pieces, outs, gain_ref = refs[:-4], refs[-4:-1], refs[-1]
    for n, chunks in enumerate(parts):
        for k in range(4):
            start = 0
            for offset, width in chunks:
                column = pl.multiple_of((member_ref[0] ^ k) * stride + offset, 128)
                for i in range(3):
                    part = pieces[4 * n + k][:, start : start + width]
                    outs[i][:, pl.ds(column, width)] = part.astype(f32)
                    start += width
    gain_ref[...] = jnp.sum(
        gate_w_ref[...].astype(f32) * outs[0][...] + up_w_ref[...].astype(f32) * outs[1][...],
        axis=1,
        keepdims=True,
    )


def mlp_final(member, gate_weight, up_weight, chunks, parts):
    rows, hidden = gate_weight.shape
    pieces = [piece for part in parts for piece in part]
    whole = pl.BlockSpec(memory_space=pltpu.VMEM)
    return pl.pallas_call(
        functools.partial(mlp_final_kernel, chunks, hidden // 4),
        in_specs=[pl.BlockSpec(memory_space=pltpu.SMEM)] + [whole] * (2 + len(pieces)),
        out_specs=[whole] * 4,
        out_shape=[jax.ShapeDtypeStruct((rows, hidden), f32)] * 3
        + [jax.ShapeDtypeStruct((rows, 1), f32)],
        cost_estimate=pl.CostEstimate(
            flops=4 * rows * hidden, bytes_accessed=22 * rows * hidden, transcendentals=0
        ),
        compiler_params=pltpu.CompilerParams(vmem_limit_bytes=VMEM_LIMIT),
        name="mlp_final",
    )(member, gate_weight, up_weight, *pieces)


TURN = [(0, 0), (1, 2), (2, 1), (3, 3)]
CROSS = [(0, 2), (1, 0), (2, 3), (3, 1)]
CROSS_BACK = [(2, 0), (0, 1), (3, 2), (1, 3)]


def vmem_call(kernel, name, out_shape, *operands):
    whole = pl.BlockSpec(memory_space=pltpu.VMEM)
    moved = sum(a.size * a.dtype.itemsize for a in operands)
    moved += sum(a.size * a.dtype.itemsize for a in out_shape)
    return pl.pallas_call(
        kernel,
        in_specs=[pl.BlockSpec(memory_space=pltpu.SMEM)] + [whole] * (len(operands) - 1),
        out_specs=[whole] * len(out_shape),
        out_shape=out_shape,
        cost_estimate=pl.CostEstimate(flops=0, bytes_accessed=moved, transcendentals=0),
        compiler_params=pltpu.CompilerParams(vmem_limit_bytes=VMEM_LIMIT),
        name=name,
    )(*operands)


def head_columns(index):
    return pl.ds(pl.multiple_of(index * HS, HS), HS)


def halves_kernel(rows, member_ref, grads_ref, keep_ref, send_ref):
    half = (member_ref[0] & 1) * 2 * rows
    for i, base in enumerate(range(0, grads_ref.shape[0], 4 * rows)):
        part = slice(i * 2 * rows, (i + 1) * 2 * rows)
        mine = pl.ds(pl.multiple_of(base + half, 2 * rows), 2 * rows)
        other = pl.ds(pl.multiple_of(base + 2 * rows - half, 2 * rows), 2 * rows)
        keep_ref[part, :] = grads_ref[mine, :]
        send_ref[part, :] = grads_ref[other, :]


def join_kernel(rows, member_ref, keep_ref, got_ref, both_ref, out_ref):
    out_ref[:, : 2 * HS] = both_ref[...]
    for i, base in enumerate(range(0, out_ref.shape[0], 4 * rows)):
        part = slice(i * 2 * rows, (i + 1) * 2 * rows)
        total = (keep_ref[part, :].astype(f32) + got_ref[part, :].astype(f32)).astype(bf16)
        out_ref[base : base + 2 * rows, 2 * HS :] = total[:, :HS]
        out_ref[base + 2 * rows : base + 4 * rows, 2 * HS :] = total[:, HS:]


def attention_pick_kernel(member_ref, source_ref, *outs):
    member, rows = member_ref[0], outs[0].shape[0]
    for k in range(4):
        at = pl.ds(pl.multiple_of((member ^ k) * rows, rows), rows)
        outs[k][...] = source_ref[at, : 2 * HS]
    for h in range(2):
        start = ((member >> 1) ^ h) * rows
        at = pl.ds(pl.multiple_of(start, rows), rows)
        outs[4 + h][:, :HS] = source_ref[at, 2 * HS :]
        at = pl.ds(pl.multiple_of(start + 2 * rows, rows), rows)
        outs[4 + h][:, HS:] = source_ref[at, 2 * HS :]


def attention_return(member, reduced):
    rows = reduced.shape[0] // 4
    *both, turned, crossed = vmem_call(
        attention_pick_kernel,
        "attention_pick",
        [jax.ShapeDtypeStruct((rows, 2 * HS), bf16)] * 6,
        member,
        reduced,
    )
    return swap_all(both) + [
        lax.ppermute(turned, PLANE, TURN),
        lax.ppermute(crossed, PLANE, CROSS_BACK),
    ]


def attention_final_kernel(member_ref, qw_ref, kw_ref, vw_ref, *refs):
    pieces = refs[:6]
    q_ref, k_ref, v_ref, o_ref, gain_ref = refs[6:]
    member = member_ref[0]
    for k in range(4):
        columns = head_columns(member ^ k)
        q_ref[:, columns] = pieces[k][:, :HS].astype(f32)
        o_ref[:, columns] = pieces[k][:, HS:].astype(f32)
    for h in range(2):
        columns = head_columns((member & 1) ^ h)
        k_ref[:, columns] = pieces[4 + h][:, :HS].astype(f32)
        v_ref[:, columns] = pieces[4 + h][:, HS:].astype(f32)

    def row_sum(weight_ref, grad_ref):
        return jnp.sum(weight_ref[...].astype(f32) * grad_ref[...], axis=1, keepdims=True)

    gain_ref[...] = row_sum(qw_ref, q_ref) + row_sum(kw_ref, k_ref) + row_sum(vw_ref, v_ref)


def attention_final(member, query_weight, key_weight, value_weight, pieces):
    rows, width = query_weight.shape
    shapes = [jax.ShapeDtypeStruct((rows, n), f32) for n in (width, width // 2, width // 2, width, 1)]
    return vmem_call(
        attention_final_kernel,
        "attention_final",
        shapes,
        member,
        query_weight,
        key_weight,
        value_weight,
        *pieces,
    )


def rms_inverse(values):
    return lax.rsqrt(jnp.mean(values * values, axis=-1, keepdims=True) + epsilon)


def rope_tables(positions):
    half_size = HS // 2
    indices = jnp.arange(half_size, dtype=f32)
    inverse = theta_base ** (-2.0 * indices / HS)
    angles = positions.astype(f32)[:, None] * inverse[None, :]
    return jnp.cos(angles), jnp.sin(angles)


def rotate(vectors, cos, sin):
    front, back = vectors[:, : HS // 2], vectors[:, HS // 2 :]
    return jnp.concatenate([front * cos - back * sin, back * cos + front * sin], axis=-1)


def unrotate(grads, cos, sin):
    front, back = grads[:, : HS // 2], grads[:, HS // 2 :]
    return jnp.concatenate([front * cos + back * sin, back * cos - front * sin], axis=-1)


def mlp_tile(width, normed, cot, weight_ref):
    both = product(normed, weight_ref[:, : 2 * width])
    d_inner = product(cot, weight_ref[:, 2 * width :])
    gate, upward = both[:, :width], both[:, width:]
    sig = 1.0 / (1.0 + jnp.exp(-gate))
    silu = gate * sig
    d_gate = d_inner * upward * sig * (1.0 + gate * (1.0 - sig))
    return (
        (silu * upward).astype(bf16),
        jnp.concatenate([d_gate, d_inner * silu], axis=1).astype(bf16),
    )


def mlp_kernel(width, normed_ref, cot_ref, weight_ref, inner_ref, grads_ref):
    inner_ref[...], grads_ref[...] = mlp_tile(
        width, normed_ref[...], cot_ref[...], weight_ref
    )


def tail_kernel(width, normed_ref, cot_ref, weight_ref, base_ref, *refs):
    inner_ref, grads_ref, front_ref, back_ref = refs[-4:]
    inner, grads = mlp_tile(width, normed_ref[...], cot_ref[...], weight_ref)
    inner_ref[...], grads_ref[...] = inner, grads
    total = times_transposed(grads, weight_ref[:, : 2 * width]) + base_ref[...]
    half = total.shape[1] // 2
    front_ref[...] = total[:, :half].astype(front_ref.dtype)
    back_ref[...] = total[:, half:].astype(back_ref.dtype)


def mlp_tail(normed, cot, weight, base, part, dtype, chained=()):
    tokens, features = normed.shape
    width = weight.shape[1] // 3
    tile, rows = 256, tokens // 2
    steps = rows // tile
    count = len(chained)
    return pl.pallas_call(
        functools.partial(tail_kernel, width),
        grid=(steps,),
        in_specs=[
            pl.BlockSpec((tile, features), lambda i: (part * steps + i, 0)),
            pl.BlockSpec((tile, features), lambda i: (part * steps + i, 0)),
            pl.BlockSpec((features, 3 * width), lambda i: (0, 0)),
            pl.BlockSpec((tile, features), lambda i: (i, 0)),
        ]
        + [pl.BlockSpec(memory_space=pl.ANY)] * count,
        out_specs=[
            pl.BlockSpec((tile, width), lambda i: (part * steps + i, 0)),
            pl.BlockSpec((tile, 2 * width), lambda i: (part * steps + i, 0)),
            pl.BlockSpec((tile, features // 2), lambda i: (i, 0)),
            pl.BlockSpec((tile, features // 2), lambda i: (i, 0)),
        ],
        out_shape=[
            jax.ShapeDtypeStruct((tokens, width), bf16),
            jax.ShapeDtypeStruct((tokens, 2 * width), bf16),
            jax.ShapeDtypeStruct((rows, features // 2), dtype),
            jax.ShapeDtypeStruct((rows, features // 2), dtype),
        ],
        input_output_aliases={4 + i: i for i in range(count)},
        cost_estimate=pl.CostEstimate(
            flops=10 * rows * features * width,
            bytes_accessed=2 * features * (5 * rows + 3 * width),
            transcendentals=rows * width,
        ),
        compiler_params=pltpu.CompilerParams(vmem_limit_bytes=VMEM_LIMIT),
        name="mlp_tail",
    )(normed, cot, weight, base, *chained)


def mlp_chunk(normed, cot, weight):
    tokens, features = normed.shape
    width = weight.shape[1] // 3
    tile = 256
    return pl.pallas_call(
        functools.partial(mlp_kernel, width),
        grid=(tokens // tile,),
        in_specs=[
            pl.BlockSpec((tile, features), lambda i: (i, 0)),
            pl.BlockSpec((tile, features), lambda i: (i, 0)),
            pl.BlockSpec((features, 3 * width), lambda i: (0, 0)),
        ],
        out_specs=[
            pl.BlockSpec((tile, width), lambda i: (i, 0)),
            pl.BlockSpec((tile, 2 * width), lambda i: (i, 0)),
        ],
        out_shape=[
            jax.ShapeDtypeStruct((tokens, width), bf16),
            jax.ShapeDtypeStruct((tokens, 2 * width), bf16),
        ],
        cost_estimate=pl.CostEstimate(
            flops=6 * tokens * features * width,
            bytes_accessed=2 * features * (2 * tokens + 3 * width),
            transcendentals=tokens * width,
        ),
        compiler_params=pltpu.CompilerParams(vmem_limit_bytes=VMEM_LIMIT),
        name="mlp_chunk",
    )(normed, cot, weight)


def sum_kernel(count, *refs):
    lefts, rights, out_ref = refs[:count], refs[count : 2 * count], refs[-1]
    total = times_transposed(lefts[0][...], rights[0][...])
    for left, right in zip(lefts[1:], rights[1:]):
        total += times_transposed(left[...], right[...])
    for base in refs[2 * count : -1]:
        total += base[...].astype(f32)
    out_ref[...] = total.astype(out_ref.dtype)


def chunk_sum(lefts, rights, column, part, half, dtype):
    count = len(lefts)
    tokens, features = lefts[0].shape[0], rights[0].shape[0]
    widths = [left.shape[1] for left in lefts]
    rows = tokens // 2
    tile = 256
    if half is not None:
        features, tile = features // 2, 512
    steps = rows // tile
    block = half or 0
    return pl.pallas_call(
        functools.partial(sum_kernel, count),
        grid=(steps,),
        in_specs=[pl.BlockSpec((tile, w), lambda i: (part * steps + i, 0)) for w in widths]
        + [pl.BlockSpec((features, w), lambda i: (block, column)) for w in widths],
        out_specs=pl.BlockSpec((tile, features), lambda i: (i, 0)),
        out_shape=jax.ShapeDtypeStruct((rows, features), dtype),
        cost_estimate=pl.CostEstimate(
            flops=2 * rows * features * sum(widths),
            bytes_accessed=2 * sum(widths) * (rows + features) + 4 * rows * features,
            transcendentals=0,
        ),
        compiler_params=pltpu.CompilerParams(vmem_limit_bytes=VMEM_LIMIT),
        name="chunk_sum",
    )(*lefts, *rights)


def grads_kernel(count, *refs):
    column = 0
    for left, right in zip(refs[:count], refs[count : 2 * count]):
        width = right.shape[1]
        refs[-1][:, column : column + width] = outer_sum(left[...], right[...]).astype(bf16)
        column += width


def weight_grads(*pairs):
    lefts = [left for left, _ in pairs]
    rights = [r if isinstance(r, tuple) else (r, r.shape[1], 0) for _, r in pairs]
    count = len(pairs)
    tokens, features = lefts[0].shape
    widths = [width for _, width, _ in rights]
    tile = 256

    def block(width, at):
        return pl.BlockSpec((tokens, width), lambda i: (0, at))

    return pl.pallas_call(
        functools.partial(grads_kernel, count),
        grid=(features // tile,),
        in_specs=[pl.BlockSpec((tokens, tile), lambda i: (0, i))] * count
        + [block(width, at) for _, width, at in rights],
        out_specs=pl.BlockSpec((tile, sum(widths)), lambda i: (i, 0)),
        out_shape=jax.ShapeDtypeStruct((features, sum(widths)), bf16),
        cost_estimate=pl.CostEstimate(
            flops=2 * tokens * features * sum(widths),
            bytes_accessed=2 * (count * tokens * features + sum(widths) * (tokens + features)),
            transcendentals=0,
        ),
        compiler_params=pltpu.CompilerParams(vmem_limit_bytes=VMEM_LIMIT),
        name="weight_grads",
    )(*lefts, *[array for array, _, _ in rights])


def project_kernel(place_ref, normed_ref, weight_ref, cos_ref, sin_ref, q_ref, k_ref, v_ref):
    step = pl.program_id(0)
    cos, sin = cos_ref[...], sin_ref[...]
    qkv = product(normed_ref[...], weight_ref[...])
    keys = rotate(qkv[:, :HS], cos, sin).astype(bf16)
    vals = qkv[:, HS : 2 * HS].astype(bf16)
    query = rotate(qkv[:, 2 * HS :], cos, sin).astype(bf16) * HS ** (-0.5)
    blocks = normed_ref.shape[0] // BLOCK
    for b in range(blocks):
        rows = pl.ds(pl.multiple_of(place_ref[step * blocks + b] * BLOCK, BLOCK), BLOCK)
        part = slice(b * BLOCK, (b + 1) * BLOCK)
        q_ref[rows, :] = query[part]
        k_ref[rows, :] = keys[part]
        v_ref[rows, :] = vals[part]


def project(place, normed, weight, cos, sin):
    tokens, features = normed.shape
    tile = 256
    whole = pl.BlockSpec((tokens, HS), lambda i, place: (0, 0))
    return pl.pallas_call(
        project_kernel,
        grid_spec=pltpu.PrefetchScalarGridSpec(
            num_scalar_prefetch=1,
            grid=(tokens // tile,),
            in_specs=[
                pl.BlockSpec((tile, features), lambda i, place: (i, 0)),
                pl.BlockSpec((features, 3 * HS), lambda i, place: (0, 0)),
                pl.BlockSpec((tile, HS // 2), lambda i, place: (i, 0)),
                pl.BlockSpec((tile, HS // 2), lambda i, place: (i, 0)),
            ],
            out_specs=[whole] * 3,
        ),
        out_shape=[jax.ShapeDtypeStruct((tokens, HS), bf16)] * 3,
        cost_estimate=pl.CostEstimate(
            flops=6 * tokens * features * HS,
            bytes_accessed=2 * features * (tokens + 3 * HS) + 10 * tokens * HS,
            transcendentals=0,
        ),
        compiler_params=pltpu.CompilerParams(vmem_limit_bytes=VMEM_LIMIT),
        name="project",
    )(place, normed, weight, cos, sin)


TILE = 256


def tile_masks():
    rows = lax.broadcasted_iota(jnp.int32, (TILE, TILE), 0)
    cols = lax.broadcasted_iota(jnp.int32, (TILE, TILE), 1)
    causal = rows >= cols
    return causal, causal & (rows // BLOCK == cols // BLOCK)


def block_rows(order_ref, index):
    return pl.ds(pl.multiple_of(order_ref[index] * BLOCK, BLOCK), BLOCK)


def forward_kernel(order_ref, q_ref, k_ref, v_ref, mixed_ref, lse_ref, peak_ref):
    causal, inside = tile_masks()
    prompt = GROUP // 2
    top = jnp.full((TILE, 1), masked_value, f32)
    for i in range(GROUP // TILE):
        rows = slice(i * TILE, (i + 1) * TILE)
        past = min(i * TILE, prompt)
        query = q_ref[rows, :]
        near = times_transposed(query, k_ref[rows, :])
        near = jnp.where(causal if i * TILE < prompt else inside, near, masked_value)
        peak = jnp.max(near, axis=1, keepdims=True)
        if past:
            far = times_transposed(query, k_ref[:past, :])
            peak = jnp.maximum(peak, jnp.max(far, axis=1, keepdims=True))
            far = jnp.exp(far - peak)
        near = jnp.exp(near - peak)
        total = jnp.sum(near, axis=1, keepdims=True)
        if past:
            total += jnp.sum(far, axis=1, keepdims=True)
        share = 1.0 / total
        mixed = product((near * share).astype(bf16), v_ref[rows, :])
        if past:
            mixed += product((far * share).astype(bf16), v_ref[:past, :])
        mixed = mixed.astype(bf16)
        for b in range(TILE // BLOCK):
            mixed_ref[block_rows(order_ref, i * (TILE // BLOCK) + b), :] = mixed[
                b * BLOCK : (b + 1) * BLOCK
            ]
        lse_ref[rows, :] = peak + jnp.log(total)
        top = jnp.maximum(top, peak)
    peak_ref[...] = jnp.full(peak_ref.shape, jnp.max(top), f32)


def attention_forward(order, query, keys, vals):
    whole = pl.BlockSpec(memory_space=pltpu.VMEM)
    return pl.pallas_call(
        forward_kernel,
        in_specs=[pl.BlockSpec(memory_space=pltpu.SMEM), whole, whole, whole],
        out_specs=[whole] * 3,
        out_shape=[
            jax.ShapeDtypeStruct((GROUP, HS), bf16),
            jax.ShapeDtypeStruct((GROUP, 1), f32),
            jax.ShapeDtypeStruct((8, 128), f32),
        ],
        cost_estimate=pl.CostEstimate(
            flops=2 * GROUP * GROUP * HS,
            bytes_accessed=8 * GROUP * HS,
            transcendentals=GROUP * GROUP // 2,
        ),
        compiler_params=pltpu.CompilerParams(vmem_limit_bytes=VMEM_LIMIT),
        name="attention_forward",
    )(order, query, keys, vals)


def backward_kernel(
    order_ref, q_ref, k_ref, v_ref, lse_ref, mixed_ref, cos_ref, sin_ref, out_ref, dk_ref, dv_ref
):
    causal, inside = tile_masks()
    prompt = GROUP // 2
    blocks = TILE // BLOCK

    def back(grad, index):
        rows = block_rows(order_ref, index)
        return rows, unrotate(grad, cos_ref[rows, :], sin_ref[rows, :]).astype(bf16)

    for i in range(GROUP // TILE):
        rows = slice(i * TILE, (i + 1) * TILE)
        past = min(i * TILE, prompt)
        query, lse = q_ref[rows, :], lse_ref[rows, :]
        d_mixed = jnp.concatenate(
            [mixed_ref[block_rows(order_ref, i * blocks + b), :] for b in range(blocks)], axis=0
        )
        near = times_transposed(query, k_ref[rows, :])
        near = jnp.where(causal if i * TILE < prompt else inside, near, masked_value)
        near = jnp.exp(near - lse)
        d_near = times_transposed(d_mixed, v_ref[rows, :])
        inner = jnp.sum(near * d_near, axis=1, keepdims=True)
        if past:
            far = jnp.exp(times_transposed(query, k_ref[:past, :]) - lse)
            d_far = times_transposed(d_mixed, v_ref[:past, :])
            inner += jnp.sum(far * d_far, axis=1, keepdims=True)
        d_near = (near * (d_near - inner)).astype(bf16)
        d_query = product(d_near, k_ref[rows, :])
        dk_ref[rows, :] = outer_sum(d_near, query)
        dv_ref[rows, :] = outer_sum(near.astype(bf16), d_mixed)
        if past:
            d_far = (far * (d_far - inner)).astype(bf16)
            d_query += product(d_far, k_ref[:past, :])
            dk_ref[:past, :] += outer_sum(d_far, query)
            dv_ref[:past, :] += outer_sum(far.astype(bf16), d_mixed)
        d_query = d_query * HS ** (-0.5)
        for b in range(blocks):
            where, grad = back(d_query[b * BLOCK : (b + 1) * BLOCK], i * blocks + b)
            out_ref[where, 2 * HS :] = grad
    for c in range(GROUP // BLOCK):
        part = slice(c * BLOCK, (c + 1) * BLOCK)
        where, grad = back(dk_ref[part, :], c)
        out_ref[where, :HS] = grad
        out_ref[where, HS : 2 * HS] = dv_ref[part, :].astype(bf16)


def attention_backward(order, query, keys, vals, lse, d_mixed, cos, sin):
    whole = pl.BlockSpec(memory_space=pltpu.VMEM)
    return pl.pallas_call(
        backward_kernel,
        in_specs=[pl.BlockSpec(memory_space=pltpu.SMEM)] + [whole] * 7,
        out_specs=whole,
        out_shape=jax.ShapeDtypeStruct((GROUP, 3 * HS), bf16),
        scratch_shapes=[pltpu.VMEM((GROUP, HS), f32), pltpu.VMEM((GROUP, HS), f32)],
        cost_estimate=pl.CostEstimate(
            flops=5 * GROUP * GROUP * HS,
            bytes_accessed=20 * GROUP * HS,
            transcendentals=GROUP * GROUP // 2,
        ),
        compiler_params=pltpu.CompilerParams(vmem_limit_bytes=VMEM_LIMIT),
        name="attention_backward",
    )(order, query, keys, vals, lse, d_mixed, cos, sin)


def local(
    tokens,
    cotangent,
    segment,
    position,
    clip_limit,
    attn_gain,
    query_weight,
    key_weight,
    value_weight,
    output_weight,
    mlp_gain,
    gate_weight,
    up_weight,
    down_weight,
):
    groups = lax.axis_size("group")
    group = lax.axis_index("group")
    core = lax.axis_index("tp")
    member = lax.axis_index(PLANE)
    token_rows = tokens.shape[0]
    own_rows, features = query_weight.shape[0], tokens.shape[1]
    hidden_own = gate_weight.shape[1] // 4
    chunks, offset = [], 0
    for part in SIXTEENTHS:
        chunks.append((offset, hidden_own * part // 16))
        offset += hidden_own * part // 16
    member_at = member.astype(jnp.int32).reshape(1)

    def own_order(array):
        parts = []
        for j in range(2):
            for k in range(4):
                start = group * GROUP + (member ^ k) * (2 * token_rows) + (core ^ j) * token_rows
                parts.append(lax.dynamic_slice_in_dim(array, start, token_rows))
        return jnp.concatenate(parts)

    def collect(blocks):
        return lax.all_gather(blocks, "group", axis=0, tiled=True)

    def mlp_exchange(some, waits):
        weights = [after(a, *waits) for a in (gate_weight, up_weight, down_weight)]
        spans = tuple((start, hidden_own, count, 0) for start, count in some for _ in range(3))
        return swap_all(split(member_at, weights * len(some), spans))

    seg, pos = own_order(segment), own_order(position)
    cos, sin = rope_tables(pos)
    seg_blocks, pos_blocks = seg[::BLOCK], pos[::BLOCK]
    half_blocks = GROUP // BLOCK // 2
    place = jnp.where(seg_blocks == 0, pos_blocks // BLOCK, half_blocks - 1 + seg_blocks)
    labels = jnp.arange(2 * half_blocks, dtype=jnp.int32)
    order = jnp.sum(jnp.where(place[None, :] == labels[:, None], labels[None, :], 0), axis=1)
    index = lax.axis_index(FSDP)
    gains = jnp.stack([attn_gain, mlp_gain])[:, None, :]
    gains = jnp.where(jnp.arange(4 * groups)[None, :, None] == index, gains, 0)
    gains, gain_rounds = combine_all(gains, groups, lambda a, b: a + b)
    gains = gains.reshape(2, features).astype(f32)
    head, pair = (0, HS, HS, 0), (0, HS, HS, 1)
    attn_pieces = swap_all(
        split(
            member_at,
            (key_weight, value_weight, query_weight, output_weight),
            (pair, pair, head, head),
        )
    )
    (attn_blocks,) = place_rows(
        member_at, [after(attn_pieces[0], *gain_rounds[0])] + attn_pieces[1:]
    )
    attn_weights = collect(attn_blocks)
    late_tokens = after(tokens, *attn_pieces[1:])
    neighbours = plane_neighbours(late_tokens)
    tokens_far = plane_far(neighbours)
    tokens_mine = [late_tokens, *neighbours, *tokens_far]
    tokens_near = [swap(piece, "tp") for piece in tokens_mine[:3]]
    normed_all = pack_normed(
        with_partner(tokens_mine, tokens_near), gains[:1], (cos, sin, place, order)
    )
    pieces_0 = mlp_exchange(chunks[:1], (*tokens_far, *tokens_near))
    (blocks_0,) = place_rows(
        member_at, [after(pieces_0[0], normed_all)] + pieces_0[1:]
    )
    late_cot = after(cotangent, *pieces_0[1:])
    cot_near = plane_neighbours(late_cot)
    cot_far = plane_far(cot_near)
    query, keys, vals = project(
        place, normed_all, attn_weights, cos, sin
    )
    mixed, logsum, peak = attention_forward(
        order, after(query, *cot_near), keys, vals
    )

    head_top = jnp.where(jnp.arange(4) == member, peak[0, :4], masked_value)
    head_top, head_rounds = combine_all(head_top, groups, jnp.maximum)

    def projected(left, column, waits=(), others=()):
        lefts = (after(left, *others) if others else left, after(left, *waits) if waits else left)
        return [
            [
                chunk_sum([lefts[j]], [attn_weights], column, j, h, bf16 if j else f32)
                for j in (0, 1)
            ]
            for h in range(2)
        ]

    attn_sums = chip_sums(*projected(mixed, 3, (), cot_far))
    arrived = reduce_first(first_operands(attn_sums))
    attn_operands = reduce_operands(attn_sums, arrived)
    attn_last = last_swaps(attn_operands, *head_rounds[0])
    hidden, own_normed = add_and_norm(attn_operands, attn_last, tokens, gains[1:])
    neighbours = plane_neighbours(own_normed)
    normed_far = plane_far(neighbours, *head_rounds[-1])
    pieces_1 = mlp_exchange(chunks[1:], normed_far)
    mlp_weights = [collect(blocks_0), collect(*place_rows(member_at, pieces_1))]
    normed_mlp = pack(with_partner([own_normed, *neighbours, *normed_far]))
    cot_all = pack(with_partner([late_cot, *cot_near, *cot_far]))

    def line_sum(partial):
        return lax.psum_scatter(partial, "group", scatter_dimension=0, tiled=True)

    inner_0, both_0 = mlp_chunk(normed_mlp, cot_all, mlp_weights[0])
    grads_0 = weight_grads((normed_mlp, both_0), (cot_all, inner_0))
    sum_0 = line_sum(grads_0)
    late_both = after(both_0, grads_0)
    early = [chunk_sum([late_both], mlp_weights[:1], 0, j, None, f32) for j in range(2)]
    inner_1, both_1, front_1, back_1 = mlp_tail(
        after(normed_mlp, *early), cot_all, mlp_weights[1], early[1], 1, bf16
    )
    inner_1, both_1, front_0, back_0 = mlp_tail(
        normed_mlp, cot_all, mlp_weights[1], early[0], 0, f32, (inner_1, both_1)
    )

    mlp_sums = chip_sums((front_0, front_1), (back_0, back_1))
    operands = first_operands(mlp_sums)
    arrived = reduce_first(operands)
    inners = [after(inner, *operands) for inner in (inner_0, inner_1)]
    out_parts = [
        [chunk_sum(inners, mlp_weights, 2, j, h, bf16 if j else f32) for j in (0, 1)]
        for h in range(2)
    ]
    mlp_operands = reduce_operands(mlp_sums, arrived)
    mlp_last = last_swaps(mlp_operands, *out_parts[0], *out_parts[1])
    d_hidden, own_d = norm_back(
        mlp_operands, mlp_last, hidden, cotangent, gains[1:], (f32, bf16)
    )
    neighbours = plane_neighbours(own_d)
    late_both = after(both_1, own_d)
    grads_1 = weight_grads((normed_mlp, late_both), (cot_all, inner_1))
    sum_1 = line_sum(after(grads_1, *neighbours))
    d_far = plane_far(neighbours, grads_1)
    d_attn_all = pack(with_partner([own_d, *neighbours, *d_far]))
    out_sums = chip_sums(*out_parts)
    out_arrived = reduce_first(first_operands(out_sums), *d_far)
    out_operands = reduce_operands(out_sums, out_arrived)
    out_last = last_swaps(out_operands)

    def send_grads(sources, *waits):
        first = after(sources[0], *waits) if waits else sources[0]
        return swap_all(pick_rows(member_at, first, *sources[1:]))


    final_0 = send_grads([sum_0], *out_arrived)
    d_mixed = product(d_attn_all, attn_weights[:, 3 * HS :]).astype(bf16)
    d_qkv = attention_backward(
        order, after(query, *out_arrived), keys, vals, logsum, d_mixed, cos, sin
    )
    pair_grads = weight_grads((normed_all, (d_qkv, 2 * HS, 0)))
    half_shape = jax.ShapeDtypeStruct((features // 2, 2 * HS), bf16)
    keep, send = vmem_call(
        functools.partial(halves_kernel, own_rows),
        "halves",
        [half_shape] * 2,
        member_at,
        pair_grads,
    )
    got = swap(send, "col")
    both_grads = weight_grads(
        (normed_all, (after(d_qkv, keep), HS, 2)), (d_attn_all, mixed)
    )
    late_qkv = after(d_qkv, both_grads, *out_last, *final_0[1:])
    qkv_parts = projected(late_qkv, 0)
    (attn_grads,) = vmem_call(
        functools.partial(join_kernel, own_rows),
        "join",
        [jax.ShapeDtypeStruct((features, 3 * HS), bf16)],
        member_at,
        after(keep, *qkv_parts[0], *qkv_parts[1]),
        got,
        both_grads,
    )
    attn_sum = line_sum(attn_grads)
    qkv_sums = chip_sums(*qkv_parts)
    arrived = reduce_first(first_operands(qkv_sums))
    qkv_operands = reduce_operands(qkv_sums, arrived)
    qkv_last = last_swaps(qkv_operands)
    (tokens_grad,) = norm_back(qkv_operands, qkv_last, tokens, d_hidden, gains[:1], (f32,))
    block_out = (hidden + reduce_last(out_operands, out_last)).astype(bf16)

    final_1 = send_grads([sum_1], *arrived)
    gate_grad, up_grad, down_grad, mlp_gain_row = mlp_final(
        member_at, gate_weight, up_weight, (chunks[:1], chunks[1:]), [final_0, final_1]
    )
    query_grad, key_grad, value_grad, output_grad, attn_gain_row = attention_final(
        member_at,
        query_weight,
        key_weight,
        value_weight,
        attention_return(member_at, after(attn_sum, *qkv_last)),
    )
    gain_grads = jnp.concatenate([attn_gain_row, mlp_gain_row], axis=1)
    gain_grads = gain_grads + swap(gain_grads, "tp")
    attn_gain_grad = gain_grads[:, 0] / attn_gain.astype(f32)
    mlp_gain_grad = gain_grads[:, 1] / mlp_gain.astype(f32)

    factor = clip_limit / jnp.maximum(head_top, clip_limit)
    query_scale = jnp.repeat(jnp.sqrt(factor), HS)
    key_factor = jnp.min(factor.reshape(2, 2), axis=1)
    key_scale = jnp.repeat(jnp.sqrt(key_factor), HS)
    query_clipped = (query_weight.astype(f32) * query_scale[None, :]).astype(bf16)
    key_clipped = (key_weight.astype(f32) * key_scale[None, :]).astype(bf16)
    return (
        block_out,
        tokens_grad,
        attn_gain_grad,
        query_grad,
        key_grad,
        value_grad,
        output_grad,
        mlp_gain_grad,
        gate_grad,
        up_grad,
        down_grad,
        head_top,
        query_clipped,
        key_clipped,
    )


def solution(mesh):
    shape = (mesh.shape["fsdp"] // 4, 2, 2, mesh.shape["tp"])
    fine = Mesh(mesh.devices.reshape(shape), ("group", "row", "col", "tp"))
    rows = P(("group", "row", "col", "tp"), None)
    weight = P(FSDP, "tp")
    gain = P(FSDP)
    heads = P("tp")
    return jax.shard_map(
        local,
        mesh=fine,
        in_specs=(
            rows, rows, P(), P(), heads, gain, weight, weight, weight, weight,
            gain, weight, weight, weight,
        ),
        out_specs=(
            rows, rows, gain, weight, weight, weight, weight, gain, weight, weight, weight,
            heads, weight, weight,
        ),
        check_vma=False,
    )
```

profile of v0, /device:TPU:0, one launch (start us, length us, event | category | flops | bytes accessed | tf_op | source)
XLA Modules:
  0.0 693.4 jit_solution(10354178714410156703)
XLA Ops:
  19.9 8.0 %collective-permute-done.13 = bf16[2,16,128]{2,1,0:T(8,128)(2,1)S(1)} collective-permute-done((bf16[2,16,128]{2,1,0:T(8,128)(2,1)S(1)}, bf16[2,16,128]{2,1,0:T(8,128)(2,1)S(1)}, u32[]{:S(2)}, u32[]{:S(2)}) %collective-permute-start.13) | collective-permute-done | bytes 8224 | tf_op jit(solution)/shard_map/ppermute | solution.py:61
  46.5 12.5 %collective-permute-done.4.refs_2_ = bf16[256,2048]{1,0:T(8,128)(2,1)} collective-permute-done((bf16[256,2048]{1,0:T(8,128)(2,1)S(1)}, bf16[256,2048]{1,0:T(8,128)(2,1)}, u32[]{:S(2)}, u32[]{:S(2)}) %collective-permute-start.4) | collective-permute-done | bytes 1048608 | tf_op jit(solution)/shard_map/ppermute | solution.py:43
  83.5 9.2 %pack_normed.1.normed_ref.refs_0_ = bf16[2048,2048]{1,0:T(8,128)(2,1)} custom-call(bf16[256,2048]{1,0:T(8,128)(2,1)S(1)} %copy-done.7, bf16[256,2048]{1,0:T(8,128)(2,1)} %collective-permute-done.3.refs_1_, bf16[256,2048]{1,0:T(8,128)(2,1)} %collective-permute-done.4.refs_2_, bf16[128,2048]{1,0:T(8,128)(2,1)S(1)} %collective-permute-done.5.refs_3_, ...), custom_call_target="tpu_custom_call" | custom-call | flops 33554432 | bytes 16777216 | tf_op jit(solution)/shard_map/pack_normed/pallas_call | solution.py:114
  92.7 10.9 %collective-permute-done.19.refs_2_ = bf16[128,1920]{1,0:T(8,128)(2,1)S(1)} collective-permute-done((bf16[128,1920]{1,0:T(8,128)(2,1)S(1)}, bf16[128,1920]{1,0:T(8,128)(2,1)S(1)}, u32[]{:S(2)}, u32[]{:S(2)}) %collective-permute-start.19) | collective-permute-done | bytes 491552 | tf_op jit(solution)/shard_map/ppermute | solution.py:47
  106.9 7.6 %all-gather.4.cloned.1.call-done.weight_ref.refs_1_ = bf16[2048,1024]{1,0:T(8,128)(2,1)} async-done(((bf16[512,1024]{1,0:T(8,128)(2,1)}), bf16[2048,1024]{1,0:T(8,128)(2,1)}) %all-gather.4.cloned.1.call-update) | async-done | bytes 4194320 | tf_op jit(solution)/shard_map/all_gather | solution.py:896
  116.9 12.0 %project.1 = (bf16[2048,256]{1,0:T(8,128)(2,1)S(1)}, bf16[2048,256]{1,0:T(8,128)(2,1)S(1)}, bf16[2048,256]{1,0:T(8,128)(2,1)S(1)}) custom-call(s32[16]{0:T(128)S(1)} %compare_select_fusion.1.refs_13_.place_ref, bf16[2048,2048]{1,0:T(8,128)(2,1)} %pack_normed.1.normed_ref.refs_0_, bf16[2048,1024]{1,0:T(8,128)(2,1)} %all-gather.4.cloned.1.call-done.weight_ref.refs_1_, ...), custom_call_target="tpu_custom_call" | custom-call | flops 6442450944 | bytes 16777216 | tf_op jit(solution)/shard_map/project/pallas_call | solution.py:701
  145.4 10.3 %collective-permute-done.24.refs_4_ = bf16[128,2048]{1,0:T(8,128)(2,1)S(1)} collective-permute-done((bf16[128,2048]{1,0:T(8,128)(2,1)S(1)}, bf16[128,2048]{1,0:T(8,128)(2,1)S(1)}, u32[]{:S(2)}, u32[]{:S(2)}) %collective-permute-start.24) | collective-permute-done | bytes 524320 | tf_op jit(solution)/shard_map/ppermute | solution.py:43
  170.6 17.6 %collective-permute-done.32 = bf16[2,256,1024]{2,1,0:T(8,128)(2,1)S(1)} collective-permute-done((bf16[2,256,1024]{2,1,0:T(8,128)(2,1)S(1)}, bf16[2,256,1024]{2,1,0:T(8,128)(2,1)S(1)}, u32[]{:S(2)}, u32[]{:S(2)}) %collective-permute-start.32) | collective-permute-done | bytes 1048608 | tf_op jit(solution)/shard_map/ppermute | solution.py:43
  194.4 8.3 %collective-permute-done.33.back_last = bf16[256,1024]{1,0:T(8,128)(2,1)S(1)} collective-permute-done((bf16[256,1024]{1,0:T(8,128)(2,1)S(1)}, bf16[256,1024]{1,0:T(8,128)(2,1)S(1)}, u32[]{:S(2)}, u32[]{:S(2)}) %collective-permute-start.33) | collective-permute-done | bytes 524320 | tf_op jit(solution)/shard_map/ppermute | solution.py:43
  213.4 15.0 %collective-permute-done.35.refs_2_ = bf16[256,2048]{1,0:T(8,128)(2,1)S(1)} collective-permute-done((bf16[256,2048]{1,0:T(8,128)(2,1)S(1)}, bf16[256,2048]{1,0:T(8,128)(2,1)S(1)}, u32[]{:S(2)}, u32[]{:S(2)}) %collective-permute-start.35) | collective-permute-done | bytes 1048608 | tf_op jit(solution)/shard_map/ppermute | solution.py:43
  234.0 6.7 collective-permute-done.40.refs_4_
  240.7 7.0 %collective-permute-done.39.refs_3_ = bf16[128,2048]{1,0:T(8,128)(2,1)S(1)} collective-permute-done((bf16[128,2048]{1,0:T(8,128)(2,1)S(1)}, bf16[128,2048]{1,0:T(8,128)(2,1)S(1)}, u32[]{:S(2)}, u32[]{:S(2)}) %collective-permute-start.39) | collective-permute-done | bytes 524320 | tf_op jit(solution)/shard_map/ppermute | solution.py:43
  285.9 24.4 %mlp_chunk.1 = (bf16[2048,640]{1,0:T(8,128)(2,1)S(1)}, bf16[2048,1280]{1,0:T(8,128)(2,1)}) custom-call(bf16[2048,2048]{1,0:T(8,128)(2,1)} %pack.3.normed_ref.refs_0_, bf16[2048,2048]{1,0:T(8,128)(2,1)} %pack.4.cot_ref.refs_1_, bf16[2048,1920]{1,0:T(8,128)(2,1)} %all-gather.6.cloned.1.call-done.weight_ref.refs_1_.refs_2_), custom_call_target="tpu_custom_call" | custom-call | flops 16106127360 | bytes 24641536 | tf_op jit(solution)/shard_map/mlp_chunk/pallas_call | solution.py:582
  310.3 24.2 %weight_grads.4 = bf16[2048,1920]{1,0:T(8,128)(2,1)} custom-call(bf16[2048,2048]{1,0:T(8,128)(2,1)} %pack.3.normed_ref.refs_0_, bf16[2048,2048]{1,0:T(8,128)(2,1)} %pack.4.cot_ref.refs_1_, bf16[2048,1280]{1,0:T(8,128)(2,1)} %get-tuple-element.143.refs_2_.refs_0_, bf16[2048,640]{1,0:T(8,128)(2,1)S(1)} %get-tuple-element.151.refs_3_.refs_0_), custom_call_target="tpu_custom_call" | custom-call | flops 16106127360 | bytes 32505856 | tf_op jit(solution)/shard_map/weight_grads/pallas_call | solution.py:664
  337.1 10.0 %chunk_sum.19.base_ref = f32[1024,2048]{1,0:T(8,128)} custom-call(bf16[2048,1280]{1,0:T(8,128)(2,1)S(1)} %copy-done.6, bf16[2048,1920]{1,0:T(8,128)(2,1)} %all-gather.6.cloned.1.call-done.weight_ref.refs_1_.refs_2_), custom_call_target="tpu_custom_call" | custom-call | flops 5368709120 | bytes 16252928 | tf_op jit(solution)/shard_map/chunk_sum/pallas_call | solution.py:628
  347.1 10.1 %chunk_sum.18.base_ref = f32[1024,2048]{1,0:T(8,128)} custom-call(bf16[2048,1280]{1,0:T(8,128)(2,1)S(1)} %copy-done.6, bf16[2048,1920]{1,0:T(8,128)(2,1)} %all-gather.6.cloned.1.call-done.weight_ref.refs_1_.refs_2_), custom_call_target="tpu_custom_call" | custom-call | flops 5368709120 | bytes 16252928 | tf_op jit(solution)/shard_map/chunk_sum/pallas_call | solution.py:628
  357.2 13.7 %mlp_tail.2 = (bf16[2048,384]{1,0:T(8,128)(2,1)S(1)}, bf16[2048,768]{1,0:T(8,128)(2,1)}, bf16[1024,1024]{1,0:T(8,128)(2,1)S(1)}, bf16[1024,1024]{1,0:T(8,128)(2,1)S(1)}) custom-call(bf16[2048,2048]{1,0:T(8,128)(2,1)} %pack.3.normed_ref.refs_0_, bf16[2048,2048]{1,0:T(8,128)(2,1)} %pack.4.cot_ref.refs_1_, ...), custom_call_target="tpu_custom_call" | custom-call | flops 8053063680 | bytes 25690112 | tf_op jit(solution)/shard_map/mlp_tail/pallas_call | solution.py:545
  373.4 15.1 %mlp_tail.3 = (bf16[2048,384]{1,0:T(8,128)(2,1)S(1)}, bf16[2048,768]{1,0:T(8,128)(2,1)S(1)}, f32[1024,1024]{1,0:T(8,128)}, f32[1024,1024]{1,0:T(8,128)}) custom-call(bf16[2048,2048]{1,0:T(8,128)(2,1)} %pack.3.normed_ref.refs_0_, bf16[2048,2048]{1,0:T(8,128)(2,1)} %pack.4.cot_ref.refs_1_, ...), custom_call_target="tpu_custom_call", output_to_operand_aliasing={{0}: (4, {}), {1}: (5, {})} | custom-call | flops 8053063680 | bytes 25690112 | tf_op jit(solution)/shard_map/mlp_tail/pallas_call | solution.py:545
  408.9 6.8 chunk_sum.22
  415.7 6.6 chunk_sum.20
  429.1 11.5 %collective-permute-done.58.front_last = bf16[256,1024]{1,0:T(8,128)(2,1)S(1)} collective-permute-done((bf16[256,1024]{1,0:T(8,128)(2,1)S(1)}, bf16[256,1024]{1,0:T(8,128)(2,1)S(1)}, u32[]{:S(2)}, u32[]{:S(2)}) %collective-permute-start.58) | collective-permute-done | bytes 524320 | tf_op jit(solution)/shard_map/ppermute | solution.py:43
  447.9 15.7 %weight_grads.5 = bf16[2048,1152]{1,0:T(8,128)(2,1)} custom-call(bf16[2048,2048]{1,0:T(8,128)(2,1)} %pack.3.normed_ref.refs_0_, bf16[2048,2048]{1,0:T(8,128)(2,1)} %pack.4.cot_ref.refs_1_, bf16[2048,768]{1,0:T(8,128)(2,1)S(1)} %copy-done.22, bf16[2048,384]{1,0:T(8,128)(2,1)S(1)} %get-tuple-element.153.refs_1_.refs_3_), custom_call_target="tpu_custom_call" | custom-call | flops 9663676416 | bytes 26214400 | tf_op jit(solution)/shard_map/weight_grads/pallas_call | solution.py:664
  463.6 6.5 collective-permute-done.63.refs_2_
  492.1 6.4 pack.5.refs_1_
  498.4 6.0 convolution_convert_fusion.mixed_ref
  504.4 9.8 %collective-permute-done.65 = bf16[512,1024]{1,0:T(8,128)(2,1)S(1)} collective-permute-done((bf16[512,1024]{1,0:T(8,128)(2,1)S(1)}, bf16[512,1024]{1,0:T(8,128)(2,1)S(1)}, u32[]{:S(2)}, u32[]{:S(2)}) %collective-permute-start.65) | collective-permute-done | bytes 1048608 | tf_op jit(solution)/shard_map/ppermute | solution.py:43
  521.6 11.3 %attention_backward.1.refs_1_.refs_2_.refs_0_ = bf16[2048,768]{1,0:T(8,128)(2,1)} custom-call(s32[16]{0:T(128)S(1)} %select_reduce_fusion.refs_14_.order_ref, bf16[2048,256]{1,0:T(8,128)(2,1)S(1)} %copy-done.67, bf16[2048,256]{1,0:T(8,128)(2,1)S(1)} %copy-done.69, bf16[2048,256]{1,0:T(8,128)(2,1)S(1)} %copy-done.71, f32[2048,1]{1,0:T(8,128)S(1)} %copy-done.73, ...), custom_call_target="tpu_custom_call" | custom-call | flops 5368709120 | bytes 10485760 | tf_op jit(solution)/shard_map/attention_backward/pallas_call | solution.py:842
  540.8 9.1 %weight_grads.6.grads_ref = bf16[2048,512]{1,0:T(8,128)(2,1)S(1)} custom-call(bf16[2048,2048]{1,0:T(8,128)(2,1)} %pack_normed.1.normed_ref.refs_0_, bf16[2048,768]{1,0:T(8,128)(2,1)S(1)} %copy-done), custom_call_target="tpu_custom_call" | custom-call | flops 4294967296 | bytes 12582912 | tf_op jit(solution)/shard_map/weight_grads/pallas_call | solution.py:664
  551.3 11.1 %weight_grads.7.both_ref = bf16[2048,512]{1,0:T(8,128)(2,1)S(1)} custom-call(bf16[2048,2048]{1,0:T(8,128)(2,1)} %pack_normed.1.normed_ref.refs_0_, bf16[2048,2048]{1,0:T(8,128)(2,1)} %pack.5.refs_1_, bf16[2048,768]{1,0:T(8,128)(2,1)} %attention_backward.1.refs_1_.refs_2_.refs_0_, bf16[2048,256]{1,0:T(8,128)(2,1)S(1)} %copy-done.5), custom_call_target="tpu_custom_call" | custom-call | flops 4294967296 | bytes 20971520 | tf_op jit(solution)/shard_map/weight_grads/pallas_call | solution.py:664
  583.3 6.1 collective-permute-done.81
  599.7 19.0 %collective-permute-done.82 = bf16[2,256,1024]{2,1,0:T(8,128)(2,1)} collective-permute-done((bf16[2,256,1024]{2,1,0:T(8,128)(2,1)}, bf16[2,256,1024]{2,1,0:T(8,128)(2,1)}, u32[]{:S(2)}, u32[]{:S(2)}) %collective-permute-start.82) | collective-permute-done | bytes 1048608 | tf_op jit(solution)/shard_map/ppermute | solution.py:43
  649.0 8.5 %collective-permute-done.91.refs_6_ = bf16[128,1152]{1,0:T(8,128)(2,1)} collective-permute-done((bf16[128,1152]{1,0:T(8,128)(2,1)}, bf16[128,1152]{1,0:T(8,128)(2,1)}, u32[]{:S(2)}, u32[]{:S(2)}) %collective-permute-start.91) | collective-permute-done | bytes 294944 | tf_op jit(solution)/shard_map/ppermute | solution.py:47
  (529 shorter events, 320.6 us)
Async XLA Ops:
  7.2 107.3 %all-gather.4.cloned.1.call-start = ((), (), s32[]{:S(2)}) async-start(), calls=%async_computation.3 | async-start | bytes 5242880 | tf_op jit(solution)/shard_map/all_gather | solution.py:896
  32.6 253.3 %all-gather.6.cloned.1.call-start = ((), (), s32[]{:S(2)}) async-start(), calls=%async_computation.4 | async-start | bytes 9830400 | tf_op jit(solution)/shard_map/all_gather | solution.py:896
  44.9 24.9 %collective-permute-start.7 = (bf16[256,2048]{1,0:T(8,128)(2,1)S(1)}, bf16[256,2048]{1,0:T(8,128)(2,1)}, u32[]{:S(2)}, u32[]{:S(2)}) collective-permute-start(bf16[256,2048]{1,0:T(8,128)(2,1)S(1)} %copy-done.7), channel_id=1, source_target_pairs={{0,1},{1,0},{2,3},{3,2},{4,5},{5,4},{6,7},{7,6},{8,9},{9,8},{10,11... | collective-permute-start | bytes 3145736 | tf_op jit(solution)/shard_map/ppermute | solution.py:43
  105.1 252.1 %all-gather.8.cloned.1.call-start = ((), (), s32[]{:S(2)}) async-start(), calls=%async_computation.5 | async-start | bytes 5898240 | tf_op jit(solution)/shard_map/all_gather | solution.py:896
  105.3 23.7 %collective-permute-start.22 = (bf16[256,2048]{1,0:T(8,128)(2,1)}, bf16[256,2048]{1,0:T(8,128)(2,1)}, u32[]{:S(2)}, u32[]{:S(2)}) collective-permute-start(bf16[256,2048]{1,0:T(8,128)(2,1)} %base_ref.1), channel_id=1, source_target_pairs={{0,4},{4,0},{1,5},{5,1},{2,6},{6,2},{3,7},{7,3},{8,12},{12,8},{9,1... | collective-permute-start | bytes 3145736 | tf_op jit(solution)/shard_map/ppermute | solution.py:43
  105.8 23.9 %collective-permute-start.21 = (bf16[256,2048]{1,0:T(8,128)(2,1)}, bf16[256,2048]{1,0:T(8,128)(2,1)}, u32[]{:S(2)}, u32[]{:S(2)}) collective-permute-start(bf16[256,2048]{1,0:T(8,128)(2,1)} %base_ref.1), channel_id=1, source_target_pairs={{0,2},{2,0},{1,3},{3,1},{4,6},{6,4},{5,7},{7,5},{8,10},{10,8},{9,1... | collective-permute-start | bytes 3145736 | tf_op jit(solution)/shard_map/ppermute | solution.py:43
  138.1 24.4 %collective-permute-start.31 = (bf16[1024,1024]{1,0:T(8,128)(2,1)}, bf16[1024,1024]{1,0:T(8,128)(2,1)}, u32[]{:S(2)}, u32[]{:S(2)}) collective-permute-start(bf16[1024,1024]{1,0:T(8,128)(2,1)} %chunk_sum.17), channel_id=1, source_target_pairs={{0,1},{1,0},{2,3},{3,2},{4,5},{5,4},{6,7},{7,6},{8,9},{9,8},{10,11... | collective-permute-start | bytes 6291464 | tf_op jit(solution)/shard_map/ppermute | solution.py:43
  140.1 24.7 %collective-permute-start.25 = (bf16[1024,1024]{1,0:T(8,128)(2,1)S(1)}, bf16[1024,1024]{1,0:T(8,128)(2,1)}, u32[]{:S(2)}, u32[]{:S(2)}) collective-permute-start(bf16[1024,1024]{1,0:T(8,128)(2,1)S(1)} %chunk_sum.15), channel_id=1, source_target_pairs={{0,1},{1,0},{2,3},{3,2},{4,5},{5,4},{6,7},{7,6},{8,9},{9,8},{10,11... | collective-permute-start | bytes 6291464 | tf_op jit(solution)/shard_map/ppermute | solution.py:43
  164.0 24.1 %collective-permute-start.32 = (bf16[2,256,1024]{2,1,0:T(8,128)(2,1)S(1)}, bf16[2,256,1024]{2,1,0:T(8,128)(2,1)S(1)}, u32[]{:S(2)}, u32[]{:S(2)}) collective-permute-start(bf16[2,256,1024]{2,1,0:T(8,128)(2,1)S(1)} %bitcast.95), channel_id=1, source_target_pairs={{0,4},{4,0},{1,5},{5,1},{2,6},{6,2},{3,7},{7,3},{8,12},{12,8},{9,1... | collective-permute-start | bytes 3145736 | tf_op jit(solution)/shard_map/ppermute | solution.py:43
  166.5 24.9 %collective-permute-start.26 = (bf16[512,1024]{1,0:T(8,128)(2,1)S(1)}, bf16[512,1024]{1,0:T(8,128)(2,1)S(1)}, u32[]{:S(2)}, u32[]{:S(2)}) collective-permute-start(bf16[512,1024]{1,0:T(8,128)(2,1)S(1)} %pad_maximum_fusion), channel_id=1, source_target_pairs={{0,2},{2,0},{1,3},{3,1},{4,6},{6,4},{5,7},{7,5},{8,10},{10,8},{9,1... | collective-permute-start | bytes 3145736 | tf_op jit(solution)/shard_map/ppermute | solution.py:43
  167.1 23.9 %collective-permute-start.29 = (f32[4]{0:T(128)S(1)}, f32[4]{0:T(128)S(1)}, u32[]{:S(2)}, u32[]{:S(2)}) collective-permute-start(f32[4]{0:T(128)S(1)} %compare_select_fusion), channel_id=1, source_target_pairs={{0,6},{2,4},{4,2},{6,0},{8,14},{10,12},{12,10},{14,8},{16,22},{18,... | collective-permute-start | bytes 56 | tf_op jit(solution)/shard_map/ppermute | solution.py:61
  207.6 24.7 %collective-permute-start.34 = (bf16[256,2048]{1,0:T(8,128)(2,1)S(1)}, bf16[256,2048]{1,0:T(8,128)(2,1)S(1)}, u32[]{:S(2)}, u32[]{:S(2)}) collective-permute-start(bf16[256,2048]{1,0:T(8,128)(2,1)S(1)} %get-tuple-element.129.refs_0_), channel_id=1, source_target_pairs={{0,2},{2,0},{1,3},{3,1},{4,6},{6,4},{5,7},{7,5},{8,10},{10,8},{9,1... | collective-permute-start | bytes 3145736 | tf_op jit(solution)/shard_map/ppermute | solution.py:43
  259.5 273.4 %reduce-scatter.4.cloned.1.call-start = ((), (), s32[]{:S(2)}) async-start(), calls=%async_computation.6 | async-start | bytes 9830400 | tf_op jit(solution)/shard_map/reduce_scatter | solution.py:975
  334.5 294.1 %reduce-scatter.8.cloned.1.call-start = ((), (), s32[]{:S(2)}) async-start(), calls=%async_computation.8 | async-start | bytes 5898240 | tf_op jit(solution)/shard_map/reduce_scatter | solution.py:975
  393.2 29.1 %collective-permute-start.59 = (bf16[2,256,1024]{2,1,0:T(8,128)(2,1)}, bf16[2,256,1024]{2,1,0:T(8,128)(2,1)}, u32[]{:S(2)}, u32[]{:S(2)}) collective-permute-start(bf16[2,256,1024]{2,1,0:T(8,128)(2,1)} %bitcast.9), channel_id=1, source_target_pairs={{0,4},{4,0},{1,5},{5,1},{2,6},{6,2},{3,7},{7,3},{8,12},{12,8},{9,1... | collective-permute-start | bytes 3145736 | tf_op jit(solution)/shard_map/ppermute | solution.py:43
  396.6 28.3 %collective-permute-start.57 = (bf16[512,1024]{1,0:T(8,128)(2,1)}, bf16[512,1024]{1,0:T(8,128)(2,1)S(1)}, u32[]{:S(2)}, u32[]{:S(2)}) collective-permute-start(bf16[512,1024]{1,0:T(8,128)(2,1)} %pad_maximum_fusion.1), channel_id=1, source_target_pairs={{0,2},{2,0},{1,3},{3,1},{4,6},{6,4},{5,7},{7,5},{8,10},{10,8},{9,1... | collective-permute-start | bytes 3145736 | tf_op jit(solution)/shard_map/ppermute | solution.py:43
  446.3 23.7 %collective-permute-start.63 = (bf16[256,2048]{1,0:T(8,128)(2,1)S(1)}, bf16[256,2048]{1,0:T(8,128)(2,1)S(1)}, u32[]{:S(2)}, u32[]{:S(2)}) collective-permute-start(bf16[256,2048]{1,0:T(8,128)(2,1)S(1)} %get-tuple-element.156.refs_0_), channel_id=1, source_target_pairs={{0,4},{4,0},{1,5},{5,1},{2,6},{6,2},{3,7},{7,3},{8,12},{12,8},{9,1... | collective-permute-start | bytes 3145736 | tf_op jit(solution)/shard_map/ppermute | solution.py:43
  470.5 172.4 %reduce-scatter.6.cloned.1.call-start = ((), (), s32[]{:S(2)}) async-start(), calls=%async_computation.7 | async-start | bytes 3932160 | tf_op jit(solution)/shard_map/reduce_scatter | solution.py:975
  489.0 25.2 %collective-permute-start.65 = (bf16[512,1024]{1,0:T(8,128)(2,1)S(1)}, bf16[512,1024]{1,0:T(8,128)(2,1)S(1)}, u32[]{:S(2)}, u32[]{:S(2)}) collective-permute-start(bf16[512,1024]{1,0:T(8,128)(2,1)S(1)} %pad_maximum_fusion.2), channel_id=1, source_target_pairs={{0,2},{2,0},{1,3},{3,1},{4,6},{6,4},{5,7},{7,5},{8,10},{10,8},{9,1... | collective-permute-start | bytes 3145736 | tf_op jit(solution)/shard_map/ppermute | solution.py:43
  490.1 25.0 %collective-permute-start.68 = (bf16[2,256,1024]{2,1,0:T(8,128)(2,1)}, bf16[2,256,1024]{2,1,0:T(8,128)(2,1)S(1)}, u32[]{:S(2)}, u32[]{:S(2)}) collective-permute-start(bf16[2,256,1024]{2,1,0:T(8,128)(2,1)} %bitcast.15), channel_id=1, source_target_pairs={{0,4},{4,0},{1,5},{5,1},{2,6},{6,2},{3,7},{7,3},{8,12},{12,8},{9,1... | collective-permute-start | bytes 3145736 | tf_op jit(solution)/shard_map/ppermute | solution.py:43
  517.8 32.3 %collective-permute-start.69 = (bf16[256,1024]{1,0:T(8,128)(2,1)S(1)}, bf16[256,1024]{1,0:T(8,128)(2,1)S(1)}, u32[]{:S(2)}, u32[]{:S(2)}) collective-permute-start(bf16[256,1024]{1,0:T(8,128)(2,1)S(1)} %fusion.14), channel_id=1, source_target_pairs={{0,2},{2,0},{1,3},{3,1},{4,6},{6,4},{5,7},{7,5},{8,10},{10,8},{9,1... | collective-permute-start | bytes 1572872 | tf_op jit(solution)/shard_map/ppermute | solution.py:43
  520.2 42.2 %collective-permute-start.66 = (bf16[256,1024]{1,0:T(8,128)(2,1)S(1)}, bf16[256,1024]{1,0:T(8,128)(2,1)S(1)}, u32[]{:S(2)}, u32[]{:S(2)}) collective-permute-start(bf16[256,1024]{1,0:T(8,128)(2,1)S(1)} %fusion.18), channel_id=1, source_target_pairs={{0,4},{4,0},{1,5},{5,1},{2,6},{6,2},{3,7},{7,3},{8,12},{12,8},{9,1... | collective-permute-start | bytes 1572872 | tf_op jit(solution)/shard_map/ppermute | solution.py:43
  535.4 27.0 %collective-permute-start.75 = (bf16[128,1920]{1,0:T(8,128)(2,1)S(1)}, bf16[128,1920]{1,0:T(8,128)(2,1)S(1)}, u32[]{:S(2)}, u32[]{:S(2)}) collective-permute-start(bf16[128,1920]{1,0:T(8,128)(2,1)S(1)} %get-tuple-element.168), channel_id=1, source_target_pairs={{0,2},{2,0},{4,6},{6,4},{1,3},{3,1},{5,7},{7,5},{8,10},{10,8},{12,... | collective-permute-start | bytes 1474568 | tf_op jit(solution)/shard_map/ppermute | solution.py:47
  536.3 26.1 %collective-permute-start.76 = (bf16[128,1920]{1,0:T(8,128)(2,1)S(1)}, bf16[128,1920]{1,0:T(8,128)(2,1)S(1)}, u32[]{:S(2)}, u32[]{:S(2)}) collective-permute-start(bf16[128,1920]{1,0:T(8,128)(2,1)S(1)} %get-tuple-element.169), channel_id=1, source_target_pairs={{0,4},{2,6},{4,0},{6,2},{1,5},{3,7},{5,1},{7,3},{8,12},{10,14},{12... | collective-permute-start | bytes 1474568 | tf_op jit(solution)/shard_map/ppermute | solution.py:47
  537.1 25.3 %collective-permute-start.77 = (bf16[128,1920]{1,0:T(8,128)(2,1)S(1)}, bf16[128,1920]{1,0:T(8,128)(2,1)S(1)}, u32[]{:S(2)}, u32[]{:S(2)}) collective-permute-start(bf16[128,1920]{1,0:T(8,128)(2,1)S(1)} %get-tuple-element.170), channel_id=1, source_target_pairs={{0,6},{2,4},{4,2},{6,0},{1,7},{3,5},{5,3},{7,1},{8,14},{10,12},{12... | collective-permute-start | bytes 1474568 | tf_op jit(solution)/shard_map/ppermute | solution.py:47
  550.1 30.6 %collective-permute-start.84 = (bf16[1024,512]{1,0:T(8,128)(2,1)S(1)}, bf16[1024,512]{1,0:T(8,128)(2,1)S(1)}, u32[]{:S(2)}, u32[]{:S(2)}) collective-permute-start(bf16[1024,512]{1,0:T(8,128)(2,1)S(1)} %get-tuple-element.174), channel_id=1, source_target_pairs={{0,2},{2,0},{1,3},{3,1},{4,6},{6,4},{5,7},{7,5},{8,10},{10,8},{9,1... | collective-permute-start | bytes 3145736 | tf_op jit(solution)/shard_map/ppermute | solution.py:43
  593.1 25.5 %collective-permute-start.82 = (bf16[2,256,1024]{2,1,0:T(8,128)(2,1)}, bf16[2,256,1024]{2,1,0:T(8,128)(2,1)}, u32[]{:S(2)}, u32[]{:S(2)}) collective-permute-start(bf16[2,256,1024]{2,1,0:T(8,128)(2,1)} %bitcast.21), channel_id=1, source_target_pairs={{0,4},{4,0},{1,5},{5,1},{2,6},{6,2},{3,7},{7,3},{8,12},{12,8},{9,1... | collective-permute-start | bytes 3145736 | tf_op jit(solution)/shard_map/ppermute | solution.py:43
  596.4 27.9 %collective-permute-start.79 = (bf16[512,1024]{1,0:T(8,128)(2,1)}, bf16[512,1024]{1,0:T(8,128)(2,1)}, u32[]{:S(2)}, u32[]{:S(2)}) collective-permute-start(bf16[512,1024]{1,0:T(8,128)(2,1)} %pad_maximum_fusion.3), channel_id=1, source_target_pairs={{0,2},{2,0},{1,3},{3,1},{4,6},{6,4},{5,7},{7,5},{8,10},{10,8},{9,1... | collective-permute-start | bytes 3145736 | tf_op jit(solution)/shard_map/ppermute | solution.py:43
  632.0 25.6 %collective-permute-start.91 = (bf16[128,1152]{1,0:T(8,128)(2,1)}, bf16[128,1152]{1,0:T(8,128)(2,1)}, u32[]{:S(2)}, u32[]{:S(2)}) collective-permute-start(bf16[128,1152]{1,0:T(8,128)(2,1)} %get-tuple-element.188), channel_id=1, source_target_pairs={{0,4},{2,6},{4,0},{6,2},{1,5},{3,7},{5,1},{7,3},{8,12},{10,14},{12... | collective-permute-start | bytes 884744 | tf_op jit(solution)/shard_map/ppermute | solution.py:47
  633.1 26.6 %collective-permute-start.92 = (bf16[128,1152]{1,0:T(8,128)(2,1)}, bf16[128,1152]{1,0:T(8,128)(2,1)}, u32[]{:S(2)}, u32[]{:S(2)}) collective-permute-start(bf16[128,1152]{1,0:T(8,128)(2,1)} %get-tuple-element.189), channel_id=1, source_target_pairs={{0,6},{2,4},{4,2},{6,0},{1,7},{3,5},{5,3},{7,1},{8,14},{10,12},{12... | collective-permute-start | bytes 884744 | tf_op jit(solution)/shard_map/ppermute | solution.py:47
  645.5 26.5 %collective-permute-start.85 = (bf16[128,512]{1,0:T(8,128)(2,1)}, bf16[128,512]{1,0:T(8,128)(2,1)}, u32[]{:S(2)}, u32[]{:S(2)}) collective-permute-start(bf16[128,512]{1,0:T(8,128)(2,1)} %get-tuple-element.177), channel_id=1, source_target_pairs={{0,2},{2,0},{4,6},{6,4},{1,3},{3,1},{5,7},{7,5},{8,10},{10,8},{12,... | collective-permute-start | bytes 393224 | tf_op jit(solution)/shard_map/ppermute | solution.py:47
  646.9 25.1 %collective-permute-start.86 = (bf16[128,512]{1,0:T(8,128)(2,1)}, bf16[128,512]{1,0:T(8,128)(2,1)}, u32[]{:S(2)}, u32[]{:S(2)}) collective-permute-start(bf16[128,512]{1,0:T(8,128)(2,1)} %get-tuple-element.178), channel_id=1, source_target_pairs={{0,4},{2,6},{4,0},{6,2},{1,5},{3,7},{5,1},{7,3},{8,12},{10,14},{12... | collective-permute-start | bytes 393224 | tf_op jit(solution)/shard_map/ppermute | solution.py:47
  (180 other events, 1648.7 us)
Sparse Core Ops, SparseCore 0:
  32.7 81.6 all-gather.3
  116.6 139.5 all-gather.5
  259.6 88.3 all-gather.7
  350.2 134.6 reduce-scatter.3
  487.1 85.7 reduce-scatter.7
  582.9 59.8 reduce-scatter.5
where the time goes:
time: 700 us; the launch traced here: 693 us
  Pallas kernels  263 us (38%)
  waiting for transfers between devices  219 us (31%)
  starting transfers between devices  77.3 us (11%)
  other arithmetic  56.2 us (8%)
  local copies, waits for them, and re-layouts  55.8 us (8%)
  between operations  16.1 us (2%)
    ppermute x62, waiting for transfers between devices, swap(): return lax.ppermute(block, axis, [(0, 1), (1, 0)])  170 us
    pallas_call x14, Pallas kernels, chunk_sum(): pl.pallas_call(functools.partial(sum_kernel, count), grid=(steps,), in_sp...  70.3 us
    pallas_call x4, Pallas kernels, weight_grads(): pl.pallas_call(functools.partial(grads_kernel, count), grid=(features //...  60.1 us
    unnamed x241, local copies, waits for them, and re-layouts  47.6 us
    ppermute x62, starting transfers between devices, swap(): return lax.ppermute(block, axis, [(0, 1), (1, 0)])  38 us
    pallas_call x2, Pallas kernels, mlp_tail(): pl.pallas_call(functools.partial(tail_kernel, width), grid=(steps,), in_s...  28.8 us
    ppermute x18, waiting for transfers between devices, swap_plane(): return lax.ppermute(block, PLANE, [(i, i ^ distance) for i in range(4)])  26.4 us
    pallas_call x1, Pallas kernels, mlp_chunk(): pl.pallas_call(functools.partial(mlp_kernel, width), grid=(tokens // tile...  24.4 us
  transfers between devices with their start and end apart: 100, of which 39 were waited for; matrix products, arithmetic and copies ran while one was open for 11% of the time, Pallas kernels for 37%

commit v1 on v0

--- a/solution.py
+++ b/solution.py
@@ -189,12 +189,6 @@
     )
 
 
-def reduce_last(operands, swapped):
-    return jnp.concatenate(
-        [keep + last.astype(f32) for (keep, _), last in zip(operands, swapped)], axis=1
-    )
-
-
 def joined(front_ref, front_last_ref, back_ref, back_last_ref):
     return jnp.concatenate(
         [
@@ -227,6 +221,25 @@
         compiler_params=pltpu.CompilerParams(vmem_limit_bytes=VMEM_LIMIT),
         name="add_and_norm",
     )(*halves, tokens, gain)
+
+
+def out_kernel(front, front_last, back, back_last, hidden_ref, out_ref):
+    out_ref[...] = (hidden_ref[...] + joined(front, front_last, back, back_last)).astype(bf16)
+
+
+def add_sum(operands, last, hidden):
+    halves = [part for (keep, _), got in zip(operands, last) for part in (keep, got)]
+    return pl.pallas_call(
+        out_kernel,
+        in_specs=[pl.BlockSpec(memory_space=pltpu.VMEM)] * 5,
+        out_specs=pl.BlockSpec(memory_space=pltpu.VMEM),
+        out_shape=jax.ShapeDtypeStruct(hidden.shape, bf16),
+        cost_estimate=pl.CostEstimate(
+            flops=2 * hidden.size, bytes_accessed=12 * hidden.size, transcendentals=0
+        ),
+        compiler_params=pltpu.CompilerParams(vmem_limit_bytes=VMEM_LIMIT),
+        name="add_sum",
+    )(*halves, hidden)
 
 
 def back_kernel(front, front_last, back, back_last, values_ref, base_ref, gain_ref, *outs):
@@ -921,7 +934,7 @@
         )
     )
     (attn_blocks,) = place_rows(
-        member_at, [after(attn_pieces[0], *gain_rounds[0])] + attn_pieces[1:]
+        member_at, attn_pieces
     )
     attn_weights = collect(attn_blocks)
     late_tokens = after(tokens, *attn_pieces[1:])
@@ -934,7 +947,7 @@
     )
     pieces_0 = mlp_exchange(chunks[:1], (*tokens_far, *tokens_near))
     (blocks_0,) = place_rows(
-        member_at, [after(pieces_0[0], normed_all)] + pieces_0[1:]
+        member_at, [after(pieces_0[0], normed_all, *gain_rounds[-1])] + pieces_0[1:]
     )
     late_cot = after(cotangent, *pieces_0[1:])
     cot_near = plane_neighbours(late_cot)
@@ -1018,9 +1031,9 @@
     final_0 = send_grads([sum_0], *out_arrived)
     d_mixed = product(d_attn_all, attn_weights[:, 3 * HS :]).astype(bf16)
     d_qkv = attention_backward(
-        order, after(query, *out_arrived), keys, vals, logsum, d_mixed, cos, sin
-    )
-    pair_grads = weight_grads((normed_all, (d_qkv, 2 * HS, 0)))
+        order, query, keys, vals, logsum, d_mixed, cos, sin
+    )
+    pair_grads = weight_grads((normed_all, (after(d_qkv, *out_arrived), 2 * HS, 0)))
     half_shape = jax.ShapeDtypeStruct((features // 2, 2 * HS), bf16)
     keep, send = vmem_call(
         functools.partial(halves_kernel, own_rows),
@@ -1046,22 +1059,25 @@
     )
     attn_sum = line_sum(attn_grads)
     qkv_sums = chip_sums(*qkv_parts)
-    arrived = reduce_first(first_operands(qkv_sums))
+    final_1 = send_grads([sum_1], attn_grads)
+    arrived = reduce_first(first_operands(qkv_sums), *final_1[1:])
     qkv_operands = reduce_operands(qkv_sums, arrived)
     qkv_last = last_swaps(qkv_operands)
     (tokens_grad,) = norm_back(qkv_operands, qkv_last, tokens, d_hidden, gains[:1], (f32,))
-    block_out = (hidden + reduce_last(out_operands, out_last)).astype(bf16)
-
-    final_1 = send_grads([sum_1], *arrived)
+    block_out = add_sum(out_operands, out_last, hidden)
+
     gate_grad, up_grad, down_grad, mlp_gain_row = mlp_final(
         member_at, gate_weight, up_weight, (chunks[:1], chunks[1:]), [final_0, final_1]
+    )
+    attn_parts = attention_return(
+        member_at, after(attn_sum, *qkv_last, mlp_gain_row, block_out)
     )
     query_grad, key_grad, value_grad, output_grad, attn_gain_row = attention_final(
         member_at,
         query_weight,
         key_weight,
         value_weight,
-        attention_return(member_at, after(attn_sum, *qkv_last)),
+        [after(attn_parts[0], tokens_grad)] + attn_parts[1:],
     )
     gain_grads = jnp.concatenate([attn_gain_row, mlp_gain_row], axis=1)
     gain_grads = gain_grads + swap(gain_grads, "tp")

time: 700 us -> 679 us (0.970)
  waiting for transfers between devices: 219 us -> 196 us
  starting transfers between devices: 77.3 us -> 91.7 us
  other arithmetic: 56.2 us -> 47.9 us
    ppermute x62, waiting for transfers between devices: 170 us -> 150 us  [swap(): return lax.ppermute(block, axis, [(0, 1), (1, 0)])]
    ppermute x18, waiting for transfers between devices: 26.4 us -> 45.1 us  [swap_plane(): return lax.ppermute(block, PLANE, [(i, i ^ distance) for i in range(4)])]
    ppermute x12, waiting for transfers between devices: 15.8 us -> 0.95 us  [combine_all(): arrived.append(lax.ppermute(values, FSDP, route))]
    all_gather x3, waiting for transfers between devices: 7.61 us -> 0.6 us  [collect(): return lax.all_gather(blocks, 'group', axis=0, tiled=True)]
    another operation x4, other arithmetic: 2.59 us -> 9.59 us
    unnamed x241 -> x239, local copies, waits for them, and re-layouts: 47.6 us -> 44.2 us
  transfers between devices with their start and end apart: 100 -> 100, of which waited for: 39 -> 43; matrix products, arithmetic and copies ran while one was open for 11% -> 10% of each run, Pallas kernels for 37% -> 39%
where the time goes in v1:
time: 679 us; the launch traced here: 673 us
  Pallas kernels  264 us (39%)
  waiting for transfers between devices  196 us (29%)
  starting transfers between devices  91.7 us (14%)
  local copies, waits for them, and re-layouts  50.8 us (7%)
  other arithmetic  47.9 us (7%)
  between operations  15.9 us (2%)
    ppermute x62, waiting for transfers between devices, swap(): return lax.ppermute(block, axis, [(0, 1), (1, 0)])  150 us
    pallas_call x14, Pallas kernels, chunk_sum(): pl.pallas_call(functools.partial(sum_kernel, count), grid=(steps,), in_sp...  70.3 us
    pallas_call x4, Pallas kernels, weight_grads(): pl.pallas_call(functools.partial(grads_kernel, count), grid=(features //...  59.8 us
    ppermute x18, waiting for transfers between devices, swap_plane(): return lax.ppermute(block, PLANE, [(i, i ^ distance) for i in range(4)])  45.1 us
    unnamed x239, local copies, waits for them, and re-layouts  44.2 us
    ppermute x62, starting transfers between devices, swap(): return lax.ppermute(block, axis, [(0, 1), (1, 0)])  42 us
    pallas_call x2, Pallas kernels, mlp_tail(): pl.pallas_call(functools.partial(tail_kernel, width), grid=(steps,), in_s...  29.9 us
    ppermute x18, starting transfers between devices, swap_plane(): return lax.ppermute(block, PLANE, [(i, i ^ distance) for i in range(4)])  25.8 us
  transfers between devices with their start and end apart: 100, of which 43 were waited for; matrix products, arithmetic and copies ran while one was open for 10% of the time, Pallas kernels for 39%

profile of v1, /device:TPU:0, one launch (start us, length us, event | category | flops | bytes accessed | tf_op | source)
XLA Modules:
  0.0 672.8 jit_solution(13644481905363704128)
XLA Ops:
  21.3 6.2 collective-permute-done.1.refs_2_
  45.8 13.1 %collective-permute-done.4.refs_2_ = bf16[256,2048]{1,0:T(8,128)(2,1)} collective-permute-done((bf16[256,2048]{1,0:T(8,128)(2,1)S(1)}, bf16[256,2048]{1,0:T(8,128)(2,1)}, u32[]{:S(2)}, u32[]{:S(2)}) %collective-permute-start.4) | collective-permute-done | bytes 1048608 | tf_op jit(solution)/shard_map/ppermute | solution.py:43
  85.0 9.2 %pack_normed.1.normed_ref.refs_0_ = bf16[2048,2048]{1,0:T(8,128)(2,1)} custom-call(bf16[256,2048]{1,0:T(8,128)(2,1)S(1)} %copy-done.7, bf16[256,2048]{1,0:T(8,128)(2,1)} %collective-permute-done.3.refs_1_, bf16[256,2048]{1,0:T(8,128)(2,1)} %collective-permute-done.4.refs_2_, bf16[128,2048]{1,0:T(8,128)(2,1)S(1)} %collective-permute-done.5.refs_3_, ...), custom_call_target="tpu_custom_call" | custom-call | flops 33554432 | bytes 16777216 | tf_op jit(solution)/shard_map/pack_normed/pallas_call | solution.py:114
  95.4 9.0 %collective-permute-done.19.refs_2_ = bf16[128,1920]{1,0:T(8,128)(2,1)S(1)} collective-permute-done((bf16[128,1920]{1,0:T(8,128)(2,1)S(1)}, bf16[128,1920]{1,0:T(8,128)(2,1)S(1)}, u32[]{:S(2)}, u32[]{:S(2)}) %collective-permute-start.19) | collective-permute-done | bytes 491552 | tf_op jit(solution)/shard_map/ppermute | solution.py:47
  113.0 12.0 %project.1 = (bf16[2048,256]{1,0:T(8,128)(2,1)S(1)}, bf16[2048,256]{1,0:T(8,128)(2,1)S(1)}, bf16[2048,256]{1,0:T(8,128)(2,1)S(1)}) custom-call(s32[16]{0:T(128)S(1)} %compare_select_fusion.1.refs_13_.place_ref, bf16[2048,2048]{1,0:T(8,128)(2,1)} %pack_normed.1.normed_ref.refs_0_, bf16[2048,1024]{1,0:T(8,128)(2,1)} %all-gather.4.cloned.1.call-done.weight_ref.refs_1_, ...), custom_call_target="tpu_custom_call" | custom-call | flops 6442450944 | bytes 16777216 | tf_op jit(solution)/shard_map/project/pallas_call | solution.py:714
  125.1 7.3 %collective-permute-done.22.refs_2_ = bf16[256,2048]{1,0:T(8,128)(2,1)} collective-permute-done((bf16[256,2048]{1,0:T(8,128)(2,1)}, bf16[256,2048]{1,0:T(8,128)(2,1)}, u32[]{:S(2)}, u32[]{:S(2)}) %collective-permute-start.22) | collective-permute-done | bytes 1048608 | tf_op jit(solution)/shard_map/ppermute | solution.py:43
  148.1 10.6 %collective-permute-done.24.refs_4_ = bf16[128,2048]{1,0:T(8,128)(2,1)S(1)} collective-permute-done((bf16[128,2048]{1,0:T(8,128)(2,1)S(1)}, bf16[128,2048]{1,0:T(8,128)(2,1)S(1)}, u32[]{:S(2)}, u32[]{:S(2)}) %collective-permute-start.24) | collective-permute-done | bytes 524320 | tf_op jit(solution)/shard_map/ppermute | solution.py:43
  174.1 15.9 %collective-permute-done.32 = bf16[2,256,1024]{2,1,0:T(8,128)(2,1)S(1)} collective-permute-done((bf16[2,256,1024]{2,1,0:T(8,128)(2,1)S(1)}, bf16[2,256,1024]{2,1,0:T(8,128)(2,1)S(1)}, u32[]{:S(2)}, u32[]{:S(2)}) %collective-permute-start.32) | collective-permute-done | bytes 1048608 | tf_op jit(solution)/shard_map/ppermute | solution.py:43
  198.0 6.7 collective-permute-done.33.back_last
  216.7 14.7 %collective-permute-done.35.refs_2_ = bf16[256,2048]{1,0:T(8,128)(2,1)S(1)} collective-permute-done((bf16[256,2048]{1,0:T(8,128)(2,1)S(1)}, bf16[256,2048]{1,0:T(8,128)(2,1)S(1)}, u32[]{:S(2)}, u32[]{:S(2)}) %collective-permute-start.35) | collective-permute-done | bytes 1048608 | tf_op jit(solution)/shard_map/ppermute | solution.py:43
  236.7 8.0 %collective-permute-done.40.refs_4_ = bf16[128,2048]{1,0:T(8,128)(2,1)S(1)} collective-permute-done((bf16[128,2048]{1,0:T(8,128)(2,1)S(1)}, bf16[128,2048]{1,0:T(8,128)(2,1)S(1)}, u32[]{:S(2)}, u32[]{:S(2)}) %collective-permute-start.40) | collective-permute-done | bytes 524320 | tf_op jit(solution)/shard_map/ppermute | solution.py:43
  253.4 7.2 %collective-permute-done.52.refs_2_ = bf16[128,1152]{1,0:T(8,128)(2,1)S(1)} collective-permute-done((bf16[128,1152]{1,0:T(8,128)(2,1)S(1)}, bf16[128,1152]{1,0:T(8,128)(2,1)S(1)}, u32[]{:S(2)}, u32[]{:S(2)}) %collective-permute-start.52) | collective-permute-done | bytes 294944 | tf_op jit(solution)/shard_map/ppermute | solution.py:47
  275.0 6.1 pack.4.cot_ref.refs_1_
  288.2 24.3 %mlp_chunk.1 = (bf16[2048,640]{1,0:T(8,128)(2,1)S(1)}, bf16[2048,1280]{1,0:T(8,128)(2,1)}) custom-call(bf16[2048,2048]{1,0:T(8,128)(2,1)} %pack.3.normed_ref.refs_0_, bf16[2048,2048]{1,0:T(8,128)(2,1)} %pack.4.cot_ref.refs_1_, bf16[2048,1920]{1,0:T(8,128)(2,1)} %all-gather.6.cloned.1.call-done.weight_ref.refs_1_.refs_2_), custom_call_target="tpu_custom_call" | custom-call | flops 16106127360 | bytes 24641536 | tf_op jit(solution)/shard_map/mlp_chunk/pallas_call | solution.py:595
  312.6 24.2 %weight_grads.4 = bf16[2048,1920]{1,0:T(8,128)(2,1)} custom-call(bf16[2048,2048]{1,0:T(8,128)(2,1)} %pack.3.normed_ref.refs_0_, bf16[2048,2048]{1,0:T(8,128)(2,1)} %pack.4.cot_ref.refs_1_, bf16[2048,1280]{1,0:T(8,128)(2,1)} %get-tuple-element.143.refs_2_.refs_0_, bf16[2048,640]{1,0:T(8,128)(2,1)S(1)} %get-tuple-element.151.refs_3_.refs_0_), custom_call_target="tpu_custom_call" | custom-call | flops 16106127360 | bytes 32505856 | tf_op jit(solution)/shard_map/weight_grads/pallas_call | solution.py:677
  339.3 10.1 %chunk_sum.19.base_ref = f32[1024,2048]{1,0:T(8,128)} custom-call(bf16[2048,1280]{1,0:T(8,128)(2,1)S(1)} %copy-done.6, bf16[2048,1920]{1,0:T(8,128)(2,1)} %all-gather.6.cloned.1.call-done.weight_ref.refs_1_.refs_2_), custom_call_target="tpu_custom_call" | custom-call | flops 5368709120 | bytes 16252928 | tf_op jit(solution)/shard_map/chunk_sum/pallas_call | solution.py:641
  349.4 10.0 %chunk_sum.18.base_ref = f32[1024,2048]{1,0:T(8,128)} custom-call(bf16[2048,1280]{1,0:T(8,128)(2,1)S(1)} %copy-done.6, bf16[2048,1920]{1,0:T(8,128)(2,1)} %all-gather.6.cloned.1.call-done.weight_ref.refs_1_.refs_2_), custom_call_target="tpu_custom_call" | custom-call | flops 5368709120 | bytes 16252928 | tf_op jit(solution)/shard_map/chunk_sum/pallas_call | solution.py:641
  359.4 14.6 %mlp_tail.2 = (bf16[2048,384]{1,0:T(8,128)(2,1)S(1)}, bf16[2048,768]{1,0:T(8,128)(2,1)}, bf16[1024,1024]{1,0:T(8,128)(2,1)S(1)}, bf16[1024,1024]{1,0:T(8,128)(2,1)S(1)}) custom-call(bf16[2048,2048]{1,0:T(8,128)(2,1)} %pack.3.normed_ref.refs_0_, bf16[2048,2048]{1,0:T(8,128)(2,1)} %pack.4.cot_ref.refs_1_, ...), custom_call_target="tpu_custom_call" | custom-call | flops 8053063680 | bytes 25690112 | tf_op jit(solution)/shard_map/mlp_tail/pallas_call | solution.py:558
  376.5 15.3 %mlp_tail.3 = (bf16[2048,384]{1,0:T(8,128)(2,1)S(1)}, bf16[2048,768]{1,0:T(8,128)(2,1)S(1)}, f32[1024,1024]{1,0:T(8,128)}, f32[1024,1024]{1,0:T(8,128)}) custom-call(bf16[2048,2048]{1,0:T(8,128)(2,1)} %pack.3.normed_ref.refs_0_, bf16[2048,2048]{1,0:T(8,128)(2,1)} %pack.4.cot_ref.refs_1_, ...), custom_call_target="tpu_custom_call", output_to_operand_aliasing={{0}: (4, {}), {1}: (5, {})} | custom-call | flops 8053063680 | bytes 25690112 | tf_op jit(solution)/shard_map/mlp_tail/pallas_call | solution.py:558
  412.5 6.8 %chunk_sum.22 = f32[1024,1024]{1,0:T(8,128)} custom-call(bf16[2048,640]{1,0:T(8,128)(2,1)S(1)} %copy-done.3, bf16[2048,384]{1,0:T(8,128)(2,1)S(1)} %get-tuple-element.153.refs_1_.refs_3_, bf16[2048,1920]{1,0:T(8,128)(2,1)} %all-gather.6.cloned.1.call-done.weight_ref.refs_1_.refs_2_, bf16[2048,1152]{1,0:T(8,128)(2,1)} %all-gather.8.cloned.1.call-done.weight_ref.refs_3_), custom_call_target="tpu_custom_call" | custom-call | flops 2147483648 | bytes 8388608 | tf_op jit(solution)/shard_map/chunk_sum/pallas_call | solution.py:641
  419.3 6.5 chunk_sum.20
  431.8 12.4 %collective-permute-done.60.back_last = bf16[256,1024]{1,0:T(8,128)(2,1)S(1)} collective-permute-done((bf16[256,1024]{1,0:T(8,128)(2,1)S(1)}, bf16[256,1024]{1,0:T(8,128)(2,1)S(1)}, u32[]{:S(2)}, u32[]{:S(2)}) %collective-permute-start.60) | collective-permute-done | bytes 524320 | tf_op jit(solution)/shard_map/ppermute | solution.py:43
  451.1 15.6 %weight_grads.5 = bf16[2048,1152]{1,0:T(8,128)(2,1)} custom-call(bf16[2048,2048]{1,0:T(8,128)(2,1)} %pack.3.normed_ref.refs_0_, bf16[2048,2048]{1,0:T(8,128)(2,1)} %pack.4.cot_ref.refs_1_, bf16[2048,768]{1,0:T(8,128)(2,1)S(1)} %copy-done.26, bf16[2048,384]{1,0:T(8,128)(2,1)S(1)} %get-tuple-element.153.refs_1_.refs_3_), custom_call_target="tpu_custom_call" | custom-call | flops 9663676416 | bytes 26214400 | tf_op jit(solution)/shard_map/weight_grads/pallas_call | solution.py:677
  466.8 6.5 collective-permute-done.63.refs_2_
  481.1 7.0 %collective-permute-done.64.refs_4_ = bf16[128,2048]{1,0:T(8,128)(2,1)S(1)} collective-permute-done((bf16[128,2048]{1,0:T(8,128)(2,1)S(1)}, bf16[128,2048]{1,0:T(8,128)(2,1)S(1)}, u32[]{:S(2)}, u32[]{:S(2)}) %collective-permute-start.64) | collective-permute-done | bytes 524320 | tf_op jit(solution)/shard_map/ppermute | solution.py:43
  497.1 6.3 pack.5.refs_1_
  503.4 6.1 convolution_convert_fusion.mixed_ref
  509.5 11.2 %attention_backward.1.refs_1_.refs_2_.refs_0_ = bf16[2048,768]{1,0:T(8,128)(2,1)} custom-call(s32[16]{0:T(128)S(1)} %select_reduce_fusion.refs_14_.order_ref, bf16[2048,256]{1,0:T(8,128)(2,1)S(1)} %copy-done.75, bf16[2048,256]{1,0:T(8,128)(2,1)S(1)} %copy-done.77, bf16[2048,256]{1,0:T(8,128)(2,1)S(1)} %copy-done.79, f32[2048,1]{1,0:T(8,128)S(1)} %copy-done.81, ...), custom_call_target="tpu_custom_call" | custom-call | flops 5368709120 | bytes 10485760 | tf_op jit(solution)/shard_map/attention_backward/pallas_call | solution.py:855
  535.1 8.9 %weight_grads.6.grads_ref = bf16[2048,512]{1,0:T(8,128)(2,1)S(1)} custom-call(bf16[2048,2048]{1,0:T(8,128)(2,1)} %pack_normed.1.normed_ref.refs_0_, bf16[2048,768]{1,0:T(8,128)(2,1)S(1)} %copy-done), custom_call_target="tpu_custom_call" | custom-call | flops 4294967296 | bytes 12582912 | tf_op jit(solution)/shard_map/weight_grads/pallas_call | solution.py:677
  545.5 11.1 %weight_grads.7.both_ref = bf16[2048,512]{1,0:T(8,128)(2,1)S(1)} custom-call(bf16[2048,2048]{1,0:T(8,128)(2,1)} %pack_normed.1.normed_ref.refs_0_, bf16[2048,2048]{1,0:T(8,128)(2,1)} %pack.5.refs_1_, bf16[2048,768]{1,0:T(8,128)(2,1)} %attention_backward.1.refs_1_.refs_2_.refs_0_, bf16[2048,256]{1,0:T(8,128)(2,1)S(1)} %copy-done.5), custom_call_target="tpu_custom_call" | custom-call | flops 4294967296 | bytes 20971520 | tf_op jit(solution)/shard_map/weight_grads/pallas_call | solution.py:677
  595.5 5.9 collective-permute-done.81.refs_6_
  605.0 20.3 %collective-permute-done.83 = bf16[512,1024]{1,0:T(8,128)(2,1)S(1)} collective-permute-done((bf16[512,1024]{1,0:T(8,128)(2,1)S(1)}, bf16[512,1024]{1,0:T(8,128)(2,1)S(1)}, u32[]{:S(2)}, u32[]{:S(2)}) %collective-permute-start.83) | collective-permute-done | bytes 1048608 | tf_op jit(solution)/shard_map/ppermute | solution.py:43
  (525 shorter events, 307.8 us)
Async XLA Ops:
  7.2 103.4 %all-gather.4.cloned.1.call-start = ((), (), s32[]{:S(2)}) async-start(), calls=%async_computation.3 | async-start | bytes 5242880 | tf_op jit(solution)/shard_map/all_gather | solution.py:909
  28.6 259.6 %all-gather.6.cloned.1.call-start = ((), (), s32[]{:S(2)}) async-start(), calls=%async_computation.4 | async-start | bytes 9830400 | tf_op jit(solution)/shard_map/all_gather | solution.py:909
  30.3 31.7 %collective-permute-start.14 = (bf16[2,16,128]{2,1,0:T(8,128)(2,1)S(1)}, bf16[2,16,128]{2,1,0:T(8,128)(2,1)S(1)}, u32[]{:S(2)}, u32[]{:S(2)}) collective-permute-start(bf16[2,16,128]{2,1,0:T(8,128)(2,1)S(1)} %broadcast_select_fusion), channel_id=1, source_target_pairs={{0,6},{2,4},{4,2},{6,0},{8,14},{10,12},{12,10},{14,8},{16,22},{18,... | collective-permute-start | bytes 24584 | tf_op jit(solution)/shard_map/ppermute | solution.py:61
  35.3 23.6 %collective-permute-start.4 = (bf16[256,2048]{1,0:T(8,128)(2,1)S(1)}, bf16[256,2048]{1,0:T(8,128)(2,1)}, u32[]{:S(2)}, u32[]{:S(2)}) collective-permute-start(bf16[256,2048]{1,0:T(8,128)(2,1)S(1)} %copy-done.7), channel_id=1, source_target_pairs={{0,4},{4,0},{1,5},{5,1},{2,6},{6,2},{3,7},{7,3},{8,12},{12,8},{9,1... | collective-permute-start | bytes 3145736 | tf_op jit(solution)/shard_map/ppermute | solution.py:43
  36.2 23.1 %collective-permute-start.3 = (bf16[256,2048]{1,0:T(8,128)(2,1)S(1)}, bf16[256,2048]{1,0:T(8,128)(2,1)}, u32[]{:S(2)}, u32[]{:S(2)}) collective-permute-start(bf16[256,2048]{1,0:T(8,128)(2,1)S(1)} %copy-done.7), channel_id=1, source_target_pairs={{0,2},{2,0},{1,3},{3,1},{4,6},{6,4},{5,7},{7,5},{8,10},{10,8},{9,1... | collective-permute-start | bytes 3145736 | tf_op jit(solution)/shard_map/ppermute | solution.py:43
  43.8 25.8 %collective-permute-start.7 = (bf16[256,2048]{1,0:T(8,128)(2,1)S(1)}, bf16[256,2048]{1,0:T(8,128)(2,1)}, u32[]{:S(2)}, u32[]{:S(2)}) collective-permute-start(bf16[256,2048]{1,0:T(8,128)(2,1)S(1)} %copy-done.7), channel_id=1, source_target_pairs={{0,1},{1,0},{2,3},{3,2},{4,5},{5,4},{6,7},{7,6},{8,9},{9,8},{10,11... | collective-permute-start | bytes 3145736 | tf_op jit(solution)/shard_map/ppermute | solution.py:43
  83.4 22.6 %collective-permute-start.20 = (bf16[128,1920]{1,0:T(8,128)(2,1)S(1)}, bf16[128,1920]{1,0:T(8,128)(2,1)S(1)}, u32[]{:S(2)}, u32[]{:S(2)}) collective-permute-start(bf16[128,1920]{1,0:T(8,128)(2,1)S(1)} %get-tuple-element.119), channel_id=1, source_target_pairs={{0,6},{2,4},{4,2},{6,0},{1,7},{3,5},{5,3},{7,1},{8,14},{10,12},{12... | collective-permute-start | bytes 1474568 | tf_op jit(solution)/shard_map/ppermute | solution.py:47
  107.4 252.0 %all-gather.8.cloned.1.call-start = ((), (), s32[]{:S(2)}) async-start(), calls=%async_computation.5 | async-start | bytes 5898240 | tf_op jit(solution)/shard_map/all_gather | solution.py:909
  107.6 24.8 %collective-permute-start.22 = (bf16[256,2048]{1,0:T(8,128)(2,1)}, bf16[256,2048]{1,0:T(8,128)(2,1)}, u32[]{:S(2)}, u32[]{:S(2)}) collective-permute-start(bf16[256,2048]{1,0:T(8,128)(2,1)} %base_ref.1), channel_id=1, source_target_pairs={{0,4},{4,0},{1,5},{5,1},{2,6},{6,2},{3,7},{7,3},{8,12},{12,8},{9,1... | collective-permute-start | bytes 3145736 | tf_op jit(solution)/shard_map/ppermute | solution.py:43
  108.5 24.2 %collective-permute-start.21 = (bf16[256,2048]{1,0:T(8,128)(2,1)}, bf16[256,2048]{1,0:T(8,128)(2,1)}, u32[]{:S(2)}, u32[]{:S(2)}) collective-permute-start(bf16[256,2048]{1,0:T(8,128)(2,1)} %base_ref.1), channel_id=1, source_target_pairs={{0,2},{2,0},{1,3},{3,1},{4,6},{6,4},{5,7},{7,5},{8,10},{10,8},{9,1... | collective-permute-start | bytes 3145736 | tf_op jit(solution)/shard_map/ppermute | solution.py:43
  141.1 23.2 %collective-permute-start.31 = (bf16[1024,1024]{1,0:T(8,128)(2,1)}, bf16[1024,1024]{1,0:T(8,128)(2,1)}, u32[]{:S(2)}, u32[]{:S(2)}) collective-permute-start(bf16[1024,1024]{1,0:T(8,128)(2,1)} %chunk_sum.17), channel_id=1, source_target_pairs={{0,1},{1,0},{2,3},{3,2},{4,5},{5,4},{6,7},{7,6},{8,9},{9,8},{10,11... | collective-permute-start | bytes 6291464 | tf_op jit(solution)/shard_map/ppermute | solution.py:43
  143.1 24.4 %collective-permute-start.25 = (bf16[1024,1024]{1,0:T(8,128)(2,1)S(1)}, bf16[1024,1024]{1,0:T(8,128)(2,1)}, u32[]{:S(2)}, u32[]{:S(2)}) collective-permute-start(bf16[1024,1024]{1,0:T(8,128)(2,1)S(1)} %chunk_sum.15), channel_id=1, source_target_pairs={{0,1},{1,0},{2,3},{3,2},{4,5},{5,4},{6,7},{7,6},{8,9},{9,8},{10,11... | collective-permute-start | bytes 6291464 | tf_op jit(solution)/shard_map/ppermute | solution.py:43
  165.9 24.1 %collective-permute-start.32 = (bf16[2,256,1024]{2,1,0:T(8,128)(2,1)S(1)}, bf16[2,256,1024]{2,1,0:T(8,128)(2,1)S(1)}, u32[]{:S(2)}, u32[]{:S(2)}) collective-permute-start(bf16[2,256,1024]{2,1,0:T(8,128)(2,1)S(1)} %bitcast.79), channel_id=1, source_target_pairs={{0,4},{4,0},{1,5},{5,1},{2,6},{6,2},{3,7},{7,3},{8,12},{12,8},{9,1... | collective-permute-start | bytes 3145736 | tf_op jit(solution)/shard_map/ppermute | solution.py:43
  169.1 25.3 %collective-permute-start.26 = (bf16[512,1024]{1,0:T(8,128)(2,1)S(1)}, bf16[512,1024]{1,0:T(8,128)(2,1)S(1)}, u32[]{:S(2)}, u32[]{:S(2)}) collective-permute-start(bf16[512,1024]{1,0:T(8,128)(2,1)S(1)} %pad_maximum_fusion), channel_id=1, source_target_pairs={{0,2},{2,0},{1,3},{3,1},{4,6},{6,4},{5,7},{7,5},{8,10},{10,8},{9,1... | collective-permute-start | bytes 3145736 | tf_op jit(solution)/shard_map/ppermute | solution.py:43
  211.1 23.0 %collective-permute-start.34 = (bf16[256,2048]{1,0:T(8,128)(2,1)S(1)}, bf16[256,2048]{1,0:T(8,128)(2,1)S(1)}, u32[]{:S(2)}, u32[]{:S(2)}) collective-permute-start(bf16[256,2048]{1,0:T(8,128)(2,1)S(1)} %get-tuple-element.129.refs_0_), channel_id=1, source_target_pairs={{0,2},{2,0},{1,3},{3,1},{4,6},{6,4},{5,7},{7,5},{8,10},{10,8},{9,1... | collective-permute-start | bytes 3145736 | tf_op jit(solution)/shard_map/ppermute | solution.py:43
  261.7 267.2 %reduce-scatter.4.cloned.1.call-start = ((), (), s32[]{:S(2)}) async-start(), calls=%async_computation.6 | async-start | bytes 9830400 | tf_op jit(solution)/shard_map/reduce_scatter | solution.py:988
  336.8 247.4 %reduce-scatter.6.cloned.1.call-start = ((), (), s32[]{:S(2)}) async-start(), calls=%async_computation.7 | async-start | bytes 5898240 | tf_op jit(solution)/shard_map/reduce_scatter | solution.py:988
  374.5 23.8 %collective-permute-start.55 = (bf16[1024,1024]{1,0:T(8,128)(2,1)S(1)}, bf16[1024,1024]{1,0:T(8,128)(2,1)S(1)}, u32[]{:S(2)}, u32[]{:S(2)}) collective-permute-start(bf16[1024,1024]{1,0:T(8,128)(2,1)S(1)} %get-tuple-element.150), channel_id=1, source_target_pairs={{0,1},{1,0},{2,3},{3,2},{4,5},{5,4},{6,7},{7,6},{8,9},{9,8},{10,11... | collective-permute-start | bytes 6291464 | tf_op jit(solution)/shard_map/ppermute | solution.py:43
  396.6 29.2 %collective-permute-start.57 = (bf16[512,1024]{1,0:T(8,128)(2,1)}, bf16[512,1024]{1,0:T(8,128)(2,1)}, u32[]{:S(2)}, u32[]{:S(2)}) collective-permute-start(bf16[512,1024]{1,0:T(8,128)(2,1)} %pad_maximum_fusion.1), channel_id=1, source_target_pairs={{0,2},{2,0},{1,3},{3,1},{4,6},{6,4},{5,7},{7,5},{8,10},{10,8},{9,1... | collective-permute-start | bytes 3145736 | tf_op jit(solution)/shard_map/ppermute | solution.py:43
  399.9 28.5 %collective-permute-start.59 = (bf16[2,256,1024]{2,1,0:T(8,128)(2,1)}, bf16[2,256,1024]{2,1,0:T(8,128)(2,1)S(1)}, u32[]{:S(2)}, u32[]{:S(2)}) collective-permute-start(bf16[2,256,1024]{2,1,0:T(8,128)(2,1)} %bitcast.9), channel_id=1, source_target_pairs={{0,4},{4,0},{1,5},{5,1},{2,6},{6,2},{3,7},{7,3},{8,12},{12,8},{9,1... | collective-permute-start | bytes 3145736 | tf_op jit(solution)/shard_map/ppermute | solution.py:43
  449.5 23.8 %collective-permute-start.63 = (bf16[256,2048]{1,0:T(8,128)(2,1)S(1)}, bf16[256,2048]{1,0:T(8,128)(2,1)S(1)}, u32[]{:S(2)}, u32[]{:S(2)}) collective-permute-start(bf16[256,2048]{1,0:T(8,128)(2,1)S(1)} %get-tuple-element.157.refs_0_), channel_id=1, source_target_pairs={{0,4},{4,0},{1,5},{5,1},{2,6},{6,2},{3,7},{7,3},{8,12},{12,8},{9,1... | collective-permute-start | bytes 3145736 | tf_op jit(solution)/shard_map/ppermute | solution.py:43
  449.8 23.6 %collective-permute-start.61 = (bf16[256,2048]{1,0:T(8,128)(2,1)S(1)}, bf16[256,2048]{1,0:T(8,128)(2,1)S(1)}, u32[]{:S(2)}, u32[]{:S(2)}) collective-permute-start(bf16[256,2048]{1,0:T(8,128)(2,1)S(1)} %get-tuple-element.157.refs_0_), channel_id=1, source_target_pairs={{0,2},{2,0},{1,3},{3,1},{4,6},{6,4},{5,7},{7,5},{8,10},{10,8},{9,1... | collective-permute-start | bytes 3145736 | tf_op jit(solution)/shard_map/ppermute | solution.py:43
  473.5 172.0 %reduce-scatter.8.cloned.1.call-start = ((), (), s32[]{:S(2)}) async-start(), calls=%async_computation.8 | async-start | bytes 3932160 | tf_op jit(solution)/shard_map/reduce_scatter | solution.py:988
  493.4 31.0 %collective-permute-start.65 = (bf16[512,1024]{1,0:T(8,128)(2,1)}, bf16[512,1024]{1,0:T(8,128)(2,1)}, u32[]{:S(2)}, u32[]{:S(2)}) collective-permute-start(bf16[512,1024]{1,0:T(8,128)(2,1)} %pad_maximum_fusion.2), channel_id=1, source_target_pairs={{0,2},{2,0},{1,3},{3,1},{4,6},{6,4},{5,7},{7,5},{8,10},{10,8},{9,1... | collective-permute-start | bytes 3145736 | tf_op jit(solution)/shard_map/ppermute | solution.py:43
  494.5 26.2 %collective-permute-start.68 = (bf16[2,256,1024]{2,1,0:T(8,128)(2,1)}, bf16[2,256,1024]{2,1,0:T(8,128)(2,1)}, u32[]{:S(2)}, u32[]{:S(2)}) collective-permute-start(bf16[2,256,1024]{2,1,0:T(8,128)(2,1)} %bitcast.15), channel_id=1, source_target_pairs={{0,4},{4,0},{1,5},{5,1},{2,6},{6,2},{3,7},{7,3},{8,12},{12,8},{9,1... | collective-permute-start | bytes 3145736 | tf_op jit(solution)/shard_map/ppermute | solution.py:43
  527.7 28.8 %collective-permute-start.66 = (bf16[256,1024]{1,0:T(8,128)(2,1)}, bf16[256,1024]{1,0:T(8,128)(2,1)}, u32[]{:S(2)}, u32[]{:S(2)}) collective-permute-start(bf16[256,1024]{1,0:T(8,128)(2,1)} %get-tuple-element.211), channel_id=1, source_target_pairs={{0,4},{4,0},{1,5},{5,1},{2,6},{6,2},{3,7},{7,3},{8,12},{12,8},{9,1... | collective-permute-start | bytes 1572872 | tf_op jit(solution)/shard_map/ppermute | solution.py:43
  531.3 25.2 %collective-permute-start.75 = (bf16[128,1920]{1,0:T(8,128)(2,1)S(1)}, bf16[128,1920]{1,0:T(8,128)(2,1)S(1)}, u32[]{:S(2)}, u32[]{:S(2)}) collective-permute-start(bf16[128,1920]{1,0:T(8,128)(2,1)S(1)} %get-tuple-element.169), channel_id=1, source_target_pairs={{0,2},{2,0},{4,6},{6,4},{1,3},{3,1},{5,7},{7,5},{8,10},{10,8},{12,... | collective-permute-start | bytes 1474568 | tf_op jit(solution)/shard_map/ppermute | solution.py:47
  532.6 29.9 %collective-permute-start.76 = (bf16[128,1920]{1,0:T(8,128)(2,1)S(1)}, bf16[128,1920]{1,0:T(8,128)(2,1)S(1)}, u32[]{:S(2)}, u32[]{:S(2)}) collective-permute-start(bf16[128,1920]{1,0:T(8,128)(2,1)S(1)} %get-tuple-element.170), channel_id=1, source_target_pairs={{0,4},{2,6},{4,0},{6,2},{1,5},{3,7},{5,1},{7,3},{8,12},{10,14},{12... | collective-permute-start | bytes 1474568 | tf_op jit(solution)/shard_map/ppermute | solution.py:47
  534.1 29.2 %collective-permute-start.77 = (bf16[128,1920]{1,0:T(8,128)(2,1)S(1)}, bf16[128,1920]{1,0:T(8,128)(2,1)S(1)}, u32[]{:S(2)}, u32[]{:S(2)}) collective-permute-start(bf16[128,1920]{1,0:T(8,128)(2,1)S(1)} %get-tuple-element.171), channel_id=1, source_target_pairs={{0,6},{2,4},{4,2},{6,0},{1,7},{3,5},{5,3},{7,1},{8,14},{10,12},{12... | collective-permute-start | bytes 1474568 | tf_op jit(solution)/shard_map/ppermute | solution.py:47
  544.1 37.4 %collective-permute-start.79 = (bf16[1024,512]{1,0:T(8,128)(2,1)S(1)}, bf16[1024,512]{1,0:T(8,128)(2,1)S(1)}, u32[]{:S(2)}, u32[]{:S(2)}) collective-permute-start(bf16[1024,512]{1,0:T(8,128)(2,1)S(1)} %get-tuple-element.175), channel_id=1, source_target_pairs={{0,2},{2,0},{1,3},{3,1},{4,6},{6,4},{5,7},{7,5},{8,10},{10,8},{9,1... | collective-permute-start | bytes 3145736 | tf_op jit(solution)/shard_map/ppermute | solution.py:43
  601.3 23.9 %collective-permute-start.83 = (bf16[512,1024]{1,0:T(8,128)(2,1)S(1)}, bf16[512,1024]{1,0:T(8,128)(2,1)S(1)}, u32[]{:S(2)}, u32[]{:S(2)}) collective-permute-start(bf16[512,1024]{1,0:T(8,128)(2,1)S(1)} %pad_maximum_fusion.3), channel_id=1, source_target_pairs={{0,2},{2,0},{1,3},{3,1},{4,6},{6,4},{5,7},{7,5},{8,10},{10,8},{9,1... | collective-permute-start | bytes 3145736 | tf_op jit(solution)/shard_map/ppermute | solution.py:43
  604.5 25.1 %collective-permute-start.86 = (bf16[2,256,1024]{2,1,0:T(8,128)(2,1)S(1)}, bf16[2,256,1024]{2,1,0:T(8,128)(2,1)S(1)}, u32[]{:S(2)}, u32[]{:S(2)}) collective-permute-start(bf16[2,256,1024]{2,1,0:T(8,128)(2,1)S(1)} %bitcast.80), channel_id=1, source_target_pairs={{0,4},{4,0},{1,5},{5,1},{2,6},{6,2},{3,7},{7,3},{8,12},{12,8},{9,1... | collective-permute-start | bytes 3145736 | tf_op jit(solution)/shard_map/ppermute | solution.py:43
  (179 other events, 1663.4 us)
Sparse Core Ops, SparseCore 0:
  28.7 81.7 all-gather.3
  112.7 139.4 all-gather.5
  261.8 91.0 all-gather.7
  355.1 134.6 reduce-scatter.3
  492.0 85.7 reduce-scatter.5
  583.7 60.2 reduce-scatter.7

commit v2 on v1

--- a/solution.py
+++ b/solution.py
@@ -951,7 +951,7 @@
     )
     late_cot = after(cotangent, *pieces_0[1:])
     cot_near = plane_neighbours(late_cot)
-    cot_far = plane_far(cot_near)
+    pieces_1 = mlp_exchange(chunks[1:], cot_near)
     query, keys, vals = project(
         place, normed_all, attn_weights, cos, sin
     )
@@ -972,14 +972,14 @@
             for h in range(2)
         ]
 
-    attn_sums = chip_sums(*projected(mixed, 3, (), cot_far))
+    attn_sums = chip_sums(*projected(mixed, 3, pieces_1[1:]))
     arrived = reduce_first(first_operands(attn_sums))
     attn_operands = reduce_operands(attn_sums, arrived)
     attn_last = last_swaps(attn_operands, *head_rounds[0])
     hidden, own_normed = add_and_norm(attn_operands, attn_last, tokens, gains[1:])
     neighbours = plane_neighbours(own_normed)
     normed_far = plane_far(neighbours, *head_rounds[-1])
-    pieces_1 = mlp_exchange(chunks[1:], normed_far)
+    cot_far = plane_far(cot_near, *normed_far)
     mlp_weights = [collect(blocks_0), collect(*place_rows(member_at, pieces_1))]
     normed_mlp = pack(with_partner([own_normed, *neighbours, *normed_far]))
     cot_all = pack(with_partner([late_cot, *cot_near, *cot_far]))
@@ -1053,7 +1053,7 @@
         "join",
         [jax.ShapeDtypeStruct((features, 3 * HS), bf16)],
         member_at,
-        after(keep, *qkv_parts[0], *qkv_parts[1]),
+        after(keep, qkv_parts[0][1], qkv_parts[1][1]),
         got,
         both_grads,
     )

time: 679 us -> 693 us (1.021)
  waiting for transfers between devices: 196 us -> 206 us
    ppermute x62, waiting for transfers between devices: 150 us -> 161 us  [swap(): return lax.ppermute(block, axis, [(0, 1), (1, 0)])]
    unnamed x239 -> x247, local copies, waits for them, and re-layouts: 44.2 us -> 49.9 us
  transfers between devices with their start and end apart: 100 -> 100, of which waited for: 43 -> 31; matrix products, arithmetic and copies ran while one was open for 10% -> 11% of each run, Pallas kernels for 39% -> 38%
where the time goes in v2:
time: 693 us; the launch traced here: 686 us
  Pallas kernels  263 us (38%)
  waiting for transfers between devices  206 us (30%)
  starting transfers between devices  87.2 us (13%)
  local copies, waits for them, and re-layouts  55.4 us (8%)
  other arithmetic  52 us (8%)
  between operations  16 us (2%)
    ppermute x62, waiting for transfers between devices, swap(): return lax.ppermute(block, axis, [(0, 1), (1, 0)])  161 us
    pallas_call x14, Pallas kernels, chunk_sum(): pl.pallas_call(functools.partial(sum_kernel, count), grid=(steps,), in_sp...  68.5 us
    pallas_call x4, Pallas kernels, weight_grads(): pl.pallas_call(functools.partial(grads_kernel, count), grid=(features //...  59.9 us
    unnamed x247, local copies, waits for them, and re-layouts  49.9 us
    ppermute x18, waiting for transfers between devices, swap_plane(): return lax.ppermute(block, PLANE, [(i, i ^ distance) for i in range(4)])  45.6 us
    ppermute x62, starting transfers between devices, swap(): return lax.ppermute(block, axis, [(0, 1), (1, 0)])  39.5 us
    pallas_call x2, Pallas kernels, mlp_tail(): pl.pallas_call(functools.partial(tail_kernel, width), grid=(steps,), in_s...  29.1 us
    pallas_call x1, Pallas kernels, mlp_chunk(): pl.pallas_call(functools.partial(mlp_kernel, width), grid=(tokens // tile...  24.3 us
  transfers between devices with their start and end apart: 100, of which 31 were waited for; matrix products, arithmetic and copies ran while one was open for 11% of the time, Pallas kernels for 38%

profile of v2, /device:TPU:0, one launch (start us, length us, event | category | flops | bytes accessed | tf_op | source)
XLA Modules:
  0.0 686.3 jit_solution(3318288574425828897)
XLA Ops:
  21.3 6.2 collective-permute-done.1.refs_2_
  45.9 13.1 %collective-permute-done.4.refs_2_ = bf16[256,2048]{1,0:T(8,128)(2,1)} collective-permute-done((bf16[256,2048]{1,0:T(8,128)(2,1)S(1)}, bf16[256,2048]{1,0:T(8,128)(2,1)}, u32[]{:S(2)}, u32[]{:S(2)}) %collective-permute-start.4) | collective-permute-done | bytes 1048608 | tf_op jit(solution)/shard_map/ppermute | solution.py:43
  85.1 9.3 %pack_normed.1.normed_ref.refs_0_ = bf16[2048,2048]{1,0:T(8,128)(2,1)} custom-call(bf16[256,2048]{1,0:T(8,128)(2,1)S(1)} %copy-done.10, bf16[256,2048]{1,0:T(8,128)(2,1)} %collective-permute-done.3.refs_1_, bf16[256,2048]{1,0:T(8,128)(2,1)} %collective-permute-done.4.refs_2_, bf16[128,2048]{1,0:T(8,128)(2,1)S(1)} %collective-permute-done.5.refs_3_, ...), custom_call_target="tpu_custom_call" | custom-call | flops 33554432 | bytes 16777216 | tf_op jit(solution)/shard_map/pack_normed/pallas_call | solution.py:114
  95.4 9.0 %collective-permute-done.19.refs_2_ = bf16[128,1920]{1,0:T(8,128)(2,1)S(1)} collective-permute-done((bf16[128,1920]{1,0:T(8,128)(2,1)S(1)}, bf16[128,1920]{1,0:T(8,128)(2,1)S(1)}, u32[]{:S(2)}, u32[]{:S(2)}) %collective-permute-start.19) | collective-permute-done | bytes 491552 | tf_op jit(solution)/shard_map/ppermute | solution.py:47
  110.0 22.3 %collective-permute-done.22.refs_2_ = bf16[256,2048]{1,0:T(8,128)(2,1)S(1)} collective-permute-done((bf16[256,2048]{1,0:T(8,128)(2,1)}, bf16[256,2048]{1,0:T(8,128)(2,1)S(1)}, u32[]{:S(2)}, u32[]{:S(2)}) %collective-permute-start.22) | collective-permute-done | bytes 1048608 | tf_op jit(solution)/shard_map/ppermute | solution.py:43
  141.5 11.6 %project.1 = (bf16[2048,256]{1,0:T(8,128)(2,1)S(1)}, bf16[2048,256]{1,0:T(8,128)(2,1)S(1)}, bf16[2048,256]{1,0:T(8,128)(2,1)S(1)}) custom-call(s32[16]{0:T(128)S(1)} %compare_select_fusion.1.refs_13_.place_ref, bf16[2048,2048]{1,0:T(8,128)(2,1)} %pack_normed.1.normed_ref.refs_0_, bf16[2048,1024]{1,0:T(8,128)(2,1)} %all-gather.4.cloned.1.call-done.weight_ref.refs_1_, ...), custom_call_target="tpu_custom_call" | custom-call | flops 6442450944 | bytes 16777216 | tf_op jit(solution)/shard_map/project/pallas_call | solution.py:714
  182.0 16.1 %collective-permute-done.33 = bf16[2,256,1024]{2,1,0:T(8,128)(2,1)} collective-permute-done((bf16[2,256,1024]{2,1,0:T(8,128)(2,1)S(1)}, bf16[2,256,1024]{2,1,0:T(8,128)(2,1)}, u32[]{:S(2)}, u32[]{:S(2)}) %collective-permute-start.33) | collective-permute-done | bytes 1048608 | tf_op jit(solution)/shard_map/ppermute | solution.py:43
  207.0 8.2 %collective-permute-done.34.back_last = bf16[256,1024]{1,0:T(8,128)(2,1)S(1)} collective-permute-done((bf16[256,1024]{1,0:T(8,128)(2,1)S(1)}, bf16[256,1024]{1,0:T(8,128)(2,1)S(1)}, u32[]{:S(2)}, u32[]{:S(2)}) %collective-permute-start.34) | collective-permute-done | bytes 524320 | tf_op jit(solution)/shard_map/ppermute | solution.py:43
  227.8 16.0 %collective-permute-done.36.refs_2_ = bf16[256,2048]{1,0:T(8,128)(2,1)S(1)} collective-permute-done((bf16[256,2048]{1,0:T(8,128)(2,1)S(1)}, bf16[256,2048]{1,0:T(8,128)(2,1)S(1)}, u32[]{:S(2)}, u32[]{:S(2)}) %collective-permute-start.36) | collective-permute-done | bytes 1048608 | tf_op jit(solution)/shard_map/ppermute | solution.py:43
  248.0 10.3 %collective-permute-done.41.refs_4_ = bf16[128,2048]{1,0:T(8,128)(2,1)S(1)} collective-permute-done((bf16[128,2048]{1,0:T(8,128)(2,1)S(1)}, bf16[128,2048]{1,0:T(8,128)(2,1)S(1)}, u32[]{:S(2)}, u32[]{:S(2)}) %collective-permute-start.41) | collective-permute-done | bytes 524320 | tf_op jit(solution)/shard_map/ppermute | solution.py:43
  262.4 10.9 %collective-permute-done.47.refs_3_ = bf16[128,2048]{1,0:T(8,128)(2,1)S(1)} collective-permute-done((bf16[128,2048]{1,0:T(8,128)(2,1)S(1)}, bf16[128,2048]{1,0:T(8,128)(2,1)S(1)}, u32[]{:S(2)}, u32[]{:S(2)}) %collective-permute-start.47) | collective-permute-done | bytes 524320 | tf_op jit(solution)/shard_map/ppermute | solution.py:43
  283.7 5.6 pack.4.cot_ref.refs_1_
  289.4 24.3 %mlp_chunk.1 = (bf16[2048,640]{1,0:T(8,128)(2,1)S(1)}, bf16[2048,1280]{1,0:T(8,128)(2,1)}) custom-call(bf16[2048,2048]{1,0:T(8,128)(2,1)} %pack.3.normed_ref.refs_0_, bf16[2048,2048]{1,0:T(8,128)(2,1)} %pack.4.cot_ref.refs_1_, bf16[2048,1920]{1,0:T(8,128)(2,1)} %all-gather.6.cloned.1.call-done.weight_ref.refs_1_.refs_2_), custom_call_target="tpu_custom_call" | custom-call | flops 16106127360 | bytes 24641536 | tf_op jit(solution)/shard_map/mlp_chunk/pallas_call | solution.py:595
  313.7 24.2 %weight_grads.4 = bf16[2048,1920]{1,0:T(8,128)(2,1)} custom-call(bf16[2048,2048]{1,0:T(8,128)(2,1)} %pack.3.normed_ref.refs_0_, bf16[2048,2048]{1,0:T(8,128)(2,1)} %pack.4.cot_ref.refs_1_, bf16[2048,1280]{1,0:T(8,128)(2,1)} %get-tuple-element.147.refs_2_.refs_0_, bf16[2048,640]{1,0:T(8,128)(2,1)S(1)} %get-tuple-element.155.refs_3_.refs_0_), custom_call_target="tpu_custom_call" | custom-call | flops 16106127360 | bytes 32505856 | tf_op jit(solution)/shard_map/weight_grads/pallas_call | solution.py:677
  340.7 10.0 %chunk_sum.19.base_ref = f32[1024,2048]{1,0:T(8,128)} custom-call(bf16[2048,1280]{1,0:T(8,128)(2,1)S(1)} %copy-done.6, bf16[2048,1920]{1,0:T(8,128)(2,1)} %all-gather.6.cloned.1.call-done.weight_ref.refs_1_.refs_2_), custom_call_target="tpu_custom_call" | custom-call | flops 5368709120 | bytes 16252928 | tf_op jit(solution)/shard_map/chunk_sum/pallas_call | solution.py:641
  350.7 10.1 %chunk_sum.18.base_ref = f32[1024,2048]{1,0:T(8,128)} custom-call(bf16[2048,1280]{1,0:T(8,128)(2,1)S(1)} %copy-done.6, bf16[2048,1920]{1,0:T(8,128)(2,1)} %all-gather.6.cloned.1.call-done.weight_ref.refs_1_.refs_2_), custom_call_target="tpu_custom_call" | custom-call | flops 5368709120 | bytes 16252928 | tf_op jit(solution)/shard_map/chunk_sum/pallas_call | solution.py:641
  360.8 13.9 %mlp_tail.2 = (bf16[2048,384]{1,0:T(8,128)(2,1)S(1)}, bf16[2048,768]{1,0:T(8,128)(2,1)}, bf16[1024,1024]{1,0:T(8,128)(2,1)S(1)}, bf16[1024,1024]{1,0:T(8,128)(2,1)S(1)}) custom-call(bf16[2048,2048]{1,0:T(8,128)(2,1)} %pack.3.normed_ref.refs_0_, bf16[2048,2048]{1,0:T(8,128)(2,1)} %pack.4.cot_ref.refs_1_, ...), custom_call_target="tpu_custom_call" | custom-call | flops 8053063680 | bytes 25690112 | tf_op jit(solution)/shard_map/mlp_tail/pallas_call | solution.py:558
  377.2 15.2 %mlp_tail.3 = (bf16[2048,384]{1,0:T(8,128)(2,1)S(1)}, bf16[2048,768]{1,0:T(8,128)(2,1)S(1)}, f32[1024,1024]{1,0:T(8,128)}, f32[1024,1024]{1,0:T(8,128)}) custom-call(bf16[2048,2048]{1,0:T(8,128)(2,1)} %pack.3.normed_ref.refs_0_, bf16[2048,2048]{1,0:T(8,128)(2,1)} %pack.4.cot_ref.refs_1_, ...), custom_call_target="tpu_custom_call", output_to_operand_aliasing={{0}: (4, {}), {1}: (5, {})} | custom-call | flops 8053063680 | bytes 25690112 | tf_op jit(solution)/shard_map/mlp_tail/pallas_call | solution.py:558
  412.6 6.8 chunk_sum.22
  419.4 6.6 chunk_sum.20
  432.4 11.8 %collective-permute-done.60.back_last = bf16[256,1024]{1,0:T(8,128)(2,1)S(1)} collective-permute-done((bf16[256,1024]{1,0:T(8,128)(2,1)S(1)}, bf16[256,1024]{1,0:T(8,128)(2,1)S(1)}, u32[]{:S(2)}, u32[]{:S(2)}) %collective-permute-start.60) | collective-permute-done | bytes 524320 | tf_op jit(solution)/shard_map/ppermute | solution.py:43
  451.1 15.6 %weight_grads.5 = bf16[2048,1152]{1,0:T(8,128)(2,1)} custom-call(bf16[2048,2048]{1,0:T(8,128)(2,1)} %pack.3.normed_ref.refs_0_, bf16[2048,2048]{1,0:T(8,128)(2,1)} %pack.4.cot_ref.refs_1_, bf16[2048,768]{1,0:T(8,128)(2,1)S(1)} %copy-done.29, bf16[2048,384]{1,0:T(8,128)(2,1)S(1)} %get-tuple-element.157.refs_1_.refs_3_), custom_call_target="tpu_custom_call" | custom-call | flops 9663676416 | bytes 26214400 | tf_op jit(solution)/shard_map/weight_grads/pallas_call | solution.py:677
  466.7 6.1 collective-permute-done.63.refs_2_
  480.7 7.0 %collective-permute-done.64.refs_4_ = bf16[128,2048]{1,0:T(8,128)(2,1)S(1)} collective-permute-done((bf16[128,2048]{1,0:T(8,128)(2,1)S(1)}, bf16[128,2048]{1,0:T(8,128)(2,1)S(1)}, u32[]{:S(2)}, u32[]{:S(2)}) %collective-permute-start.64) | collective-permute-done | bytes 524320 | tf_op jit(solution)/shard_map/ppermute | solution.py:43
  496.7 5.6 pack.5.refs_1_
  502.4 6.2 convolution_convert_fusion.mixed_ref
  508.7 11.1 %attention_backward.1.refs_1_.refs_2_.refs_0_ = bf16[2048,768]{1,0:T(8,128)(2,1)} custom-call(s32[16]{0:T(128)S(1)} %select_reduce_fusion.refs_14_.order_ref, bf16[2048,256]{1,0:T(8,128)(2,1)S(1)} %copy-done.77, bf16[2048,256]{1,0:T(8,128)(2,1)S(1)} %copy-done.79, bf16[2048,256]{1,0:T(8,128)(2,1)S(1)} %copy-done.81, f32[2048,1]{1,0:T(8,128)S(1)} %copy-done.83, ...), custom_call_target="tpu_custom_call" | custom-call | flops 5368709120 | bytes 10485760 | tf_op jit(solution)/shard_map/attention_backward/pallas_call | solution.py:855
  524.2 9.1 %weight_grads.6.grads_ref = bf16[2048,512]{1,0:T(8,128)(2,1)S(1)} custom-call(bf16[2048,2048]{1,0:T(8,128)(2,1)} %pack_normed.1.normed_ref.refs_0_, bf16[2048,768]{1,0:T(8,128)(2,1)S(1)} %copy-done), custom_call_target="tpu_custom_call" | custom-call | flops 4294967296 | bytes 12582912 | tf_op jit(solution)/shard_map/weight_grads/pallas_call | solution.py:677
  548.0 11.0 %weight_grads.7.both_ref = bf16[2048,512]{1,0:T(8,128)(2,1)S(1)} custom-call(bf16[2048,2048]{1,0:T(8,128)(2,1)} %pack_normed.1.normed_ref.refs_0_, bf16[2048,2048]{1,0:T(8,128)(2,1)} %pack.5.refs_1_, bf16[2048,768]{1,0:T(8,128)(2,1)} %attention_backward.1.refs_1_.refs_2_.refs_0_, bf16[2048,256]{1,0:T(8,128)(2,1)S(1)} %copy-done.5), custom_call_target="tpu_custom_call" | custom-call | flops 4294967296 | bytes 20971520 | tf_op jit(solution)/shard_map/weight_grads/pallas_call | solution.py:677
  559.1 13.8 %collective-permute-done.75.refs_1_ = bf16[128,1920]{1,0:T(8,128)(2,1)S(1)} collective-permute-done((bf16[128,1920]{1,0:T(8,128)(2,1)S(1)}, bf16[128,1920]{1,0:T(8,128)(2,1)S(1)}, u32[]{:S(2)}, u32[]{:S(2)}) %collective-permute-start.75) | collective-permute-done | bytes 491552 | tf_op jit(solution)/shard_map/ppermute | solution.py:47
  574.4 7.8 %collective-permute-done.77.refs_3_ = bf16[128,1920]{1,0:T(8,128)(2,1)S(1)} collective-permute-done((bf16[128,1920]{1,0:T(8,128)(2,1)S(1)}, bf16[128,1920]{1,0:T(8,128)(2,1)S(1)}, u32[]{:S(2)}, u32[]{:S(2)}) %collective-permute-start.77) | collective-permute-done | bytes 491552 | tf_op jit(solution)/shard_map/ppermute | solution.py:47
  618.3 20.2 %collective-permute-done.83 = bf16[512,1024]{1,0:T(8,128)(2,1)S(1)} collective-permute-done((bf16[512,1024]{1,0:T(8,128)(2,1)S(1)}, bf16[512,1024]{1,0:T(8,128)(2,1)S(1)}, u32[]{:S(2)}, u32[]{:S(2)}) %collective-permute-start.83) | collective-permute-done | bytes 1048608 | tf_op jit(solution)/shard_map/ppermute | solution.py:43
  (533 shorter events, 295.1 us)
Async XLA Ops:
  7.2 131.8 %all-gather.4.cloned.1.call-start = ((), (), s32[]{:S(2)}) async-start(), calls=%async_computation.3 | async-start | bytes 5242880 | tf_op jit(solution)/shard_map/all_gather | solution.py:909
  28.6 260.8 %all-gather.6.cloned.1.call-start = ((), (), s32[]{:S(2)}) async-start(), calls=%async_computation.4 | async-start | bytes 9830400 | tf_op jit(solution)/shard_map/all_gather | solution.py:909
  30.3 31.7 %collective-permute-start.14 = (bf16[2,16,128]{2,1,0:T(8,128)(2,1)S(1)}, bf16[2,16,128]{2,1,0:T(8,128)(2,1)S(1)}, u32[]{:S(2)}, u32[]{:S(2)}) collective-permute-start(bf16[2,16,128]{2,1,0:T(8,128)(2,1)S(1)} %broadcast_select_fusion), channel_id=1, source_target_pairs={{0,6},{2,4},{4,2},{6,0},{8,14},{10,12},{12,10},{14,8},{16,22},{18,... | collective-permute-start | bytes 24584 | tf_op jit(solution)/shard_map/ppermute | solution.py:61
  35.4 23.6 %collective-permute-start.4 = (bf16[256,2048]{1,0:T(8,128)(2,1)S(1)}, bf16[256,2048]{1,0:T(8,128)(2,1)}, u32[]{:S(2)}, u32[]{:S(2)}) collective-permute-start(bf16[256,2048]{1,0:T(8,128)(2,1)S(1)} %copy-done.10), channel_id=1, source_target_pairs={{0,4},{4,0},{1,5},{5,1},{2,6},{6,2},{3,7},{7,3},{8,12},{12,8},{9,1... | collective-permute-start | bytes 3145736 | tf_op jit(solution)/shard_map/ppermute | solution.py:43
  43.8 25.8 %collective-permute-start.7 = (bf16[256,2048]{1,0:T(8,128)(2,1)S(1)}, bf16[256,2048]{1,0:T(8,128)(2,1)}, u32[]{:S(2)}, u32[]{:S(2)}) collective-permute-start(bf16[256,2048]{1,0:T(8,128)(2,1)S(1)} %copy-done.10), channel_id=1, source_target_pairs={{0,1},{1,0},{2,3},{3,2},{4,5},{5,4},{6,7},{7,6},{8,9},{9,8},{10,11... | collective-permute-start | bytes 3145736 | tf_op jit(solution)/shard_map/ppermute | solution.py:43
  107.4 253.4 %all-gather.8.cloned.1.call-start = ((), (), s32[]{:S(2)}) async-start(), calls=%async_computation.5 | async-start | bytes 5898240 | tf_op jit(solution)/shard_map/all_gather | solution.py:909
  107.6 24.7 %collective-permute-start.22 = (bf16[256,2048]{1,0:T(8,128)(2,1)}, bf16[256,2048]{1,0:T(8,128)(2,1)S(1)}, u32[]{:S(2)}, u32[]{:S(2)}) collective-permute-start(bf16[256,2048]{1,0:T(8,128)(2,1)} %base_ref.1), channel_id=1, source_target_pairs={{0,4},{4,0},{1,5},{5,1},{2,6},{6,2},{3,7},{7,3},{8,12},{12,8},{9,1... | collective-permute-start | bytes 3145736 | tf_op jit(solution)/shard_map/ppermute | solution.py:43
  108.6 24.7 %collective-permute-start.21 = (bf16[256,2048]{1,0:T(8,128)(2,1)}, bf16[256,2048]{1,0:T(8,128)(2,1)}, u32[]{:S(2)}, u32[]{:S(2)}) collective-permute-start(bf16[256,2048]{1,0:T(8,128)(2,1)} %base_ref.1), channel_id=1, source_target_pairs={{0,2},{2,0},{1,3},{3,1},{4,6},{6,4},{5,7},{7,5},{8,10},{10,8},{9,1... | collective-permute-start | bytes 3145736 | tf_op jit(solution)/shard_map/ppermute | solution.py:43
  135.5 23.6 %collective-permute-start.23 = (bf16[128,1152]{1,0:T(8,128)(2,1)}, bf16[128,1152]{1,0:T(8,128)(2,1)S(1)}, u32[]{:S(2)}, u32[]{:S(2)}) collective-permute-start(bf16[128,1152]{1,0:T(8,128)(2,1)} %get-tuple-element.130), channel_id=1, source_target_pairs={{0,2},{2,0},{4,6},{6,4},{1,3},{3,1},{5,7},{7,5},{8,10},{10,8},{12,... | collective-permute-start | bytes 884744 | tf_op jit(solution)/shard_map/ppermute | solution.py:47
  136.1 23.7 %collective-permute-start.24 = (bf16[128,1152]{1,0:T(8,128)(2,1)}, bf16[128,1152]{1,0:T(8,128)(2,1)S(1)}, u32[]{:S(2)}, u32[]{:S(2)}) collective-permute-start(bf16[128,1152]{1,0:T(8,128)(2,1)} %get-tuple-element.131), channel_id=1, source_target_pairs={{0,4},{2,6},{4,0},{6,2},{1,5},{3,7},{5,1},{7,3},{8,12},{10,14},{12... | collective-permute-start | bytes 884744 | tf_op jit(solution)/shard_map/ppermute | solution.py:47
  137.0 23.5 %collective-permute-start.25 = (bf16[128,1152]{1,0:T(8,128)(2,1)}, bf16[128,1152]{1,0:T(8,128)(2,1)S(1)}, u32[]{:S(2)}, u32[]{:S(2)}) collective-permute-start(bf16[128,1152]{1,0:T(8,128)(2,1)} %get-tuple-element.132), channel_id=1, source_target_pairs={{0,6},{2,4},{4,2},{6,0},{1,7},{3,5},{5,3},{7,1},{8,14},{10,12},{12... | collective-permute-start | bytes 884744 | tf_op jit(solution)/shard_map/ppermute | solution.py:47
  172.8 25.3 %collective-permute-start.33 = (bf16[2,256,1024]{2,1,0:T(8,128)(2,1)S(1)}, bf16[2,256,1024]{2,1,0:T(8,128)(2,1)}, u32[]{:S(2)}, u32[]{:S(2)}) collective-permute-start(bf16[2,256,1024]{2,1,0:T(8,128)(2,1)S(1)} %bitcast.79), channel_id=1, source_target_pairs={{0,4},{4,0},{1,5},{5,1},{2,6},{6,2},{3,7},{7,3},{8,12},{12,8},{9,1... | collective-permute-start | bytes 3145736 | tf_op jit(solution)/shard_map/ppermute | solution.py:43
  176.4 26.4 %collective-permute-start.27 = (bf16[512,1024]{1,0:T(8,128)(2,1)}, bf16[512,1024]{1,0:T(8,128)(2,1)}, u32[]{:S(2)}, u32[]{:S(2)}) collective-permute-start(bf16[512,1024]{1,0:T(8,128)(2,1)} %pad_maximum_fusion), channel_id=1, source_target_pairs={{0,2},{2,0},{1,3},{3,1},{4,6},{6,4},{5,7},{7,5},{8,10},{10,8},{9,1... | collective-permute-start | bytes 3145736 | tf_op jit(solution)/shard_map/ppermute | solution.py:43
  178.2 361.9 %reduce-scatter.4.cloned.1.call-start = ((), (), s32[]{:S(2)}) async-start(), calls=%async_computation.6 | async-start | bytes 9830400 | tf_op jit(solution)/shard_map/reduce_scatter | solution.py:988
  178.4 23.7 %collective-permute-start.30 = (f32[4]{0:T(128)S(1)}, f32[4]{0:T(128)S(1)}, u32[]{:S(2)}, u32[]{:S(2)}) collective-permute-start(f32[4]{0:T(128)S(1)} %compare_select_fusion), channel_id=1, source_target_pairs={{0,6},{2,4},{4,2},{6,0},{8,14},{10,12},{12,10},{14,8},{16,22},{18,... | collective-permute-start | bytes 56 | tf_op jit(solution)/shard_map/ppermute | solution.py:61
  220.6 23.2 %collective-permute-start.36 = (bf16[256,2048]{1,0:T(8,128)(2,1)S(1)}, bf16[256,2048]{1,0:T(8,128)(2,1)S(1)}, u32[]{:S(2)}, u32[]{:S(2)}) collective-permute-start(bf16[256,2048]{1,0:T(8,128)(2,1)S(1)} %get-tuple-element.137.refs_0_), channel_id=1, source_target_pairs={{0,4},{4,0},{1,5},{5,1},{2,6},{6,2},{3,7},{7,3},{8,12},{12,8},{9,1... | collective-permute-start | bytes 3145736 | tf_op jit(solution)/shard_map/ppermute | solution.py:43
  221.5 23.9 %collective-permute-start.35 = (bf16[256,2048]{1,0:T(8,128)(2,1)S(1)}, bf16[256,2048]{1,0:T(8,128)(2,1)S(1)}, u32[]{:S(2)}, u32[]{:S(2)}) collective-permute-start(bf16[256,2048]{1,0:T(8,128)(2,1)S(1)} %get-tuple-element.137.refs_0_), channel_id=1, source_target_pairs={{0,2},{2,0},{1,3},{3,1},{4,6},{6,4},{5,7},{7,5},{8,10},{10,8},{9,1... | collective-permute-start | bytes 3145736 | tf_op jit(solution)/shard_map/ppermute | solution.py:43
  337.9 258.7 %reduce-scatter.6.cloned.1.call-start = ((), (), s32[]{:S(2)}) async-start(), calls=%async_computation.7 | async-start | bytes 5898240 | tf_op jit(solution)/shard_map/reduce_scatter | solution.py:988
  374.9 23.3 %collective-permute-start.55 = (bf16[1024,1024]{1,0:T(8,128)(2,1)S(1)}, bf16[1024,1024]{1,0:T(8,128)(2,1)S(1)}, u32[]{:S(2)}, u32[]{:S(2)}) collective-permute-start(bf16[1024,1024]{1,0:T(8,128)(2,1)S(1)} %get-tuple-element.154), channel_id=1, source_target_pairs={{0,1},{1,0},{2,3},{3,2},{4,5},{5,4},{6,7},{7,6},{8,9},{9,8},{10,11... | collective-permute-start | bytes 6291464 | tf_op jit(solution)/shard_map/ppermute | solution.py:43
  397.0 29.0 %collective-permute-start.57 = (bf16[512,1024]{1,0:T(8,128)(2,1)}, bf16[512,1024]{1,0:T(8,128)(2,1)}, u32[]{:S(2)}, u32[]{:S(2)}) collective-permute-start(bf16[512,1024]{1,0:T(8,128)(2,1)} %pad_maximum_fusion.1), channel_id=1, source_target_pairs={{0,2},{2,0},{1,3},{3,1},{4,6},{6,4},{5,7},{7,5},{8,10},{10,8},{9,1... | collective-permute-start | bytes 3145736 | tf_op jit(solution)/shard_map/ppermute | solution.py:43
  399.9 28.8 %collective-permute-start.59 = (bf16[2,256,1024]{2,1,0:T(8,128)(2,1)}, bf16[2,256,1024]{2,1,0:T(8,128)(2,1)S(1)}, u32[]{:S(2)}, u32[]{:S(2)}) collective-permute-start(bf16[2,256,1024]{2,1,0:T(8,128)(2,1)} %bitcast.9), channel_id=1, source_target_pairs={{0,4},{4,0},{1,5},{5,1},{2,6},{6,2},{3,7},{7,3},{8,12},{12,8},{9,1... | collective-permute-start | bytes 3145736 | tf_op jit(solution)/shard_map/ppermute | solution.py:43
  449.3 23.5 %collective-permute-start.63 = (bf16[256,2048]{1,0:T(8,128)(2,1)S(1)}, bf16[256,2048]{1,0:T(8,128)(2,1)S(1)}, u32[]{:S(2)}, u32[]{:S(2)}) collective-permute-start(bf16[256,2048]{1,0:T(8,128)(2,1)S(1)} %get-tuple-element.161.refs_0_), channel_id=1, source_target_pairs={{0,4},{4,0},{1,5},{5,1},{2,6},{6,2},{3,7},{7,3},{8,12},{12,8},{9,1... | collective-permute-start | bytes 3145736 | tf_op jit(solution)/shard_map/ppermute | solution.py:43
  449.9 23.2 %collective-permute-start.61 = (bf16[256,2048]{1,0:T(8,128)(2,1)S(1)}, bf16[256,2048]{1,0:T(8,128)(2,1)S(1)}, u32[]{:S(2)}, u32[]{:S(2)}) collective-permute-start(bf16[256,2048]{1,0:T(8,128)(2,1)S(1)} %get-tuple-element.161.refs_0_), channel_id=1, source_target_pairs={{0,2},{2,0},{1,3},{3,1},{4,6},{6,4},{5,7},{7,5},{8,10},{10,8},{9,1... | collective-permute-start | bytes 3145736 | tf_op jit(solution)/shard_map/ppermute | solution.py:43
  473.1 184.4 %reduce-scatter.8.cloned.1.call-start = ((), (), s32[]{:S(2)}) async-start(), calls=%async_computation.8 | async-start | bytes 3932160 | tf_op jit(solution)/shard_map/reduce_scatter | solution.py:988
  493.2 26.6 %collective-permute-start.65 = (bf16[512,1024]{1,0:T(8,128)(2,1)}, bf16[512,1024]{1,0:T(8,128)(2,1)}, u32[]{:S(2)}, u32[]{:S(2)}) collective-permute-start(bf16[512,1024]{1,0:T(8,128)(2,1)} %pad_maximum_fusion.2), channel_id=1, source_target_pairs={{0,2},{2,0},{1,3},{3,1},{4,6},{6,4},{5,7},{7,5},{8,10},{10,8},{9,1... | collective-permute-start | bytes 3145736 | tf_op jit(solution)/shard_map/ppermute | solution.py:43
  494.3 25.5 %collective-permute-start.68 = (bf16[2,256,1024]{2,1,0:T(8,128)(2,1)}, bf16[2,256,1024]{2,1,0:T(8,128)(2,1)}, u32[]{:S(2)}, u32[]{:S(2)}) collective-permute-start(bf16[2,256,1024]{2,1,0:T(8,128)(2,1)} %bitcast.15), channel_id=1, source_target_pairs={{0,4},{4,0},{1,5},{5,1},{2,6},{6,2},{3,7},{7,3},{8,12},{12,8},{9,1... | collective-permute-start | bytes 3145736 | tf_op jit(solution)/shard_map/ppermute | solution.py:43
  536.0 56.6 %collective-permute-start.79 = (bf16[1024,512]{1,0:T(8,128)(2,1)}, bf16[1024,512]{1,0:T(8,128)(2,1)}, u32[]{:S(2)}, u32[]{:S(2)}) collective-permute-start(bf16[1024,512]{1,0:T(8,128)(2,1)} %get-tuple-element.179), channel_id=1, source_target_pairs={{0,2},{2,0},{1,3},{3,1},{4,6},{6,4},{5,7},{7,5},{8,10},{10,8},{9,1... | collective-permute-start | bytes 3145736 | tf_op jit(solution)/shard_map/ppermute | solution.py:43
  542.5 30.3 %collective-permute-start.75 = (bf16[128,1920]{1,0:T(8,128)(2,1)S(1)}, bf16[128,1920]{1,0:T(8,128)(2,1)S(1)}, u32[]{:S(2)}, u32[]{:S(2)}) collective-permute-start(bf16[128,1920]{1,0:T(8,128)(2,1)S(1)} %get-tuple-element.173), channel_id=1, source_target_pairs={{0,2},{2,0},{4,6},{6,4},{1,3},{3,1},{5,7},{7,5},{8,10},{10,8},{12,... | collective-permute-start | bytes 1474568 | tf_op jit(solution)/shard_map/ppermute | solution.py:47
  543.4 30.2 %collective-permute-start.76 = (bf16[128,1920]{1,0:T(8,128)(2,1)S(1)}, bf16[128,1920]{1,0:T(8,128)(2,1)S(1)}, u32[]{:S(2)}, u32[]{:S(2)}) collective-permute-start(bf16[128,1920]{1,0:T(8,128)(2,1)S(1)} %get-tuple-element.174), channel_id=1, source_target_pairs={{0,4},{2,6},{4,0},{6,2},{1,5},{3,7},{5,1},{7,3},{8,12},{10,14},{12... | collective-permute-start | bytes 1474568 | tf_op jit(solution)/shard_map/ppermute | solution.py:47
  545.1 37.1 %collective-permute-start.77 = (bf16[128,1920]{1,0:T(8,128)(2,1)S(1)}, bf16[128,1920]{1,0:T(8,128)(2,1)S(1)}, u32[]{:S(2)}, u32[]{:S(2)}) collective-permute-start(bf16[128,1920]{1,0:T(8,128)(2,1)S(1)} %get-tuple-element.175), channel_id=1, source_target_pairs={{0,6},{2,4},{4,2},{6,0},{1,7},{3,5},{5,3},{7,1},{8,14},{10,12},{12... | collective-permute-start | bytes 1474568 | tf_op jit(solution)/shard_map/ppermute | solution.py:47
  614.1 24.4 %collective-permute-start.83 = (bf16[512,1024]{1,0:T(8,128)(2,1)S(1)}, bf16[512,1024]{1,0:T(8,128)(2,1)S(1)}, u32[]{:S(2)}, u32[]{:S(2)}) collective-permute-start(bf16[512,1024]{1,0:T(8,128)(2,1)S(1)} %pad_maximum_fusion.3), channel_id=1, source_target_pairs={{0,2},{2,0},{1,3},{3,1},{4,6},{6,4},{5,7},{7,5},{8,10},{10,8},{9,1... | collective-permute-start | bytes 3145736 | tf_op jit(solution)/shard_map/ppermute | solution.py:43
  617.0 25.1 %collective-permute-start.86 = (bf16[2,256,1024]{2,1,0:T(8,128)(2,1)S(1)}, bf16[2,256,1024]{2,1,0:T(8,128)(2,1)S(1)}, u32[]{:S(2)}, u32[]{:S(2)}) collective-permute-start(bf16[2,256,1024]{2,1,0:T(8,128)(2,1)S(1)} %bitcast.80), channel_id=1, source_target_pairs={{0,4},{4,0},{1,5},{5,1},{2,6},{6,2},{3,7},{7,3},{8,12},{12,8},{9,1... | collective-permute-start | bytes 3145736 | tf_op jit(solution)/shard_map/ppermute | solution.py:43
  (183 other events, 1719.8 us)
Sparse Core Ops, SparseCore 0:
  28.7 81.7 all-gather.3
  112.7 139.4 all-gather.5
  254.4 87.6 all-gather.7
  344.2 134.6 reduce-scatter.3
  481.1 85.7 reduce-scatter.5
  596.1 61.1 reduce-scatter.7

commit v3 on v2

--- a/solution.py
+++ b/solution.py
@@ -1019,21 +1019,21 @@
     d_far = plane_far(neighbours, grads_1)
     d_attn_all = pack(with_partner([own_d, *neighbours, *d_far]))
     out_sums = chip_sums(*out_parts)
-    out_arrived = reduce_first(first_operands(out_sums), *d_far)
-    out_operands = reduce_operands(out_sums, out_arrived)
-    out_last = last_swaps(out_operands)
-
     def send_grads(sources, *waits):
         first = after(sources[0], *waits) if waits else sources[0]
         return swap_all(pick_rows(member_at, first, *sources[1:]))
 
 
-    final_0 = send_grads([sum_0], *out_arrived)
+    final_0 = send_grads([sum_0], *d_far)
+    out_arrived = reduce_first(first_operands(out_sums), *final_0[1:])
+    out_operands = reduce_operands(out_sums, out_arrived)
+    out_last = last_swaps(out_operands)
+
     d_mixed = product(d_attn_all, attn_weights[:, 3 * HS :]).astype(bf16)
     d_qkv = attention_backward(
-        order, query, keys, vals, logsum, d_mixed, cos, sin
-    )
-    pair_grads = weight_grads((normed_all, (after(d_qkv, *out_arrived), 2 * HS, 0)))
+        order, after(query, *final_0[1:]), keys, vals, logsum, d_mixed, cos, sin
+    )
+    pair_grads = weight_grads((normed_all, (d_qkv, 2 * HS, 0)))
     half_shape = jax.ShapeDtypeStruct((features // 2, 2 * HS), bf16)
     keep, send = vmem_call(
         functools.partial(halves_kernel, own_rows),
@@ -1044,10 +1044,10 @@
     )
     got = swap(send, "col")
     both_grads = weight_grads(
-        (normed_all, (after(d_qkv, keep), HS, 2)), (d_attn_all, mixed)
-    )
-    late_qkv = after(d_qkv, both_grads, *out_last, *final_0[1:])
-    qkv_parts = projected(late_qkv, 0)
+        (normed_all, (after(d_qkv, keep, *out_arrived), HS, 2)), (d_attn_all, mixed)
+    )
+    late_qkv = after(d_qkv, both_grads)
+    qkv_parts = projected(late_qkv, 0, (), out_last)
     (attn_grads,) = vmem_call(
         functools.partial(join_kernel, own_rows),
         "join",

time: 693 us -> 697 us (level)
    ppermute x18, waiting for transfers between devices: 45.6 us -> 36.8 us  [swap_plane(): return lax.ppermute(block, PLANE, [(i, i ^ distance) for i in range(4)])]
    ppermute x62, waiting for transfers between devices: 161 us -> 169 us  [swap(): return lax.ppermute(block, axis, [(0, 1), (1, 0)])]
    unnamed x247 -> x249, local copies, waits for them, and re-layouts: 49.9 us -> 54.4 us
  transfers between devices with their start and end apart: 100 -> 100, of which waited for: 31 -> 32; matrix products, arithmetic and copies ran while one was open for 11% -> 11% of each run, Pallas kernels for 38% -> 37%
where the time goes in v3:
time: 697 us; the launch traced here: 691 us
  Pallas kernels  262 us (38%)
  waiting for transfers between devices  206 us (30%)
  starting transfers between devices  88.2 us (13%)
  local copies, waits for them, and re-layouts  60 us (9%)
  other arithmetic  52 us (7%)
  between operations  16 us (2%)
    ppermute x62, waiting for transfers between devices, swap(): return lax.ppermute(block, axis, [(0, 1), (1, 0)])  169 us
    pallas_call x14, Pallas kernels, chunk_sum(): pl.pallas_call(functools.partial(sum_kernel, count), grid=(steps,), in_sp...  68.2 us
    pallas_call x4, Pallas kernels, weight_grads(): pl.pallas_call(functools.partial(grads_kernel, count), grid=(features //...  60.7 us
    unnamed x249, local copies, waits for them, and re-layouts  54.4 us
    ppermute x62, starting transfers between devices, swap(): return lax.ppermute(block, axis, [(0, 1), (1, 0)])  39.7 us
    ppermute x18, waiting for transfers between devices, swap_plane(): return lax.ppermute(block, PLANE, [(i, i ^ distance) for i in range(4)])  36.8 us
    pallas_call x2, Pallas kernels, mlp_tail(): pl.pallas_call(functools.partial(tail_kernel, width), grid=(steps,), in_s...  29 us
    pallas_call x1, Pallas kernels, mlp_chunk(): pl.pallas_call(functools.partial(mlp_kernel, width), grid=(tokens // tile...  24.3 us
  transfers between devices with their start and end apart: 100, of which 32 were waited for; matrix products, arithmetic and copies ran while one was open for 11% of the time, Pallas kernels for 37%

profile of v3, /device:TPU:0, one launch (start us, length us, event | category | flops | bytes accessed | tf_op | source)
XLA Modules:
  0.0 690.6 jit_solution(5047802716405974708)
XLA Ops:
  15.7 5.6 collective-permute-done.refs_1_
  21.3 6.2 collective-permute-done.1.refs_2_
  45.9 13.1 %collective-permute-done.4.refs_2_ = bf16[256,2048]{1,0:T(8,128)(2,1)} collective-permute-done((bf16[256,2048]{1,0:T(8,128)(2,1)S(1)}, bf16[256,2048]{1,0:T(8,128)(2,1)}, u32[]{:S(2)}, u32[]{:S(2)}) %collective-permute-start.4) | collective-permute-done | bytes 1048608 | tf_op jit(solution)/shard_map/ppermute | solution.py:43
  85.1 9.3 %pack_normed.1.normed_ref.refs_0_ = bf16[2048,2048]{1,0:T(8,128)(2,1)} custom-call(bf16[256,2048]{1,0:T(8,128)(2,1)S(1)} %copy-done.10, bf16[256,2048]{1,0:T(8,128)(2,1)} %collective-permute-done.3.refs_1_, bf16[256,2048]{1,0:T(8,128)(2,1)} %collective-permute-done.4.refs_2_, bf16[128,2048]{1,0:T(8,128)(2,1)S(1)} %collective-permute-done.5.refs_3_, ...), custom_call_target="tpu_custom_call" | custom-call | flops 33554432 | bytes 16777216 | tf_op jit(solution)/shard_map/pack_normed/pallas_call | solution.py:114
  95.4 9.0 %collective-permute-done.19.refs_2_ = bf16[128,1920]{1,0:T(8,128)(2,1)S(1)} collective-permute-done((bf16[128,1920]{1,0:T(8,128)(2,1)S(1)}, bf16[128,1920]{1,0:T(8,128)(2,1)S(1)}, u32[]{:S(2)}, u32[]{:S(2)}) %collective-permute-start.19) | collective-permute-done | bytes 491552 | tf_op jit(solution)/shard_map/ppermute | solution.py:47
  110.0 22.3 %collective-permute-done.22.refs_2_ = bf16[256,2048]{1,0:T(8,128)(2,1)S(1)} collective-permute-done((bf16[256,2048]{1,0:T(8,128)(2,1)}, bf16[256,2048]{1,0:T(8,128)(2,1)S(1)}, u32[]{:S(2)}, u32[]{:S(2)}) %collective-permute-start.22) | collective-permute-done | bytes 1048608 | tf_op jit(solution)/shard_map/ppermute | solution.py:43
  141.5 11.6 %project.1 = (bf16[2048,256]{1,0:T(8,128)(2,1)S(1)}, bf16[2048,256]{1,0:T(8,128)(2,1)S(1)}, bf16[2048,256]{1,0:T(8,128)(2,1)S(1)}) custom-call(s32[16]{0:T(128)S(1)} %compare_select_fusion.1.refs_13_.place_ref, bf16[2048,2048]{1,0:T(8,128)(2,1)} %pack_normed.1.normed_ref.refs_0_, bf16[2048,1024]{1,0:T(8,128)(2,1)} %all-gather.4.cloned.1.call-done.weight_ref.refs_1_, ...), custom_call_target="tpu_custom_call" | custom-call | flops 6442450944 | bytes 16777216 | tf_op jit(solution)/shard_map/project/pallas_call | solution.py:714
  182.0 16.1 %collective-permute-done.33 = bf16[2,256,1024]{2,1,0:T(8,128)(2,1)} collective-permute-done((bf16[2,256,1024]{2,1,0:T(8,128)(2,1)S(1)}, bf16[2,256,1024]{2,1,0:T(8,128)(2,1)}, u32[]{:S(2)}, u32[]{:S(2)}) %collective-permute-start.33) | collective-permute-done | bytes 1048608 | tf_op jit(solution)/shard_map/ppermute | solution.py:43
  207.1 8.2 %collective-permute-done.34.back_last = bf16[256,1024]{1,0:T(8,128)(2,1)S(1)} collective-permute-done((bf16[256,1024]{1,0:T(8,128)(2,1)S(1)}, bf16[256,1024]{1,0:T(8,128)(2,1)S(1)}, u32[]{:S(2)}, u32[]{:S(2)}) %collective-permute-start.34) | collective-permute-done | bytes 524320 | tf_op jit(solution)/shard_map/ppermute | solution.py:43
  227.8 16.0 %collective-permute-done.36.refs_2_ = bf16[256,2048]{1,0:T(8,128)(2,1)S(1)} collective-permute-done((bf16[256,2048]{1,0:T(8,128)(2,1)S(1)}, bf16[256,2048]{1,0:T(8,128)(2,1)S(1)}, u32[]{:S(2)}, u32[]{:S(2)}) %collective-permute-start.36) | collective-permute-done | bytes 1048608 | tf_op jit(solution)/shard_map/ppermute | solution.py:43
  248.0 10.3 %collective-permute-done.41.refs_4_ = bf16[128,2048]{1,0:T(8,128)(2,1)S(1)} collective-permute-done((bf16[128,2048]{1,0:T(8,128)(2,1)S(1)}, bf16[128,2048]{1,0:T(8,128)(2,1)S(1)}, u32[]{:S(2)}, u32[]{:S(2)}) %collective-permute-start.41) | collective-permute-done | bytes 524320 | tf_op jit(solution)/shard_map/ppermute | solution.py:43
  262.4 11.0 %collective-permute-done.47.refs_3_ = bf16[128,2048]{1,0:T(8,128)(2,1)S(1)} collective-permute-done((bf16[128,2048]{1,0:T(8,128)(2,1)S(1)}, bf16[128,2048]{1,0:T(8,128)(2,1)S(1)}, u32[]{:S(2)}, u32[]{:S(2)}) %collective-permute-start.47) | collective-permute-done | bytes 524320 | tf_op jit(solution)/shard_map/ppermute | solution.py:43
  283.8 5.6 pack.4.cot_ref.refs_1_
  289.4 24.3 %mlp_chunk.1 = (bf16[2048,640]{1,0:T(8,128)(2,1)S(1)}, bf16[2048,1280]{1,0:T(8,128)(2,1)}) custom-call(bf16[2048,2048]{1,0:T(8,128)(2,1)} %pack.3.normed_ref.refs_0_, bf16[2048,2048]{1,0:T(8,128)(2,1)} %pack.4.cot_ref.refs_1_, bf16[2048,1920]{1,0:T(8,128)(2,1)} %all-gather.6.cloned.1.call-done.weight_ref.refs_1_.refs_2_), custom_call_target="tpu_custom_call" | custom-call | flops 16106127360 | bytes 24641536 | tf_op jit(solution)/shard_map/mlp_chunk/pallas_call | solution.py:595
  313.8 24.2 %weight_grads.4 = bf16[2048,1920]{1,0:T(8,128)(2,1)} custom-call(bf16[2048,2048]{1,0:T(8,128)(2,1)} %pack.3.normed_ref.refs_0_, bf16[2048,2048]{1,0:T(8,128)(2,1)} %pack.4.cot_ref.refs_1_, bf16[2048,1280]{1,0:T(8,128)(2,1)} %get-tuple-element.148.refs_2_.refs_0_, bf16[2048,640]{1,0:T(8,128)(2,1)S(1)} %get-tuple-element.156.refs_3_.refs_0_), custom_call_target="tpu_custom_call" | custom-call | flops 16106127360 | bytes 32505856 | tf_op jit(solution)/shard_map/weight_grads/pallas_call | solution.py:677
  340.9 10.0 %chunk_sum.19.base_ref = f32[1024,2048]{1,0:T(8,128)} custom-call(bf16[2048,1280]{1,0:T(8,128)(2,1)S(1)} %copy-done.6, bf16[2048,1920]{1,0:T(8,128)(2,1)} %all-gather.6.cloned.1.call-done.weight_ref.refs_1_.refs_2_), custom_call_target="tpu_custom_call" | custom-call | flops 5368709120 | bytes 16252928 | tf_op jit(solution)/shard_map/chunk_sum/pallas_call | solution.py:641
  351.0 10.1 %chunk_sum.18.base_ref = f32[1024,2048]{1,0:T(8,128)} custom-call(bf16[2048,1280]{1,0:T(8,128)(2,1)S(1)} %copy-done.6, bf16[2048,1920]{1,0:T(8,128)(2,1)} %all-gather.6.cloned.1.call-done.weight_ref.refs_1_.refs_2_), custom_call_target="tpu_custom_call" | custom-call | flops 5368709120 | bytes 16252928 | tf_op jit(solution)/shard_map/chunk_sum/pallas_call | solution.py:641
  361.0 13.9 %mlp_tail.2 = (bf16[2048,384]{1,0:T(8,128)(2,1)S(1)}, bf16[2048,768]{1,0:T(8,128)(2,1)}, bf16[1024,1024]{1,0:T(8,128)(2,1)S(1)}, bf16[1024,1024]{1,0:T(8,128)(2,1)S(1)}) custom-call(bf16[2048,2048]{1,0:T(8,128)(2,1)} %pack.3.normed_ref.refs_0_, bf16[2048,2048]{1,0:T(8,128)(2,1)} %pack.4.cot_ref.refs_1_, ...), custom_call_target="tpu_custom_call" | custom-call | flops 8053063680 | bytes 25690112 | tf_op jit(solution)/shard_map/mlp_tail/pallas_call | solution.py:558
  377.4 15.1 %mlp_tail.3 = (bf16[2048,384]{1,0:T(8,128)(2,1)S(1)}, bf16[2048,768]{1,0:T(8,128)(2,1)S(1)}, f32[1024,1024]{1,0:T(8,128)}, f32[1024,1024]{1,0:T(8,128)}) custom-call(bf16[2048,2048]{1,0:T(8,128)(2,1)} %pack.3.normed_ref.refs_0_, bf16[2048,2048]{1,0:T(8,128)(2,1)} %pack.4.cot_ref.refs_1_, ...), custom_call_target="tpu_custom_call", output_to_operand_aliasing={{0}: (4, {}), {1}: (5, {})} | custom-call | flops 8053063680 | bytes 25690112 | tf_op jit(solution)/shard_map/mlp_tail/pallas_call | solution.py:558
  412.7 6.8 chunk_sum.22
  419.5 6.4 chunk_sum.20
  432.3 11.7 %collective-permute-done.60.back_last = bf16[256,1024]{1,0:T(8,128)(2,1)S(1)} collective-permute-done((bf16[256,1024]{1,0:T(8,128)(2,1)S(1)}, bf16[256,1024]{1,0:T(8,128)(2,1)S(1)}, u32[]{:S(2)}, u32[]{:S(2)}) %collective-permute-start.60) | collective-permute-done | bytes 524320 | tf_op jit(solution)/shard_map/ppermute | solution.py:43
  451.0 15.6 %weight_grads.5 = bf16[2048,1152]{1,0:T(8,128)(2,1)} custom-call(bf16[2048,2048]{1,0:T(8,128)(2,1)} %pack.3.normed_ref.refs_0_, bf16[2048,2048]{1,0:T(8,128)(2,1)} %pack.4.cot_ref.refs_1_, bf16[2048,768]{1,0:T(8,128)(2,1)S(1)} %copy-done.29, bf16[2048,384]{1,0:T(8,128)(2,1)S(1)} %get-tuple-element.158.refs_1_.refs_3_), custom_call_target="tpu_custom_call" | custom-call | flops 9663676416 | bytes 26214400 | tf_op jit(solution)/shard_map/weight_grads/pallas_call | solution.py:677
  466.6 6.1 collective-permute-done.63.refs_2_
  480.7 7.0 %collective-permute-done.64.refs_4_ = bf16[128,2048]{1,0:T(8,128)(2,1)S(1)} collective-permute-done((bf16[128,2048]{1,0:T(8,128)(2,1)S(1)}, bf16[128,2048]{1,0:T(8,128)(2,1)S(1)}, u32[]{:S(2)}, u32[]{:S(2)}) %collective-permute-start.64) | collective-permute-done | bytes 524320 | tf_op jit(solution)/shard_map/ppermute | solution.py:43
  505.3 6.5 convolution_convert_fusion.mixed_ref
  516.5 9.1 %collective-permute-done.66.refs_2_ = bf16[128,1920]{1,0:T(8,128)(2,1)S(1)} collective-permute-done((bf16[128,1920]{1,0:T(8,128)(2,1)S(1)}, bf16[128,1920]{1,0:T(8,128)(2,1)S(1)}, u32[]{:S(2)}, u32[]{:S(2)}) %collective-permute-start.66) | collective-permute-done | bytes 491552 | tf_op jit(solution)/shard_map/ppermute | solution.py:47
  530.5 11.2 %attention_backward.1.refs_1_.refs_2_.refs_0_ = bf16[2048,768]{1,0:T(8,128)(2,1)} custom-call(s32[16]{0:T(128)S(1)} %select_reduce_fusion.refs_14_.order_ref, bf16[2048,256]{1,0:T(8,128)(2,1)S(1)} %copy-done.71, bf16[2048,256]{1,0:T(8,128)(2,1)S(1)} %copy-done.73, bf16[2048,256]{1,0:T(8,128)(2,1)S(1)} %copy-done.75, f32[2048,1]{1,0:T(8,128)S(1)} %copy-done.77, ...), custom_call_target="tpu_custom_call" | custom-call | flops 5368709120 | bytes 10485760 | tf_op jit(solution)/shard_map/attention_backward/pallas_call | solution.py:855
  543.6 8.9 %weight_grads.6.grads_ref = bf16[2048,512]{1,0:T(8,128)(2,1)S(1)} custom-call(bf16[2048,2048]{1,0:T(8,128)(2,1)} %pack_normed.1.normed_ref.refs_0_, bf16[2048,768]{1,0:T(8,128)(2,1)S(1)} %copy-done), custom_call_target="tpu_custom_call" | custom-call | flops 4294967296 | bytes 12582912 | tf_op jit(solution)/shard_map/weight_grads/pallas_call | solution.py:677
  553.9 12.0 %weight_grads.7.both_ref = bf16[2048,512]{1,0:T(8,128)(2,1)S(1)} custom-call(bf16[2048,2048]{1,0:T(8,128)(2,1)} %pack_normed.1.normed_ref.refs_0_, bf16[2048,2048]{1,0:T(8,128)(2,1)} %pack.5.refs_1_, bf16[2048,768]{1,0:T(8,128)(2,1)} %attention_backward.1.refs_1_.refs_2_.refs_0_, bf16[2048,256]{1,0:T(8,128)(2,1)S(1)} %copy-done.5), custom_call_target="tpu_custom_call" | custom-call | flops 4294967296 | bytes 20971520 | tf_op jit(solution)/shard_map/weight_grads/pallas_call | solution.py:677
  590.9 7.8 %collective-permute-done.72.back_last = bf16[256,1024]{1,0:T(8,128)(2,1)} collective-permute-done((bf16[256,1024]{1,0:T(8,128)(2,1)}, bf16[256,1024]{1,0:T(8,128)(2,1)}, u32[]{:S(2)}, u32[]{:S(2)}) %collective-permute-start.72) | collective-permute-done | bytes 524320 | tf_op jit(solution)/shard_map/ppermute | solution.py:43
  619.8 19.5 %collective-permute-done.83 = bf16[512,1024]{1,0:T(8,128)(2,1)S(1)} collective-permute-done((bf16[512,1024]{1,0:T(8,128)(2,1)S(1)}, bf16[512,1024]{1,0:T(8,128)(2,1)S(1)}, u32[]{:S(2)}, u32[]{:S(2)}) %collective-permute-start.83) | collective-permute-done | bytes 1048608 | tf_op jit(solution)/shard_map/ppermute | solution.py:43
  (535 shorter events, 304.4 us)
Async XLA Ops:
  7.2 131.8 %all-gather.4.cloned.1.call-start = ((), (), s32[]{:S(2)}) async-start(), calls=%async_computation.3 | async-start | bytes 5242880 | tf_op jit(solution)/shard_map/all_gather | solution.py:909
  28.6 260.8 %all-gather.6.cloned.1.call-start = ((), (), s32[]{:S(2)}) async-start(), calls=%async_computation.4 | async-start | bytes 9830400 | tf_op jit(solution)/shard_map/all_gather | solution.py:909
  30.3 31.7 %collective-permute-start.14 = (bf16[2,16,128]{2,1,0:T(8,128)(2,1)S(1)}, bf16[2,16,128]{2,1,0:T(8,128)(2,1)S(1)}, u32[]{:S(2)}, u32[]{:S(2)}) collective-permute-start(bf16[2,16,128]{2,1,0:T(8,128)(2,1)S(1)} %broadcast_select_fusion), channel_id=1, source_target_pairs={{0,6},{2,4},{4,2},{6,0},{8,14},{10,12},{12,10},{14,8},{16,22},{18,... | collective-permute-start | bytes 24584 | tf_op jit(solution)/shard_map/ppermute | solution.py:61
  35.4 23.6 %collective-permute-start.4 = (bf16[256,2048]{1,0:T(8,128)(2,1)S(1)}, bf16[256,2048]{1,0:T(8,128)(2,1)}, u32[]{:S(2)}, u32[]{:S(2)}) collective-permute-start(bf16[256,2048]{1,0:T(8,128)(2,1)S(1)} %copy-done.10), channel_id=1, source_target_pairs={{0,4},{4,0},{1,5},{5,1},{2,6},{6,2},{3,7},{7,3},{8,12},{12,8},{9,1... | collective-permute-start | bytes 3145736 | tf_op jit(solution)/shard_map/ppermute | solution.py:43
  36.2 23.1 %collective-permute-start.3 = (bf16[256,2048]{1,0:T(8,128)(2,1)S(1)}, bf16[256,2048]{1,0:T(8,128)(2,1)}, u32[]{:S(2)}, u32[]{:S(2)}) collective-permute-start(bf16[256,2048]{1,0:T(8,128)(2,1)S(1)} %copy-done.10), channel_id=1, source_target_pairs={{0,2},{2,0},{1,3},{3,1},{4,6},{6,4},{5,7},{7,5},{8,10},{10,8},{9,1... | collective-permute-start | bytes 3145736 | tf_op jit(solution)/shard_map/ppermute | solution.py:43
  43.8 25.8 %collective-permute-start.7 = (bf16[256,2048]{1,0:T(8,128)(2,1)S(1)}, bf16[256,2048]{1,0:T(8,128)(2,1)}, u32[]{:S(2)}, u32[]{:S(2)}) collective-permute-start(bf16[256,2048]{1,0:T(8,128)(2,1)S(1)} %copy-done.10), channel_id=1, source_target_pairs={{0,1},{1,0},{2,3},{3,2},{4,5},{5,4},{6,7},{7,6},{8,9},{9,8},{10,11... | collective-permute-start | bytes 3145736 | tf_op jit(solution)/shard_map/ppermute | solution.py:43
  107.4 253.6 %all-gather.8.cloned.1.call-start = ((), (), s32[]{:S(2)}) async-start(), calls=%async_computation.5 | async-start | bytes 5898240 | tf_op jit(solution)/shard_map/all_gather | solution.py:909
  107.6 24.7 %collective-permute-start.22 = (bf16[256,2048]{1,0:T(8,128)(2,1)}, bf16[256,2048]{1,0:T(8,128)(2,1)S(1)}, u32[]{:S(2)}, u32[]{:S(2)}) collective-permute-start(bf16[256,2048]{1,0:T(8,128)(2,1)} %base_ref.1), channel_id=1, source_target_pairs={{0,4},{4,0},{1,5},{5,1},{2,6},{6,2},{3,7},{7,3},{8,12},{12,8},{9,1... | collective-permute-start | bytes 3145736 | tf_op jit(solution)/shard_map/ppermute | solution.py:43
  108.6 24.7 %collective-permute-start.21 = (bf16[256,2048]{1,0:T(8,128)(2,1)}, bf16[256,2048]{1,0:T(8,128)(2,1)}, u32[]{:S(2)}, u32[]{:S(2)}) collective-permute-start(bf16[256,2048]{1,0:T(8,128)(2,1)} %base_ref.1), channel_id=1, source_target_pairs={{0,2},{2,0},{1,3},{3,1},{4,6},{6,4},{5,7},{7,5},{8,10},{10,8},{9,1... | collective-permute-start | bytes 3145736 | tf_op jit(solution)/shard_map/ppermute | solution.py:43
  135.5 23.6 %collective-permute-start.23 = (bf16[128,1152]{1,0:T(8,128)(2,1)}, bf16[128,1152]{1,0:T(8,128)(2,1)S(1)}, u32[]{:S(2)}, u32[]{:S(2)}) collective-permute-start(bf16[128,1152]{1,0:T(8,128)(2,1)} %get-tuple-element.131), channel_id=1, source_target_pairs={{0,2},{2,0},{4,6},{6,4},{1,3},{3,1},{5,7},{7,5},{8,10},{10,8},{12,... | collective-permute-start | bytes 884744 | tf_op jit(solution)/shard_map/ppermute | solution.py:47
  136.1 23.7 %collective-permute-start.24 = (bf16[128,1152]{1,0:T(8,128)(2,1)}, bf16[128,1152]{1,0:T(8,128)(2,1)S(1)}, u32[]{:S(2)}, u32[]{:S(2)}) collective-permute-start(bf16[128,1152]{1,0:T(8,128)(2,1)} %get-tuple-element.132), channel_id=1, source_target_pairs={{0,4},{2,6},{4,0},{6,2},{1,5},{3,7},{5,1},{7,3},{8,12},{10,14},{12... | collective-permute-start | bytes 884744 | tf_op jit(solution)/shard_map/ppermute | solution.py:47
  137.0 23.6 %collective-permute-start.25 = (bf16[128,1152]{1,0:T(8,128)(2,1)}, bf16[128,1152]{1,0:T(8,128)(2,1)S(1)}, u32[]{:S(2)}, u32[]{:S(2)}) collective-permute-start(bf16[128,1152]{1,0:T(8,128)(2,1)} %get-tuple-element.133), channel_id=1, source_target_pairs={{0,6},{2,4},{4,2},{6,0},{1,7},{3,5},{5,3},{7,1},{8,14},{10,12},{12... | collective-permute-start | bytes 884744 | tf_op jit(solution)/shard_map/ppermute | solution.py:47
  172.8 25.3 %collective-permute-start.33 = (bf16[2,256,1024]{2,1,0:T(8,128)(2,1)S(1)}, bf16[2,256,1024]{2,1,0:T(8,128)(2,1)}, u32[]{:S(2)}, u32[]{:S(2)}) collective-permute-start(bf16[2,256,1024]{2,1,0:T(8,128)(2,1)S(1)} %bitcast.81), channel_id=1, source_target_pairs={{0,4},{4,0},{1,5},{5,1},{2,6},{6,2},{3,7},{7,3},{8,12},{12,8},{9,1... | collective-permute-start | bytes 3145736 | tf_op jit(solution)/shard_map/ppermute | solution.py:43
  176.4 26.4 %collective-permute-start.27 = (bf16[512,1024]{1,0:T(8,128)(2,1)}, bf16[512,1024]{1,0:T(8,128)(2,1)}, u32[]{:S(2)}, u32[]{:S(2)}) collective-permute-start(bf16[512,1024]{1,0:T(8,128)(2,1)} %pad_maximum_fusion), channel_id=1, source_target_pairs={{0,2},{2,0},{1,3},{3,1},{4,6},{6,4},{5,7},{7,5},{8,10},{10,8},{9,1... | collective-permute-start | bytes 3145736 | tf_op jit(solution)/shard_map/ppermute | solution.py:43
  178.2 321.7 %reduce-scatter.4.cloned.1.call-start = ((), (), s32[]{:S(2)}) async-start(), calls=%async_computation.6 | async-start | bytes 9830400 | tf_op jit(solution)/shard_map/reduce_scatter | solution.py:988
  178.5 23.7 %collective-permute-start.30 = (f32[4]{0:T(128)S(1)}, f32[4]{0:T(128)S(1)}, u32[]{:S(2)}, u32[]{:S(2)}) collective-permute-start(f32[4]{0:T(128)S(1)} %compare_select_fusion), channel_id=1, source_target_pairs={{0,6},{2,4},{4,2},{6,0},{8,14},{10,12},{12,10},{14,8},{16,22},{18,... | collective-permute-start | bytes 56 | tf_op jit(solution)/shard_map/ppermute | solution.py:61
  220.6 23.1 %collective-permute-start.36 = (bf16[256,2048]{1,0:T(8,128)(2,1)S(1)}, bf16[256,2048]{1,0:T(8,128)(2,1)S(1)}, u32[]{:S(2)}, u32[]{:S(2)}) collective-permute-start(bf16[256,2048]{1,0:T(8,128)(2,1)S(1)} %get-tuple-element.138.refs_0_), channel_id=1, source_target_pairs={{0,4},{4,0},{1,5},{5,1},{2,6},{6,2},{3,7},{7,3},{8,12},{12,8},{9,1... | collective-permute-start | bytes 3145736 | tf_op jit(solution)/shard_map/ppermute | solution.py:43
  221.5 23.9 %collective-permute-start.35 = (bf16[256,2048]{1,0:T(8,128)(2,1)S(1)}, bf16[256,2048]{1,0:T(8,128)(2,1)S(1)}, u32[]{:S(2)}, u32[]{:S(2)}) collective-permute-start(bf16[256,2048]{1,0:T(8,128)(2,1)S(1)} %get-tuple-element.138.refs_0_), channel_id=1, source_target_pairs={{0,2},{2,0},{1,3},{3,1},{4,6},{6,4},{5,7},{7,5},{8,10},{10,8},{9,1... | collective-permute-start | bytes 3145736 | tf_op jit(solution)/shard_map/ppermute | solution.py:43
  337.9 250.5 %reduce-scatter.6.cloned.1.call-start = ((), (), s32[]{:S(2)}) async-start(), calls=%async_computation.7 | async-start | bytes 5898240 | tf_op jit(solution)/shard_map/reduce_scatter | solution.py:988
  375.1 23.2 %collective-permute-start.55 = (bf16[1024,1024]{1,0:T(8,128)(2,1)S(1)}, bf16[1024,1024]{1,0:T(8,128)(2,1)S(1)}, u32[]{:S(2)}, u32[]{:S(2)}) collective-permute-start(bf16[1024,1024]{1,0:T(8,128)(2,1)S(1)} %get-tuple-element.155), channel_id=1, source_target_pairs={{0,1},{1,0},{2,3},{3,2},{4,5},{5,4},{6,7},{7,6},{8,9},{9,8},{10,11... | collective-permute-start | bytes 6291464 | tf_op jit(solution)/shard_map/ppermute | solution.py:43
  397.2 28.6 %collective-permute-start.57 = (bf16[512,1024]{1,0:T(8,128)(2,1)}, bf16[512,1024]{1,0:T(8,128)(2,1)}, u32[]{:S(2)}, u32[]{:S(2)}) collective-permute-start(bf16[512,1024]{1,0:T(8,128)(2,1)} %pad_maximum_fusion.1), channel_id=1, source_target_pairs={{0,2},{2,0},{1,3},{3,1},{4,6},{6,4},{5,7},{7,5},{8,10},{10,8},{9,1... | collective-permute-start | bytes 3145736 | tf_op jit(solution)/shard_map/ppermute | solution.py:43
  399.9 28.5 %collective-permute-start.59 = (bf16[2,256,1024]{2,1,0:T(8,128)(2,1)}, bf16[2,256,1024]{2,1,0:T(8,128)(2,1)S(1)}, u32[]{:S(2)}, u32[]{:S(2)}) collective-permute-start(bf16[2,256,1024]{2,1,0:T(8,128)(2,1)} %bitcast.9), channel_id=1, source_target_pairs={{0,4},{4,0},{1,5},{5,1},{2,6},{6,2},{3,7},{7,3},{8,12},{12,8},{9,1... | collective-permute-start | bytes 3145736 | tf_op jit(solution)/shard_map/ppermute | solution.py:43
  449.2 23.5 %collective-permute-start.63 = (bf16[256,2048]{1,0:T(8,128)(2,1)S(1)}, bf16[256,2048]{1,0:T(8,128)(2,1)S(1)}, u32[]{:S(2)}, u32[]{:S(2)}) collective-permute-start(bf16[256,2048]{1,0:T(8,128)(2,1)S(1)} %get-tuple-element.162.refs_0_), channel_id=1, source_target_pairs={{0,4},{4,0},{1,5},{5,1},{2,6},{6,2},{3,7},{7,3},{8,12},{12,8},{9,1... | collective-permute-start | bytes 3145736 | tf_op jit(solution)/shard_map/ppermute | solution.py:43
  449.8 23.2 %collective-permute-start.61 = (bf16[256,2048]{1,0:T(8,128)(2,1)S(1)}, bf16[256,2048]{1,0:T(8,128)(2,1)S(1)}, u32[]{:S(2)}, u32[]{:S(2)}) collective-permute-start(bf16[256,2048]{1,0:T(8,128)(2,1)S(1)} %get-tuple-element.162.refs_0_), channel_id=1, source_target_pairs={{0,2},{2,0},{1,3},{3,1},{4,6},{6,4},{5,7},{7,5},{8,10},{10,8},{9,1... | collective-permute-start | bytes 3145736 | tf_op jit(solution)/shard_map/ppermute | solution.py:43
  473.0 188.8 %reduce-scatter.8.cloned.1.call-start = ((), (), s32[]{:S(2)}) async-start(), calls=%async_computation.8 | async-start | bytes 3932160 | tf_op jit(solution)/shard_map/reduce_scatter | solution.py:988
  527.4 26.4 %collective-permute-start.68 = (bf16[512,1024]{1,0:T(8,128)(2,1)S(1)}, bf16[512,1024]{1,0:T(8,128)(2,1)S(1)}, u32[]{:S(2)}, u32[]{:S(2)}) collective-permute-start(bf16[512,1024]{1,0:T(8,128)(2,1)S(1)} %copy-done.103), channel_id=1, source_target_pairs={{0,2},{2,0},{1,3},{3,1},{4,6},{6,4},{5,7},{7,5},{8,10},{10,8},{9,1... | collective-permute-start | bytes 3145736 | tf_op jit(solution)/shard_map/ppermute | solution.py:43
  528.5 25.3 %collective-permute-start.71 = (bf16[2,256,1024]{2,1,0:T(8,128)(2,1)S(1)}, bf16[2,256,1024]{2,1,0:T(8,128)(2,1)S(1)}, u32[]{:S(2)}, u32[]{:S(2)}) collective-permute-start(bf16[2,256,1024]{2,1,0:T(8,128)(2,1)S(1)} %bitcast.80), channel_id=1, source_target_pairs={{0,4},{4,0},{1,5},{5,1},{2,6},{6,2},{3,7},{7,3},{8,12},{12,8},{9,1... | collective-permute-start | bytes 3145736 | tf_op jit(solution)/shard_map/ppermute | solution.py:43
  577.6 35.9 %collective-permute-start.78 = (bf16[1024,1024]{1,0:T(8,128)(2,1)}, bf16[1024,1024]{1,0:T(8,128)(2,1)}, u32[]{:S(2)}, u32[]{:S(2)}) collective-permute-start(bf16[1024,1024]{1,0:T(8,128)(2,1)} %copy-done.37), channel_id=1, source_target_pairs={{0,1},{1,0},{2,3},{3,2},{4,5},{5,4},{6,7},{7,6},{8,9},{9,8},{10,11... | collective-permute-start | bytes 6291464 | tf_op jit(solution)/shard_map/ppermute | solution.py:43
  577.7 39.4 %collective-permute-start.85 = (bf16[1024,1024]{1,0:T(8,128)(2,1)}, bf16[1024,1024]{1,0:T(8,128)(2,1)}, u32[]{:S(2)}, u32[]{:S(2)}) collective-permute-start(bf16[1024,1024]{1,0:T(8,128)(2,1)} %copy-done.36), channel_id=1, source_target_pairs={{0,1},{1,0},{2,3},{3,2},{4,5},{5,4},{6,7},{7,6},{8,9},{9,8},{10,11... | collective-permute-start | bytes 6291464 | tf_op jit(solution)/shard_map/ppermute | solution.py:43
  589.8 26.2 %collective-permute-start.80 = (bf16[128,1152]{1,0:T(8,128)(2,1)S(1)}, bf16[128,1152]{1,0:T(8,128)(2,1)S(1)}, u32[]{:S(2)}, u32[]{:S(2)}) collective-permute-start(bf16[128,1152]{1,0:T(8,128)(2,1)S(1)} %get-tuple-element.183), channel_id=1, source_target_pairs={{0,2},{2,0},{4,6},{6,4},{1,3},{3,1},{5,7},{7,5},{8,10},{10,8},{12,... | collective-permute-start | bytes 884744 | tf_op jit(solution)/shard_map/ppermute | solution.py:47
  616.0 23.2 %collective-permute-start.83 = (bf16[512,1024]{1,0:T(8,128)(2,1)S(1)}, bf16[512,1024]{1,0:T(8,128)(2,1)S(1)}, u32[]{:S(2)}, u32[]{:S(2)}) collective-permute-start(bf16[512,1024]{1,0:T(8,128)(2,1)S(1)} %pad_maximum_fusion.3), channel_id=1, source_target_pairs={{0,2},{2,0},{1,3},{3,1},{4,6},{6,4},{5,7},{7,5},{8,10},{10,8},{9,1... | collective-permute-start | bytes 3145736 | tf_op jit(solution)/shard_map/ppermute | solution.py:43
  618.8 24.1 %collective-permute-start.86 = (bf16[2,256,1024]{2,1,0:T(8,128)(2,1)S(1)}, bf16[2,256,1024]{2,1,0:T(8,128)(2,1)S(1)}, u32[]{:S(2)}, u32[]{:S(2)}) collective-permute-start(bf16[2,256,1024]{2,1,0:T(8,128)(2,1)S(1)} %bitcast.82), channel_id=1, source_target_pairs={{0,4},{4,0},{1,5},{5,1},{2,6},{6,2},{3,7},{7,3},{8,12},{12,8},{9,1... | collective-permute-start | bytes 3145736 | tf_op jit(solution)/shard_map/ppermute | solution.py:43
  (184 other events, 1837.2 us)
Sparse Core Ops, SparseCore 0:
  28.7 81.7 all-gather.3
  112.7 139.4 all-gather.5
  254.4 87.6 all-gather.7
  344.2 134.6 reduce-scatter.3
  481.1 85.7 reduce-scatter.5
  577.7 61.5 reduce-scatter.7
